TPU v7x, 128 devices: a whole 4x4x4 slice. The times are simulated.
128 devices in a mesh: outer: 4 (over x_hi, core), inner: 32 (over y, z, x_lo).
Axes of the slice: x: 4 (x_hi: 2, x_lo: 2; x = x_hi * 2 + x_lo), y: 4, z: 4, core: 2. Of those that a mesh axis runs over, the one named last changes fastest.
Arguments:
- queries: bfloat16 [32768, 1024], P(('outer', 'inner'))
- keys: bfloat16 [32768, 128], P(('outer', 'inner'))
- values: bfloat16 [32768, 128], P(('outer', 'inner')), may hold values from -6 to 6
- positions: int32 [32768], P(('outer', 'inner')), may hold values from 0 to 32767, as said below
Outputs:
- attended: bfloat16 [32768, 1024], P(('outer', 'inner'))
Inputs may be any that keep to these rules, and one draw needn't show every extreme that they name: The stored tokens form 32768 // 256 consecutive groups of 256 rows, one group a device; each group's first 128 rows hold the positions b * (128) onward in increasing order by one, and its last 128 rows the positions from (255 - b) * (128) onward likewise, for a b below 128 that each group has for itself; every position occurs once.
All inputs are finite; a program needn't handle non-finite values.
Results may differ from a plain program's by a relative error of at most 0.0055.
Values may be sent and summed in bfloat16 or wider, within the bound.
No kernel may reach another device: no remote copies, remote signals or barrier semaphores. Data moves between devices by JAX's collectives and lax.ppermute only.
A program may use at most 128 MiB of HBM per device.

v0:
```python
import jax
import jax.numpy as jnp
from jax import lax
from jax.sharding import PartitionSpec as P

NEG = -1e30


def attend_block(state, query_rows, query_pos, key_block, value_block, keypos_block, masked, scale):
    best, total, accum = state
    scores = (
        lax.dot_general(
            query_rows, key_block, (((1,), (1,)), ((), ())), preferred_element_type=jnp.float32
        )
        * scale
    )
    if masked:
        scores = jnp.where(keypos_block[None, :] <= query_pos[:, None], scores, NEG)
    newbest = jnp.maximum(best, jnp.max(scores, axis=1))
    factor = jnp.exp(best - newbest)
    expd = jnp.exp(scores - newbest[:, None])
    total = total * factor + jnp.sum(expd, axis=1)
    accum = accum * factor[:, None] + jnp.dot(
        expd.astype(jnp.bfloat16), value_block, preferred_element_type=jnp.float32
    )
    return (newbest, total, accum)


def attend_runs(state, query_rows, query_pos, key_rows, value_rows, keypos_rows, masked, scale):
    count = key_rows.shape[0]
    width = 1
    for cand in range(min(count, 1024), 0, -1):
        if count % cand == 0:
            width = cand
            break
    steps = count // width
    head_dim = key_rows.shape[1]
    stacked = (
        key_rows.reshape(steps, width, head_dim),
        value_rows.reshape(steps, width, head_dim),
        keypos_rows.reshape(steps, width),
    )

    def advance(carry, blocks):
        return (
            attend_block(
                carry, query_rows, query_pos, blocks[0], blocks[1], blocks[2], masked, scale
            ),
            None,
        )

    state, unused = lax.scan(advance, state, stacked)
    return state


def body(queries, keys, values, positions):
    tok_rows = queries.shape[0]
    head_dim = keys.shape[1]
    heads = queries.shape[1] // head_dim
    run_len = tok_rows // 2
    scale = head_dim ** (-0.5)
    query_rows = queries.reshape(tok_rows * heads, head_dim)
    row_pos = jnp.repeat(positions, heads)
    lower_rows, upper_rows = (query_rows[: run_len * heads], query_rows[run_len * heads :])
    lower_pos, upper_pos = (row_pos[: run_len * heads], row_pos[run_len * heads :])
    all_pos = lax.all_gather(positions, ("outer", "inner"), axis=0, tiled=True)

    def fresh(count):
        return (
            jnp.full((count,), NEG, jnp.float32),
            jnp.zeros((count,), jnp.float32),
            jnp.zeros((count, head_dim), jnp.float32),
        )

    key_piece = lax.all_gather(keys, ("outer", "inner"), axis=0, tiled=True)
    value_piece = lax.all_gather(values, ("outer", "inner"), axis=0, tiled=True)
    count = key_piece.shape[0]
    shards = count // tok_rows
    keypos = lax.dynamic_slice_in_dim(all_pos, jnp.int32(0), count)
    key_split = key_piece.reshape(shards, 2, run_len, head_dim)
    value_split = value_piece.reshape(shards, 2, run_len, head_dim)
    pos_split = keypos.reshape(shards, 2, run_len)
    low_keys = key_split[:, 0].reshape(shards * run_len, head_dim)
    high_keys = key_split[:, 1].reshape(shards * run_len, head_dim)
    low_values = value_split[:, 0].reshape(shards * run_len, head_dim)
    high_values = value_split[:, 1].reshape(shards * run_len, head_dim)
    low_kpos = pos_split[:, 0].reshape(shards * run_len)
    high_kpos = pos_split[:, 1].reshape(shards * run_len)
    lower_state = fresh(run_len * heads)
    upper_state = fresh(run_len * heads)
    lower_state = attend_runs(
        lower_state, lower_rows, lower_pos, low_keys, low_values, low_kpos, True, scale
    )
    upper_state = attend_runs(
        upper_state, upper_rows, upper_pos, low_keys, low_values, low_kpos, False, scale
    )
    upper_state = attend_runs(
        upper_state, upper_rows, upper_pos, high_keys, high_values, high_kpos, True, scale
    )
    final = (lower_state, upper_state)
    lower_state, upper_state = final
    lower_out = lower_state[2] / lower_state[1][:, None]
    upper_out = upper_state[2] / upper_state[1][:, None]
    merged = jnp.concatenate([lower_out, upper_out], axis=0)
    return merged.astype(jnp.bfloat16).reshape(tok_rows, heads * head_dim)


def solution(mesh):
    return jax.shard_map(
        body,
        mesh=mesh,
        in_specs=(
            P(("outer", "inner"), None),
            P(("outer", "inner"), None),
            P(("outer", "inner"), None),
            P(("outer", "inner")),
        ),
        out_specs=P(("outer", "inner"), None),
        check_vma=False,
    )
```

profile of v0, /device:TPU:1, one launch (start us, length us, event | category | flops | bytes accessed | tf_op | source)
XLA Modules:
  0.0 1042.4 jit_solution(7931175948559206218)
XLA Ops:
  9.3 281.8 %all-gather = s32[128,1,256]{2,1,0:T(1,128)S(1)} all-gather(s32[1,1,256]{2,1,0:T(1,128)} %bitcast.118), channel_id=1, replica_groups=mesh['outer'=4,'inner'=32] {'outer','inner'}, dimensions={0}, use_global_device_ids=true | all-gather | bytes 132096 | tf_op jit(solution)/shard_map/all_gather | solution.py:66
  292.3 32.8 %all-gather.4.cloned.1.call-done = bf16[32768,128]{1,0:T(8,128)(2,1)} async-done(((bf16[256,128]{1,0:T(8,128)(2,1)}), bf16[32768,128]{1,0:T(8,128)(2,1)}) %all-gather.4.cloned.1.call-update) | async-done | bytes 8388624 | tf_op jit(solution)/shard_map/all_gather | solution.py:75
  325.1 6.0 fusion.60
  331.1 309.1 %all-gather.6.cloned.1.call-done = bf16[32768,128]{1,0:T(8,128)(2,1)} async-done(((bf16[256,128]{1,0:T(8,128)(2,1)}), bf16[32768,128]{1,0:T(8,128)(2,1)}) %all-gather.6.cloned.1.call-update) | async-done | bytes 8388624 | tf_op jit(solution)/shard_map/all_gather | solution.py:76
  640.2 6.0 fusion.59
  646.2 144.2 %while.47 = (s32[]{:T(128)}, f32[1024]{0:T(1024)S(1)}, f32[1024]{0:T(1024)S(1)}, f32[1024,128]{1,0:T(8,128)S(1)}, bf16[16,1024,128]{2,1,0:T(8,128)(2,1)}, /*inde...) while((s32[]{:T(128)}, f32[1024]{0:T(1024)S(1)}, ...), condition=%wide.region_7.8_spmd.clone, body=%wide.region_4.7_spmd.clone.sunk | while | flops 545657856 | bytes 31261828 | solution.py:52
  790.4 87.3 %while.45 = (s32[]{:T(128)}, f32[1024]{0:T(1024)S(1)}, f32[1024]{0:T(1024)S(1)}, f32[1024,128]{1,0:T(8,128)S(1)}, s32[16,1024]{1,0:T(8,128)S(1)}, /*index=5*/bf1...) while((s32[]{:T(128)}, f32[1024]{0:T(1024)S(1)}, ...), condition=%wide.region_11.12_spmd.clone, body=%wide.region_8.11_spmd.clone.sunk | while | flops 551815168 | bytes 14530153 | solution.py:52
  877.7 156.4 %while.46 = (s32[]{:T(128)}, f32[1024]{0:T(1024)S(1)}, f32[1024]{0:T(1024)S(1)}, f32[1024,128]{1,0:T(8,128)S(1)}, s32[16,1024]{1,0:T(8,128)S(1)}, /*index=5*/bf1...) while((s32[]{:T(128)}, f32[1024]{0:T(1024)S(1)}, ...), condition=%wide.region_3.4_spmd.clone, body=%wide.region_0.3_spmd.clone.sunk | while | flops 551949312 | bytes 31307416 | solution.py:52
  877.9 3.6 fusion.95
  887.7 3.6 fusion.95
  897.4 3.6 fusion.95
  907.2 3.6 fusion.95
  917.0 3.6 fusion.95
  926.8 3.6 fusion.95
  936.5 3.6 fusion.95
  946.3 3.6 fusion.95
  956.1 3.6 fusion.95
  965.9 3.6 fusion.95
  975.6 3.6 fusion.95
  985.4 3.6 fusion.95
  995.2 3.6 fusion.95
  1005.0 3.6 fusion.95
  1014.8 3.6 fusion.95
  1024.5 3.6 fusion.95
  (455 shorter events, 332.4 us)
Async XLA Ops:
  6.5 318.5 %all-gather.4.cloned.1.call-start = ((), (), s32[]{:S(2)}) async-start(), calls=%async_computation | async-start | bytes 8454144 | tf_op jit(solution)/shard_map/all_gather | solution.py:75
  7.3 632.9 %all-gather.6.cloned.1.call-start = ((), (), s32[]{:S(2)}) async-start(), calls=%async_computation.1 | async-start | bytes 8454144 | tf_op jit(solution)/shard_map/all_gather | solution.py:76
  649.8 3.4 copy-start
  658.8 3.4 copy-start
  667.8 3.4 copy-start
  676.8 3.4 copy-start
  685.8 3.4 copy-start
  694.8 3.4 copy-start
  703.9 3.4 copy-start
  712.9 3.4 copy-start
  721.9 3.4 copy-start
  730.9 3.4 copy-start
  739.9 3.4 copy-start
  748.9 3.4 copy-start
  757.9 3.4 copy-start
  766.9 3.4 copy-start
  775.9 3.4 copy-start
  784.9 3.4 copy-start
  881.5 3.4 copy-start.1
  891.3 3.4 copy-start.1
  901.1 3.4 copy-start.1
  959.7 3.4 copy-start.1
  969.5 3.4 copy-start.1
  979.3 3.4 copy-start.1
  (10 other events, 34.5 us)
Sparse Core Ops, SparseCore 0:
  9.0 315.9 all-gather.3
  326.8 313.3 all-gather.5
where the time goes:
time: 1050 us; the launch traced here: 1040 us
  waiting for transfers between devices  343 us (33%)
  blocking collectives  282 us (27%)
  matrix products  253 us (24%)
  other arithmetic  121 us (12%)
  local copies, waits for them, and re-layouts  27.9 us (3%)
  between operations  13.6 us (1%)
    all_gather x1, waiting for transfers between devices, body(): value_piece = lax.all_gather(values, ('outer', 'inner'), axis=0, tiled=True)  309 us
    all_gather x1, blocking collectives, body(): all_pos = lax.all_gather(positions, ('outer', 'inner'), axis=0, tiled=True)  282 us
    dot_general x48, matrix products, attend_block(): lax.dot_general(query_rows, key_block, (((1,), (1,)), ((), ())), preferre...  143 us
    reduce_sum x48, other arithmetic, attend_block(): total = total * factor + jnp.sum(expd, axis=1)  120 us
    dot_general x48, matrix products, attend_block(): jnp.dot(expd.astype(jnp.bfloat16), value_block, preferred_element_type=jn...  110 us
    all_gather x1, waiting for transfers between devices, body(): key_piece = lax.all_gather(keys, ('outer', 'inner'), axis=0, tiled=True)  32.8 us
  transfers between devices with their start and end apart: 2, of which 2 were waited for; matrix products, arithmetic and copies ran while one was open for 1% of the time, Pallas kernels for 0%

commit v1 on v0

v1 whole, which is shorter than its diff:
```python
import functools
import math

import jax
import jax.numpy as jnp
from jax import lax
from jax.experimental import pallas as pl
from jax.experimental.pallas import tpu as pltpu
from jax.sharding import PartitionSpec as P

AXES = ("outer", "inner")
RUN = 128
HD = 128
HEADS = 8
ROWS = RUN * HEADS
SHARD = 4 * RUN + 16
QROWS = 2 * RUN + 16
ACC = HD + 16
GROUP = 8
COEF = HD**-0.5 * math.log2(math.e)
NEG = -1e30
LIMIT = 2.0**100
VMEM_BYTES = 56 * 2**20


def dot(a, b, ca, cb):
    return lax.dot_general(a, b, (((ca,), (cb,)), ((), ())), preferred_element_type=jnp.float32)


def split3(x):
    hi = x.astype(jnp.bfloat16)
    rest = x - hi.astype(jnp.float32)
    mid = rest.astype(jnp.bfloat16)
    low = (rest - mid.astype(jnp.float32)).astype(jnp.bfloat16)
    return hi, mid, low


def stack_rows(rows, width):
    at = lax.broadcasted_iota(jnp.int32, (16, width), 0)
    tile = jnp.zeros((16, width), jnp.float32)
    for i, row in enumerate(rows):
        tile = jnp.where(at == i, row.astype(jnp.float32), tile)
    return tile.astype(jnp.bfloat16)


def pack_kv_kernel(pos_ref, key_ref, value_ref, out_ref):
    out_ref[0 : 2 * RUN, :] = key_ref[...]
    for half in range(2):
        v = value_ref[half * RUN : (half + 1) * RUN, :].astype(jnp.float32)
        out_ref[(2 + half) * RUN : (3 + half) * RUN, :] = v.T.astype(jnp.bfloat16)
    block = (pos_ref[0] // RUN).astype(jnp.float32)
    out_ref[4 * RUN : SHARD, :] = jnp.full((16, HD), block, jnp.float32).astype(jnp.bfloat16)


def pack_kv(positions, keys, values):
    return pl.pallas_call(
        pack_kv_kernel,
        out_shape=jax.ShapeDtypeStruct((SHARD, HD), jnp.bfloat16),
        in_specs=[
            pl.BlockSpec(memory_space=pltpu.SMEM),
            pl.BlockSpec(memory_space=pltpu.VMEM),
            pl.BlockSpec(memory_space=pltpu.VMEM),
        ],
        out_specs=pl.BlockSpec(memory_space=pltpu.VMEM),
        name="pack_kv",
    )(positions, keys, values)


def query_tile(ref, half):
    rows = slice(half * RUN, (half + 1) * RUN)
    return jnp.concatenate([ref[rows, h * HD : (h + 1) * HD] for h in range(HEADS)], axis=0)


def pack_q_kernel(query_ref, shard_ref, out_ref, acc_ref):
    out_ref[0 : 2 * RUN, :] = query_ref[...]
    shifts = []
    key_at = lax.broadcasted_iota(jnp.int32, (RUN, ROWS), 0)
    row_at = lax.broadcasted_iota(jnp.int32, (RUN, ROWS), 1) % RUN
    ones = jnp.ones((16, RUN), jnp.bfloat16)
    for half in range(2):
        scores = dot(shard_ref[half * RUN : (half + 1) * RUN, :], query_tile(query_ref, half), 1, 1)
        scores = jnp.where(key_at <= row_at, scores * COEF, NEG)
        shift = jnp.max(scores, axis=0, keepdims=True)
        weights = jnp.exp2(scores - shift).astype(jnp.bfloat16)
        vt = jnp.concatenate([shard_ref[(2 + half) * RUN : (3 + half) * RUN, :], ones], axis=0)
        acc_ref[:, half * ROWS : (half + 1) * ROWS] = dot(vt, weights, 1, 0)
        shifts.append(shift)
    block = jnp.concatenate([shard_ref[4 * RUN : 4 * RUN + 1, :]] * HEADS, axis=1)
    out_ref[2 * RUN : QROWS, :] = stack_rows(split3(shifts[0]) + split3(shifts[1]) + (block,), ROWS)


def pack_q(queries, shard):
    return pl.pallas_call(
        pack_q_kernel,
        out_shape=(
            jax.ShapeDtypeStruct((QROWS, ROWS), jnp.bfloat16),
            jax.ShapeDtypeStruct((ACC, 2 * ROWS), jnp.float32),
        ),
        in_specs=[pl.BlockSpec(memory_space=pltpu.VMEM)] * 2,
        out_specs=(pl.BlockSpec(memory_space=pltpu.VMEM),) * 2,
        compiler_params=pltpu.CompilerParams(vmem_limit_bytes=VMEM_BYTES),
        name="pack_q",
    )(queries, shard)


def attend_kernel(count, shards, own, *refs):
    q_refs = refs[:count]
    kv_ref = refs[count]
    at = count + 1
    acc0_ref = None
    if own:
        acc0_ref = refs[at]
        at += 1
    out_refs = refs[at : at + count]
    q_buf, m_buf, acc_ref, ints, blocks, tasks, sem = refs[at + count :]
    total = 2 * shards

    for i in range(shards):
        row = kv_ref[i * SHARD + 4 * RUN : i * SHARD + SHARD, :].astype(jnp.float32)[0:1]
        ints[i : i + 1, :] = row.astype(jnp.int32)
    for j in range(count):
        row = q_refs[j][2 * RUN : QROWS, 0:HD].astype(jnp.float32)[6:7]
        ints[shards + j : shards + j + 1, :] = row.astype(jnp.int32)
    copy = pltpu.make_async_copy(ints, blocks, sem)
    copy.start()
    copy.wait()

    def key_block(task):
        shard = task // 2
        start = pl.multiple_of(shard * SHARD + (task - 2 * shard) * RUN, 16)
        return kv_ref[pl.ds(start, RUN), :]

    def value_block(task):
        shard = task // 2
        start = pl.multiple_of(shard * SHARD + (2 + task - 2 * shard) * RUN, 16)
        return kv_ref[pl.ds(start, RUN), :]

    ones = jnp.ones((16, GROUP * RUN), jnp.bfloat16)

    for j in range(count):
        q_ref = q_refs[j]
        here = blocks[shards + j, 0]
        tail = q_ref[2 * RUN : QROWS, :].astype(jnp.float32)
        for half in range(2):
            q_buf[half] = query_tile(q_ref, half)
            m_buf[half] = jnp.broadcast_to(
                tail[3 * half : 3 * half + 1]
                + tail[3 * half + 1 : 3 * half + 2]
                + tail[3 * half + 2 : 3 * half + 3],
                (8, ROWS),
            )
            if own:
                acc_ref[half] = acc0_ref[:, half * ROWS : (half + 1) * ROWS]
            else:
                acc_ref[half] = jnp.zeros((ACC, ROWS), jnp.float32)

        def place(i, ends):
            low, high = ends
            block = blocks[i, 0]
            tasks[high] = 2 * i
            high = high - 1
            later = block > here
            tasks[jnp.where(later, high, total)] = 2 * i + 1
            high = high - later.astype(jnp.int32)
            earlier = block < here
            tasks[jnp.where(earlier, low, total)] = 2 * i
            low = low + earlier.astype(jnp.int32)
            return low, high

        for i in range(total):
            tasks[i] = 0
        low_end, high_end = lax.fori_loop(0, shards, place, (jnp.int32(0), jnp.int32(total - 1)))
        high_start = high_end + 1

        def pure(first, half):
            query = q_buf[half]
            shift = m_buf[half][0:1]
            parts = []
            for b in range(0, GROUP, 2):
                keys = jnp.concatenate([key_block(tasks[first + b]), key_block(tasks[first + b + 1])], axis=0)
                parts.append(jnp.exp2(dot(keys, query, 1, 1) * COEF - shift).astype(jnp.bfloat16))
            weights = jnp.concatenate(parts, axis=0)
            vt = jnp.concatenate([value_block(tasks[first + b]) for b in range(GROUP)], axis=1)
            vt = jnp.concatenate([vt, ones], axis=0)
            acc_ref[half] += dot(vt, weights, 1, 0)

        def mixed(first):
            parts = []
            for b in range(GROUP):
                half = (first + b >= high_start).astype(jnp.int32)
                scores = dot(key_block(tasks[first + b]), q_buf[half], 1, 1)
                parts.append(jnp.exp2(scores * COEF - m_buf[half][0:1]).astype(jnp.bfloat16))
            weights = jnp.concatenate(parts, axis=0)
            vt = jnp.concatenate([value_block(tasks[first + b]) for b in range(GROUP)], axis=1)
            vt = jnp.concatenate([vt, ones], axis=0)
            index = first + lax.broadcasted_iota(jnp.int32, (1, GROUP * RUN), 1) // RUN
            zero = jnp.zeros((), jnp.bfloat16)
            acc_ref[0] += dot(jnp.where(index < low_end, vt, zero), weights, 1, 0)
            acc_ref[1] += dot(jnp.where(index >= high_start, vt, zero), weights, 1, 0)

        @pl.loop(0, total // GROUP)
        def _(g):
            first = g * GROUP
            is_low = first + GROUP <= low_end
            is_high = first >= high_start

            @pl.when(jnp.logical_or(is_low, is_high))
            def _():
                pure(first, is_high.astype(jnp.int32))

            @pl.when(jnp.logical_not(jnp.logical_or(is_low, is_high)))
            def _():
                mixed(first)

        sums = jnp.maximum(acc_ref[0][HD : HD + 8], acc_ref[1][HD : HD + 8])
        fine = jnp.min(jnp.where(sums < LIMIT, 1.0, 0.0)) > 0.5

        @pl.when(jnp.logical_not(fine))
        def _():
            for half in range(2):
                if own:
                    acc_ref[half] = acc0_ref[:, half * ROWS : (half + 1) * ROWS]
                else:
                    acc_ref[half] = jnp.zeros((ACC, ROWS), jnp.float32)

            @pl.loop(0, total)
            def _(t):
                @pl.when(jnp.logical_or(t < low_end, t >= high_start))
                def _():
                    half = (t >= high_start).astype(jnp.int32)
                    scores = dot(key_block(tasks[t]), q_buf[half], 1, 1) * COEF
                    old = m_buf[half][0:1]
                    new = jnp.maximum(old, jnp.max(scores, axis=0, keepdims=True))
                    weights = jnp.exp2(scores - new).astype(jnp.bfloat16)
                    vt = jnp.concatenate([value_block(tasks[t]), ones[:, :RUN]], axis=0)
                    acc_ref[half] = acc_ref[half] * jnp.exp2(old - new) + dot(vt, weights, 1, 0)
                    m_buf[half] = jnp.broadcast_to(new, (8, ROWS))

        for half in range(2):
            span = slice(half * ROWS, (half + 1) * ROWS)
            if own:
                out_refs[j][0 : HD + 8, span] = acc_ref[half][0 : HD + 8]
                out_refs[j][HD + 8 : ACC, span] = m_buf[half]
            else:
                acc = acc_ref[half]
                out_refs[j][0:HD, span] = acc[0:HD].astype(jnp.bfloat16)
                out_refs[j][HD:ACC, span] = stack_rows(
                    split3(acc[HD : HD + 1]) + split3(m_buf[half][0:1]), ROWS
                )


def attend(q_list, kv, acc0=None):
    count, shards = len(q_list), kv.shape[0] // SHARD
    own = acc0 is not None
    int_rows = -(-(shards + count) // 8) * 8
    args = tuple(q_list) + (kv,) + ((acc0,) if own else ())
    out = jax.ShapeDtypeStruct((ACC, 2 * ROWS), jnp.float32 if own else jnp.bfloat16)
    pairs = count * 2 * shards * RUN * ROWS
    return pl.pallas_call(
        functools.partial(attend_kernel, count, shards, own),
        out_shape=(out,) * count,
        in_specs=[pl.BlockSpec(memory_space=pltpu.VMEM)] * len(args),
        out_specs=(pl.BlockSpec(memory_space=pltpu.VMEM),) * count,
        scratch_shapes=[
            pltpu.VMEM((2, ROWS, HD), jnp.bfloat16),
            pltpu.VMEM((2, 8, ROWS), jnp.float32),
            pltpu.VMEM((2, ACC, ROWS), jnp.float32),
            pltpu.VMEM((int_rows, HD), jnp.int32),
            pltpu.SMEM((int_rows, HD), jnp.int32),
            pltpu.SMEM((2 * shards + 8,), jnp.int32),
            pltpu.SemaphoreType.DMA,
        ],
        compiler_params=pltpu.CompilerParams(vmem_limit_bytes=VMEM_BYTES),
        cost_estimate=pl.CostEstimate(flops=pairs * HD * 8, bytes_accessed=8 << 20, transcendentals=pairs),
        name="attend",
    )(*args)


def combine_kernel(own_ref, one_ref, two_ref, three_ref, out_ref):
    for half in range(2):
        for h in range(HEADS):
            span = slice(half * ROWS + h * RUN, half * ROWS + (h + 1) * RUN)
            parts = [(own_ref[0:HD, span], own_ref[HD : HD + 1, span], own_ref[HD + 8 : HD + 9, span])]
            for ref in (one_ref, two_ref, three_ref):
                tail = ref[HD:ACC, span].astype(jnp.float32)
                parts.append(
                    (
                        ref[0:HD, span].astype(jnp.float32),
                        tail[0:1] + tail[1:2] + tail[2:3],
                        tail[3:4] + tail[4:5] + tail[5:6],
                    )
                )
            top = functools.reduce(jnp.maximum, [p[2] for p in parts])
            factors = [jnp.exp2(p[2] - top) for p in parts]
            numer = sum(p[0] * f for p, f in zip(parts, factors))
            total = sum(p[1] * f for p, f in zip(parts, factors))
            out_ref[half * RUN : (half + 1) * RUN, h * HD : (h + 1) * HD] = (
                (numer / total).T.astype(jnp.bfloat16)
            )


def combine(own, others):
    return pl.pallas_call(
        combine_kernel,
        out_shape=jax.ShapeDtypeStruct((2 * RUN, ROWS), jnp.bfloat16),
        in_specs=[pl.BlockSpec(memory_space=pltpu.VMEM)] * 4,
        out_specs=pl.BlockSpec(memory_space=pltpu.VMEM),
        compiler_params=pltpu.CompilerParams(vmem_limit_bytes=VMEM_BYTES),
        name="combine",
    )(own, *others)


def place_of(x, y, z, core):
    return ((x // 2) * 2 + core) * 32 + (y * 4 + z) * 2 + x % 2


def swap(array, flips):
    pairs = []
    for x in range(4):
        for y in range(4):
            for z in range(4):
                for core in range(2):
                    dx, dy, dz, dc = flips(core)
                    pairs.append((place_of(x, y, z, core), place_of(x ^ dx, y ^ dy, z ^ dz, core ^ dc)))
    return lax.ppermute(array, AXES, pairs)


def ring_x(array, step):
    return swap(array, lambda core: (step, 0, 0, 0))


def ring_first(array, step):
    return swap(array, lambda core: (0, step, 0, 0) if core else (0, 0, step, 0))


def ring_second(array, step):
    return swap(array, lambda core: (0, 0, step, 0) if core else (0, step, 0, 0))


def cores(array):
    return swap(array, lambda core: (0, 0, 0, 1))


STEPS = (1, 3, 2)


def body(queries, keys, values, positions):
    shard = pack_kv(positions, keys, values)
    near = [ring_first(shard, s) for s in STEPS]
    packed, acc0 = pack_q(queries, shard)
    others = [ring_x(packed, s) for s in STEPS]
    line = jnp.concatenate([shard] + near, axis=0)
    far = [ring_second(line, s) for s in STEPS]
    plane = jnp.concatenate([line] + far, axis=0)
    kv = jnp.concatenate([plane, cores(plane)], axis=0)
    part1, part3 = attend(others[:2], kv)
    back1, back3 = ring_x(part1, 1), ring_x(part3, 3)
    (part2,) = attend(others[2:], kv)
    back2 = ring_x(part2, 2)
    (mine,) = attend([packed], kv, acc0)
    return combine(mine, (back1, back3, back2))


def solution(mesh):
    return jax.shard_map(
        body,
        mesh=mesh,
        in_specs=(P(AXES, None), P(AXES, None), P(AXES, None), P(AXES)),
        out_specs=P(AXES, None),
        check_vma=False,
    )
```

time: 1050 us -> 131 us (0.12)
  waiting for transfers between devices: 343 us -> 38.5 us
  blocking collectives: 282 us -> 0 us
  matrix products: 253 us -> 0 us
  other arithmetic: 121 us -> 0.94 us
  Pallas kernels: 0 us -> 59.8 us
  starting transfers between devices: 0.04 us -> 22.5 us
  local copies, waits for them, and re-layouts: 27.9 us -> 8.4 us
  between operations: 13.6 us -> 0.14 us
    all_gather x2 -> x0, waiting for transfers between devices: 342 us -> none  [the longest x1 309 us: body(): value_piece = lax.all_gather(values, ('outer', 'inner'), axis=0, tiled=True)]
    all_gather x1 -> x0, blocking collectives: 282 us -> none  [body(): all_pos = lax.all_gather(positions, ('outer', 'inner'), axis=0, tiled=True)]
    dot_general x96 -> x0, matrix products: 253 us -> none  [the longest x48 143 us: attend_block(): lax.dot_general(query_rows, key_block, (((1,), (1,)), ((), ())), preferre...]
    reduce_sum x48 -> x0, other arithmetic: 120 us -> none  [attend_block(): total = total * factor + jnp.sum(expd, axis=1)]
    pallas_call x0 -> x6, Pallas kernels: none -> 59.8 us  [the longest x3 51.9 us: attend(): pl.pallas_call(functools.partial(attend_kernel, count, shards, own), out_...]
    ppermute x0 -> x13, waiting for transfers between devices: none -> 38.5 us  [swap(): return lax.ppermute(array, AXES, pairs)]
    ppermute x0 -> x13, starting transfers between devices: none -> 22.5 us  [swap(): return lax.ppermute(array, AXES, pairs)]
    slice x41 -> x0, local copies, waits for them, and re-layouts: 17.5 us -> none  [the longest x1 6.03 us: body(): high_keys = key_split[:, 1].reshape(shards * run_len, head_dim)]
  transfers between devices with their start and end apart: 2 -> 13, of which waited for: 2 -> 7; matrix products, arithmetic and copies ran while one was open for 1% -> 2% of each run, Pallas kernels for 0% -> 42%
where the time goes in v1:
time: 131 us; the launch traced here: 130 us
  Pallas kernels  59.8 us (46%)
  waiting for transfers between devices  38.5 us (29%)
  starting transfers between devices  22.5 us (17%)
  local copies, waits for them, and re-layouts  8.4 us (6%)
    pallas_call x3, Pallas kernels, attend(): pl.pallas_call(functools.partial(attend_kernel, count, shards, own), out_...  51.9 us
    ppermute x13, waiting for transfers between devices, swap(): return lax.ppermute(array, AXES, pairs)  38.5 us
    ppermute x13, starting transfers between devices, swap(): return lax.ppermute(array, AXES, pairs)  22.5 us
    unnamed x20, local copies, waits for them, and re-layouts  6.84 us
    pallas_call x1, Pallas kernels, combine(): pl.pallas_call(combine_kernel, out_shape=jax.ShapeDtypeStruct((2 * RUN, R...  3.16 us
    pallas_call x1, Pallas kernels, pack_q(): pl.pallas_call(pack_q_kernel, out_shape=(jax.ShapeDtypeStruct((QROWS, ROW...  3.11 us
  transfers between devices with their start and end apart: 13, of which 7 were waited for; matrix products, arithmetic and copies ran while one was open for 2% of the time, Pallas kernels for 42%

profile of v1, /device:TPU:1, one launch (start us, length us, event | category | flops | bytes accessed | tf_op | source)
XLA Modules:
  0.0 130.3 jit_solution(1668844006613387807)
XLA Ops:
  0.0 1.6 %pack_kv.1.shard_ref = bf16[528,128]{1,0:T(8,128)(2,1)} custom-call(s32[256]{0:T(256)} %pos_ref.1, bf16[256,128]{1,0:T(8,128)(2,1)} %key_ref.1, bf16[256,128]{1,0:T(8,128)(2,1)} %value_ref.1), custom_call_target="tpu_custom_call" | custom-call | tf_op jit(solution)/shard_map/pack_kv/pallas_call | solution.py:56
  1.6 2.1 %collective-permute-start = (bf16[528,128]{1,0:T(8,128)(2,1)}, bf16[528,128]{1,0:T(8,128)(2,1)S(1)}, u32[]{:S(2)}, u32[]{:S(2)}) collective-permute-start(bf16[528,128]{1,0:T(8,128)(2,1)} %pack_kv.1.shard_ref), channel_id=1, source_target_pairs={{0,2},{32,40},{2,0},{34,42},{4,6},{36,44},{6,4},{38,46},{8,10},{40... | collective-permute-start | bytes 405512 | tf_op jit(solution)/shard_map/ppermute | solution.py:325
  3.8 1.9 %collective-permute-start.1 = (bf16[528,128]{1,0:T(8,128)(2,1)}, bf16[528,128]{1,0:T(8,128)(2,1)S(1)}, u32[]{:S(2)}, u32[]{:S(2)}) collective-permute-start(bf16[528,128]{1,0:T(8,128)(2,1)} %pack_kv.1.shard_ref), channel_id=1, source_target_pairs={{0,6},{32,56},{2,4},{34,58},{4,2},{36,60},{6,0},{38,62},{8,14},{40... | collective-permute-start | bytes 405512 | tf_op jit(solution)/shard_map/ppermute | solution.py:325
  6.7 2.8 %collective-permute-done.1 = bf16[528,128]{1,0:T(8,128)(2,1)S(1)} collective-permute-done((bf16[528,128]{1,0:T(8,128)(2,1)}, bf16[528,128]{1,0:T(8,128)(2,1)S(1)}, u32[]{:S(2)}, u32[]{:S(2)}) %collective-permute-start.1) | collective-permute-done | bytes 135200 | tf_op jit(solution)/shard_map/ppermute | solution.py:325
  9.4 1.8 %collective-permute-done.2 = bf16[528,128]{1,0:T(8,128)(2,1)S(1)} collective-permute-done((bf16[528,128]{1,0:T(8,128)(2,1)}, bf16[528,128]{1,0:T(8,128)(2,1)S(1)}, u32[]{:S(2)}, u32[]{:S(2)}) %collective-permute-start.2) | collective-permute-done | bytes 135200 | tf_op jit(solution)/shard_map/ppermute | solution.py:325
  12.2 1.7 %collective-permute-start.3 = (bf16[2112,128]{1,0:T(8,128)(2,1)S(1)}, bf16[2112,128]{1,0:T(8,128)(2,1)S(1)}, u32[]{:S(2)}, u32[]{:S(2)}) collective-permute-start(bf16[2112,128]{1,0:T(8,128)(2,1)S(1)} %pad_maximum_fusion), channel_id=1, source_target_pairs={{0,8},{32,34},{2,10},{34,32},{4,12},{36,38},{6,14},{38,36},{8,0},{... | collective-permute-start | bytes 1622024 | tf_op jit(solution)/shard_map/ppermute | solution.py:325
  14.9 2.3 %collective-permute-start.4 = (bf16[2112,128]{1,0:T(8,128)(2,1)S(1)}, bf16[2112,128]{1,0:T(8,128)(2,1)S(1)}, u32[]{:S(2)}, u32[]{:S(2)}) collective-permute-start(bf16[2112,128]{1,0:T(8,128)(2,1)S(1)} %pad_maximum_fusion), channel_id=1, source_target_pairs={{0,24},{32,38},{2,26},{34,36},{4,28},{36,34},{6,30},{38,32},{8,16}... | collective-permute-start | bytes 1622024 | tf_op jit(solution)/shard_map/ppermute | solution.py:325
  17.2 1.2 collective-permute-start.5
  18.5 2.5 %collective-permute-done.3 = bf16[2112,128]{1,0:T(8,128)(2,1)S(1)} collective-permute-done((bf16[2112,128]{1,0:T(8,128)(2,1)S(1)}, bf16[2112,128]{1,0:T(8,128)(2,1)S(1)}, u32[]{:S(2)}, u32[]{:S(2)}) %collective-permute-start.3) | collective-permute-done | bytes 540704 | tf_op jit(solution)/shard_map/ppermute | solution.py:325
  21.1 9.3 %collective-permute-done.4 = bf16[2112,128]{1,0:T(8,128)(2,1)S(1)} collective-permute-done((bf16[2112,128]{1,0:T(8,128)(2,1)S(1)}, bf16[2112,128]{1,0:T(8,128)(2,1)S(1)}, u32[]{:S(2)}, u32[]{:S(2)}) %collective-permute-start.4) | collective-permute-done | bytes 540704 | tf_op jit(solution)/shard_map/ppermute | solution.py:325
  30.8 2.0 %copy-done.3 = bf16[16896,128]{1,0:T(8,128)(2,1)} copy-done((bf16[16896,128]{1,0:T(8,128)(2,1)}, bf16[16896,128]{1,0:T(8,128)(2,1)S(1)}, u32[]{:S(2)}) %copy-start.3) | copy-done | bytes 4325400
  32.7 3.9 %collective-permute-start.6 = (bf16[8448,128]{1,0:T(8,128)(2,1)S(1)}, bf16[8448,128]{1,0:T(8,128)(2,1)S(1)}, u32[]{:S(2)}, u32[]{:S(2)}) collective-permute-start(bf16[8448,128]{1,0:T(8,128)(2,1)S(1)} %get-tuple-element.13), channel_id=1, source_target_pairs={{0,32},{32,0},{2,34},{34,2},{4,36},{36,4},{6,38},{38,6},{8,40},{40... | collective-permute-start | bytes 6488072 | tf_op jit(solution)/shard_map/ppermute | solution.py:325
  36.6 3.1 %pack_q.1 = (bf16[272,1024]{1,0:T(8,128)(2,1)}, f32[144,2048]{1,0:T(8,128)}) custom-call(bf16[256,1024]{1,0:T(8,128)(2,1)} %query_ref.1, bf16[528,128]{1,0:T(8,128)(2,1)} %pack_kv.1.shard_ref), custom_call_target="tpu_custom_call" | custom-call | tf_op jit(solution)/shard_map/pack_q/pallas_call | solution.py:93
  39.7 1.2 collective-permute-start.7
  40.9 1.8 %collective-permute-start.8 = (bf16[272,1024]{1,0:T(8,128)(2,1)}, bf16[272,1024]{1,0:T(8,128)(2,1)S(1)}, u32[]{:S(2)}, u32[]{:S(2)}) collective-permute-start(bf16[272,1024]{1,0:T(8,128)(2,1)} %get-tuple-element.9.refs_0_), channel_id=1, source_target_pairs={{0,65},{32,97},{2,67},{34,99},{4,69},{36,101},{6,71},{38,103},{8,7... | collective-permute-start | bytes 1671176 | tf_op jit(solution)/shard_map/ppermute | solution.py:325
  43.4 1.4 %constant_dynamic-update-slice_fusion.7.refs_1_.refs_2_ = bf16[16896,128]{1,0:T(8,128)(2,1)} fusion(bf16[16896,128]{1,0:T(8,128)(2,1)} %copy-done.3, bf16[8448,128]{1,0:T(8,128)(2,1)S(1)} %collective-permute-done.6), kind=kLoop, calls=%fused_computation.8 | loop fusion | bytes 4325376 | tf_op jit(solution)/shard_map/concatenate | solution.py:355
  44.8 9.4 %collective-permute-done.7.refs_0_ = bf16[272,1024]{1,0:T(8,128)(2,1)S(1)} collective-permute-done((bf16[272,1024]{1,0:T(8,128)(2,1)}, bf16[272,1024]{1,0:T(8,128)(2,1)S(1)}, u32[]{:S(2)}, u32[]{:S(2)}) %collective-permute-start.7) | collective-permute-done | bytes 557088 | tf_op jit(solution)/shard_map/ppermute | solution.py:325
  54.2 12.4 %collective-permute-done.8.refs_1_ = bf16[272,1024]{1,0:T(8,128)(2,1)S(1)} collective-permute-done((bf16[272,1024]{1,0:T(8,128)(2,1)}, bf16[272,1024]{1,0:T(8,128)(2,1)S(1)}, u32[]{:S(2)}, u32[]{:S(2)}) %collective-permute-start.8) | collective-permute-done | bytes 557088 | tf_op jit(solution)/shard_map/ppermute | solution.py:325
  67.4 23.7 %attend.4 = (bf16[144,2048]{1,0:T(8,128)(2,1)}, bf16[144,2048]{1,0:T(8,128)(2,1)}) custom-call(bf16[272,1024]{1,0:T(8,128)(2,1)} %copy-done.5, bf16[272,1024]{1,0:T(8,128)(2,1)} %copy-done.6, bf16[16896,128]{1,0:T(8,128)(2,1)} %constant_dynamic-update-slice_fusion.7.refs_1_.refs_2_), custom_call_target="tpu_custom_call" | custom-call | flops 17179869184 | bytes 8388608 | tf_op jit(solution)/shard_map/attend/pallas_call | solution.py:259
  91.2 3.5 %collective-permute-start.10 = (bf16[144,2048]{1,0:T(8,128)(2,1)}, bf16[144,2048]{1,0:T(8,128)(2,1)S(1)}, u32[]{:S(2)}, u32[]{:S(2)}) collective-permute-start(bf16[144,2048]{1,0:T(8,128)(2,1)} %get-tuple-element.12), channel_id=1, source_target_pairs={{0,65},{32,97},{2,67},{34,99},{4,69},{36,101},{6,71},{38,103},{8,7... | collective-permute-start | bytes 1769480 | tf_op jit(solution)/shard_map/ppermute | solution.py:325
  95.5 13.8 %attend.5 = bf16[144,2048]{1,0:T(8,128)(2,1)} custom-call(bf16[272,1024]{1,0:T(8,128)(2,1)} %copy-done.4, bf16[16896,128]{1,0:T(8,128)(2,1)} %constant_dynamic-update-slice_fusion.7.refs_1_.refs_2_), custom_call_target="tpu_custom_call" | custom-call | flops 8589934592 | bytes 8388608 | tf_op jit(solution)/shard_map/attend/pallas_call | solution.py:259
  109.4 1.5 %collective-permute-start.12 = (bf16[144,2048]{1,0:T(8,128)(2,1)}, bf16[144,2048]{1,0:T(8,128)(2,1)S(1)}, u32[]{:S(2)}, u32[]{:S(2)}) collective-permute-start(bf16[144,2048]{1,0:T(8,128)(2,1)} %attend.5), channel_id=1, source_target_pairs={{0,64},{32,96},{2,66},{34,98},{4,68},{36,100},{6,70},{38,102},{8,7... | collective-permute-start | bytes 1769480 | tf_op jit(solution)/shard_map/ppermute | solution.py:325
  110.9 14.3 %attend.3.own_ref = f32[144,2048]{1,0:T(8,128)} custom-call(bf16[272,1024]{1,0:T(8,128)(2,1)} %get-tuple-element.9.refs_0_, bf16[16896,128]{1,0:T(8,128)(2,1)} %constant_dynamic-update-slice_fusion.7.refs_1_.refs_2_, f32[144,2048]{1,0:T(8,128)} %get-tuple-element.10.refs_2_), custom_call_target="tpu_custom_call" | custom-call | flops 8589934592 | bytes 8388608 | tf_op jit(solution)/shard_map/attend/pallas_call | solution.py:259
  127.1 3.2 %combine.1 = bf16[256,1024]{1,0:T(8,128)(2,1)} custom-call(f32[144,2048]{1,0:T(8,128)} %attend.3.own_ref, bf16[144,2048]{1,0:T(8,128)(2,1)} %copy-done.1, bf16[144,2048]{1,0:T(8,128)(2,1)} %copy-done, bf16[144,2048]{1,0:T(8,128)(2,1)} %copy-done.2), custom_call_target="tpu_custom_call" | custom-call | tf_op jit(solution)/shard_map/combine/pallas_call | solution.py:303
  (31 shorter events, 7.6 us)
Async XLA Ops:
  1.6 5.0 %collective-permute-start = (bf16[528,128]{1,0:T(8,128)(2,1)}, bf16[528,128]{1,0:T(8,128)(2,1)S(1)}, u32[]{:S(2)}, u32[]{:S(2)}) collective-permute-start(bf16[528,128]{1,0:T(8,128)(2,1)} %pack_kv.1.shard_ref), channel_id=1, source_target_pairs={{0,2},{32,40},{2,0},{34,42},{4,6},{36,44},{6,4},{38,46},{8,10},{40... | collective-permute-start | bytes 405512 | tf_op jit(solution)/shard_map/ppermute | solution.py:325
  3.8 5.7 %collective-permute-start.1 = (bf16[528,128]{1,0:T(8,128)(2,1)}, bf16[528,128]{1,0:T(8,128)(2,1)S(1)}, u32[]{:S(2)}, u32[]{:S(2)}) collective-permute-start(bf16[528,128]{1,0:T(8,128)(2,1)} %pack_kv.1.shard_ref), channel_id=1, source_target_pairs={{0,6},{32,56},{2,4},{34,58},{4,2},{36,60},{6,0},{38,62},{8,14},{40... | collective-permute-start | bytes 405512 | tf_op jit(solution)/shard_map/ppermute | solution.py:325
  5.7 5.6 %collective-permute-start.2 = (bf16[528,128]{1,0:T(8,128)(2,1)}, bf16[528,128]{1,0:T(8,128)(2,1)S(1)}, u32[]{:S(2)}, u32[]{:S(2)}) collective-permute-start(bf16[528,128]{1,0:T(8,128)(2,1)} %pack_kv.1.shard_ref), channel_id=1, source_target_pairs={{0,4},{32,48},{2,6},{34,50},{4,0},{36,52},{6,2},{38,54},{8,12},{40... | collective-permute-start | bytes 405512 | tf_op jit(solution)/shard_map/ppermute | solution.py:325
  12.2 8.8 %collective-permute-start.3 = (bf16[2112,128]{1,0:T(8,128)(2,1)S(1)}, bf16[2112,128]{1,0:T(8,128)(2,1)S(1)}, u32[]{:S(2)}, u32[]{:S(2)}) collective-permute-start(bf16[2112,128]{1,0:T(8,128)(2,1)S(1)} %pad_maximum_fusion), channel_id=1, source_target_pairs={{0,8},{32,34},{2,10},{34,32},{4,12},{36,38},{6,14},{38,36},{8,0},{... | collective-permute-start | bytes 1622024 | tf_op jit(solution)/shard_map/ppermute | solution.py:325
  14.9 15.6 %collective-permute-start.4 = (bf16[2112,128]{1,0:T(8,128)(2,1)S(1)}, bf16[2112,128]{1,0:T(8,128)(2,1)S(1)}, u32[]{:S(2)}, u32[]{:S(2)}) collective-permute-start(bf16[2112,128]{1,0:T(8,128)(2,1)S(1)} %pad_maximum_fusion), channel_id=1, source_target_pairs={{0,24},{32,38},{2,26},{34,36},{4,28},{36,34},{6,30},{38,32},{8,16}... | collective-permute-start | bytes 1622024 | tf_op jit(solution)/shard_map/ppermute | solution.py:325
  17.2 13.4 %collective-permute-start.5 = (bf16[2112,128]{1,0:T(8,128)(2,1)S(1)}, bf16[2112,128]{1,0:T(8,128)(2,1)S(1)}, u32[]{:S(2)}, u32[]{:S(2)}) collective-permute-start(bf16[2112,128]{1,0:T(8,128)(2,1)S(1)} %pad_maximum_fusion), channel_id=1, source_target_pairs={{0,16},{32,36},{2,18},{34,38},{4,20},{36,32},{6,22},{38,34},{8,24}... | collective-permute-start | bytes 1622024 | tf_op jit(solution)/shard_map/ppermute | solution.py:325
  30.7 2.0 %copy-start.3 = (bf16[16896,128]{1,0:T(8,128)(2,1)}, bf16[16896,128]{1,0:T(8,128)(2,1)S(1)}, u32[]{:S(2)}) copy-start(bf16[16896,128]{1,0:T(8,128)(2,1)S(1)} %get-tuple-element.14) | copy-start | bytes 12976132
  32.7 10.6 %collective-permute-start.6 = (bf16[8448,128]{1,0:T(8,128)(2,1)S(1)}, bf16[8448,128]{1,0:T(8,128)(2,1)S(1)}, u32[]{:S(2)}, u32[]{:S(2)}) collective-permute-start(bf16[8448,128]{1,0:T(8,128)(2,1)S(1)} %get-tuple-element.13), channel_id=1, source_target_pairs={{0,32},{32,0},{2,34},{34,2},{4,36},{36,4},{6,38},{38,6},{8,40},{40... | collective-permute-start | bytes 6488072 | tf_op jit(solution)/shard_map/ppermute | solution.py:325
  39.7 14.5 %collective-permute-start.7 = (bf16[272,1024]{1,0:T(8,128)(2,1)}, bf16[272,1024]{1,0:T(8,128)(2,1)S(1)}, u32[]{:S(2)}, u32[]{:S(2)}) collective-permute-start(bf16[272,1024]{1,0:T(8,128)(2,1)} %get-tuple-element.9.refs_0_), channel_id=1, source_target_pairs={{0,1},{32,33},{2,3},{34,35},{4,5},{36,37},{6,7},{38,39},{8,9},{40,... | collective-permute-start | bytes 1671176 | tf_op jit(solution)/shard_map/ppermute | solution.py:325
  40.9 25.7 %collective-permute-start.8 = (bf16[272,1024]{1,0:T(8,128)(2,1)}, bf16[272,1024]{1,0:T(8,128)(2,1)S(1)}, u32[]{:S(2)}, u32[]{:S(2)}) collective-permute-start(bf16[272,1024]{1,0:T(8,128)(2,1)} %get-tuple-element.9.refs_0_), channel_id=1, source_target_pairs={{0,65},{32,97},{2,67},{34,99},{4,69},{36,101},{6,71},{38,103},{8,7... | collective-permute-start | bytes 1671176 | tf_op jit(solution)/shard_map/ppermute | solution.py:325
  42.8 52.0 %collective-permute-start.11 = (bf16[272,1024]{1,0:T(8,128)(2,1)}, bf16[272,1024]{1,0:T(8,128)(2,1)S(1)}, u32[]{:S(2)}, u32[]{:S(2)}) collective-permute-start(bf16[272,1024]{1,0:T(8,128)(2,1)} %get-tuple-element.9.refs_0_), channel_id=1, source_target_pairs={{0,64},{32,96},{2,66},{34,98},{4,68},{36,100},{6,70},{38,102},{8,7... | collective-permute-start | bytes 1671176 | tf_op jit(solution)/shard_map/ppermute | solution.py:325
  54.2 12.4 %copy-start.5 = (bf16[272,1024]{1,0:T(8,128)(2,1)}, bf16[272,1024]{1,0:T(8,128)(2,1)S(1)}, u32[]{:S(2)}) copy-start(bf16[272,1024]{1,0:T(8,128)(2,1)S(1)} %collective-permute-done.7.refs_0_) | copy-start | bytes 1671172
  66.6 0.8 copy-start.6
  91.2 34.0 %collective-permute-start.10 = (bf16[144,2048]{1,0:T(8,128)(2,1)}, bf16[144,2048]{1,0:T(8,128)(2,1)S(1)}, u32[]{:S(2)}, u32[]{:S(2)}) collective-permute-start(bf16[144,2048]{1,0:T(8,128)(2,1)} %get-tuple-element.12), channel_id=1, source_target_pairs={{0,65},{32,97},{2,67},{34,99},{4,69},{36,101},{6,71},{38,103},{8,7... | collective-permute-start | bytes 1769480 | tf_op jit(solution)/shard_map/ppermute | solution.py:325
  94.7 30.5 %collective-permute-start.9 = (bf16[144,2048]{1,0:T(8,128)(2,1)}, bf16[144,2048]{1,0:T(8,128)(2,1)S(1)}, u32[]{:S(2)}, u32[]{:S(2)}) collective-permute-start(bf16[144,2048]{1,0:T(8,128)(2,1)} %get-tuple-element.11), channel_id=1, source_target_pairs={{0,1},{32,33},{2,3},{34,35},{4,5},{36,37},{6,7},{38,39},{8,9},{40,... | collective-permute-start | bytes 1769480 | tf_op jit(solution)/shard_map/ppermute | solution.py:325
  94.7 0.8 copy-start.4
  109.4 15.9 %collective-permute-start.12 = (bf16[144,2048]{1,0:T(8,128)(2,1)}, bf16[144,2048]{1,0:T(8,128)(2,1)S(1)}, u32[]{:S(2)}, u32[]{:S(2)}) collective-permute-start(bf16[144,2048]{1,0:T(8,128)(2,1)} %attend.5), channel_id=1, source_target_pairs={{0,64},{32,96},{2,66},{34,98},{4,68},{36,100},{6,70},{38,102},{8,7... | collective-permute-start | bytes 1769480 | tf_op jit(solution)/shard_map/ppermute | solution.py:325
  125.2 0.8 copy-start
  125.2 1.0 copy-start.1
  126.3 0.8 copy-start.2

commit v2 on v1

--- a/solution.py
+++ b/solution.py
@@ -103,27 +103,37 @@
     )(queries, shard)
 
 
-def attend_kernel(count, shards, own, *refs):
+def attend_kernel(count, sizes, old, have, base, final, *refs):
     q_refs = refs[:count]
-    kv_ref = refs[count]
-    at = count + 1
-    acc0_ref = None
-    if own:
-        acc0_ref = refs[at]
-        at += 1
+    at = count
+    piece_refs = refs[at : at + len(sizes)]
+    at += len(sizes)
+    in_refs = refs[at : at + count] if have else None
+    at += count if have else 0
+    base_ref = refs[at] if base else None
+    at += 1 if base else 0
     out_refs = refs[at : at + count]
-    q_buf, m_buf, acc_ref, ints, blocks, tasks, sem = refs[at + count :]
-    total = 2 * shards
-
-    for i in range(shards):
-        row = kv_ref[i * SHARD + 4 * RUN : i * SHARD + SHARD, :].astype(jnp.float32)[0:1]
-        ints[i : i + 1, :] = row.astype(jnp.int32)
+    kv_ref, q_buf, m_buf, acc_ref, ints, blocks, tasks, sems, sem = refs[at + count :]
+    starts = [sum(sizes[:i]) for i in range(len(sizes) + 1)]
+    shards = starts[-1]
+
+    def piece_copy(i):
+        there = kv_ref.at[pl.ds(starts[i] * SHARD, sizes[i] * SHARD), :]
+        return pltpu.make_async_copy(piece_refs[i], there, sems.at[i])
+
+    def read_blocks(first, last):
+        for i in range(first, last):
+            row = kv_ref[i * SHARD + 4 * RUN : i * SHARD + SHARD, :].astype(jnp.float32)[0:1]
+            ints[i : i + 1, :] = row.astype(jnp.int32)
+        copy = pltpu.make_async_copy(ints, blocks, sem)
+        copy.start()
+        copy.wait()
+
+    for i in range(old, len(sizes)):
+        piece_copy(i).start()
     for j in range(count):
         row = q_refs[j][2 * RUN : QROWS, 0:HD].astype(jnp.float32)[6:7]
         ints[shards + j : shards + j + 1, :] = row.astype(jnp.int32)
-    copy = pltpu.make_async_copy(ints, blocks, sem)
-    copy.start()
-    copy.wait()
 
     def key_block(task):
         shard = task // 2
@@ -135,24 +145,8 @@
         start = pl.multiple_of(shard * SHARD + (2 + task - 2 * shard) * RUN, 16)
         return kv_ref[pl.ds(start, RUN), :]
 
-    ones = jnp.ones((16, GROUP * RUN), jnp.bfloat16)
-
-    for j in range(count):
-        q_ref = q_refs[j]
-        here = blocks[shards + j, 0]
-        tail = q_ref[2 * RUN : QROWS, :].astype(jnp.float32)
-        for half in range(2):
-            q_buf[half] = query_tile(q_ref, half)
-            m_buf[half] = jnp.broadcast_to(
-                tail[3 * half : 3 * half + 1]
-                + tail[3 * half + 1 : 3 * half + 2]
-                + tail[3 * half + 2 : 3 * half + 3],
-                (8, ROWS),
-            )
-            if own:
-                acc_ref[half] = acc0_ref[:, half * ROWS : (half + 1) * ROWS]
-            else:
-                acc_ref[half] = jnp.zeros((ACC, ROWS), jnp.float32)
+    def list_tasks(here, first, last):
+        total = 2 * (last - first)
 
         def place(i, ends):
             low, high = ends
@@ -168,9 +162,36 @@
             return low, high
 
         for i in range(total):
-            tasks[i] = 0
-        low_end, high_end = lax.fori_loop(0, shards, place, (jnp.int32(0), jnp.int32(total - 1)))
-        high_start = high_end + 1
+            tasks[i] = 2 * first
+        low_end, high_end = lax.fori_loop(first, last, place, (jnp.int32(0), jnp.int32(total - 1)))
+        return low_end, high_end + 1
+
+    ones = jnp.ones((16, GROUP * RUN), jnp.bfloat16)
+
+    for j in range(count):
+        q_ref = q_refs[j]
+        tail = q_ref[2 * RUN : QROWS, :].astype(jnp.float32)
+        for half in range(2):
+            span = slice(half * ROWS, (half + 1) * ROWS)
+            q_buf[half] = query_tile(q_ref, half)
+            m_buf[half] = jnp.broadcast_to(
+                tail[3 * half : 3 * half + 1]
+                + tail[3 * half + 1 : 3 * half + 2]
+                + tail[3 * half + 2 : 3 * half + 3],
+                (8, ROWS),
+            )
+            if have:
+                acc_ref[half] = in_refs[j][:, span]
+            elif base:
+                acc_ref[half] = base_ref[:, span]
+            else:
+                acc_ref[half] = jnp.zeros((ACC, ROWS), jnp.float32)
+        if j == 0:
+            for i in range(old, len(sizes)):
+                piece_copy(i).wait()
+            read_blocks(starts[old], shards)
+        here = blocks[shards + j, 0]
+        low_end, high_start = list_tasks(here, starts[old], shards)
 
         def pure(first, half):
             query = q_buf[half]
@@ -198,7 +219,7 @@
             acc_ref[0] += dot(jnp.where(index < low_end, vt, zero), weights, 1, 0)
             acc_ref[1] += dot(jnp.where(index >= high_start, vt, zero), weights, 1, 0)
 
-        @pl.loop(0, total // GROUP)
+        @pl.loop(0, 2 * (shards - starts[old]) // GROUP)
         def _(g):
             first = g * GROUP
             is_low = first + GROUP <= low_end
@@ -212,33 +233,44 @@
             def _():
                 mixed(first)
 
+        if not final:
+            for half in range(2):
+                out_refs[j][:, half * ROWS : (half + 1) * ROWS] = acc_ref[half]
+            continue
+
         sums = jnp.maximum(acc_ref[0][HD : HD + 8], acc_ref[1][HD : HD + 8])
         fine = jnp.min(jnp.where(sums < LIMIT, 1.0, 0.0)) > 0.5
 
         @pl.when(jnp.logical_not(fine))
         def _():
+            for i in range(old):
+                piece_copy(i).start()
+            for i in range(old):
+                piece_copy(i).wait()
+            read_blocks(0, starts[old])
+            low_all, high_all = list_tasks(here, 0, shards)
             for half in range(2):
-                if own:
-                    acc_ref[half] = acc0_ref[:, half * ROWS : (half + 1) * ROWS]
+                if base:
+                    acc_ref[half] = base_ref[:, half * ROWS : (half + 1) * ROWS]
                 else:
                     acc_ref[half] = jnp.zeros((ACC, ROWS), jnp.float32)
 
-            @pl.loop(0, total)
+            @pl.loop(0, 2 * shards)
             def _(t):
-                @pl.when(jnp.logical_or(t < low_end, t >= high_start))
+                @pl.when(jnp.logical_or(t < low_all, t >= high_all))
                 def _():
-                    half = (t >= high_start).astype(jnp.int32)
+                    half = (t >= high_all).astype(jnp.int32)
                     scores = dot(key_block(tasks[t]), q_buf[half], 1, 1) * COEF
-                    old = m_buf[half][0:1]
-                    new = jnp.maximum(old, jnp.max(scores, axis=0, keepdims=True))
+                    before = m_buf[half][0:1]
+                    new = jnp.maximum(before, jnp.max(scores, axis=0, keepdims=True))
                     weights = jnp.exp2(scores - new).astype(jnp.bfloat16)
                     vt = jnp.concatenate([value_block(tasks[t]), ones[:, :RUN]], axis=0)
-                    acc_ref[half] = acc_ref[half] * jnp.exp2(old - new) + dot(vt, weights, 1, 0)
+                    acc_ref[half] = acc_ref[half] * jnp.exp2(before - new) + dot(vt, weights, 1, 0)
                     m_buf[half] = jnp.broadcast_to(new, (8, ROWS))
 
         for half in range(2):
             span = slice(half * ROWS, (half + 1) * ROWS)
-            if own:
+            if base:
                 out_refs[j][0 : HD + 8, span] = acc_ref[half][0 : HD + 8]
                 out_refs[j][HD + 8 : ACC, span] = m_buf[half]
             else:
@@ -249,29 +281,36 @@
                 )
 
 
-def attend(q_list, kv, acc0=None):
-    count, shards = len(q_list), kv.shape[0] // SHARD
-    own = acc0 is not None
+def attend(q_list, new, old=(), acc=None, base=None, final=True):
+    count = len(q_list)
+    pieces = (tuple(old) if final else ()) + tuple(new)
+    skip = len(old) if final else 0
+    sizes = tuple(p.shape[0] // SHARD for p in pieces)
+    shards = sum(sizes)
     int_rows = -(-(shards + count) // 8) * 8
-    args = tuple(q_list) + (kv,) + ((acc0,) if own else ())
-    out = jax.ShapeDtypeStruct((ACC, 2 * ROWS), jnp.float32 if own else jnp.bfloat16)
-    pairs = count * 2 * shards * RUN * ROWS
+    vmem = pl.BlockSpec(memory_space=pltpu.VMEM)
+    args = tuple(q_list) + pieces + (tuple(acc) if acc is not None else ()) + ((base,) if base is not None else ())
+    extra = len(args) - count - len(pieces)
+    out = jax.ShapeDtypeStruct((ACC, 2 * ROWS), jnp.bfloat16 if final and base is None else jnp.float32)
+    pairs = count * 2 * sum(sizes[skip:]) * RUN * ROWS
     return pl.pallas_call(
-        functools.partial(attend_kernel, count, shards, own),
+        functools.partial(attend_kernel, count, sizes, skip, acc is not None, base is not None, final),
         out_shape=(out,) * count,
-        in_specs=[pl.BlockSpec(memory_space=pltpu.VMEM)] * len(args),
-        out_specs=(pl.BlockSpec(memory_space=pltpu.VMEM),) * count,
+        in_specs=[vmem] * count + [pl.BlockSpec(memory_space=pl.ANY)] * len(pieces) + [vmem] * extra,
+        out_specs=(vmem,) * count,
         scratch_shapes=[
+            pltpu.VMEM((shards * SHARD, HD), jnp.bfloat16),
             pltpu.VMEM((2, ROWS, HD), jnp.bfloat16),
             pltpu.VMEM((2, 8, ROWS), jnp.float32),
             pltpu.VMEM((2, ACC, ROWS), jnp.float32),
             pltpu.VMEM((int_rows, HD), jnp.int32),
             pltpu.SMEM((int_rows, HD), jnp.int32),
             pltpu.SMEM((2 * shards + 8,), jnp.int32),
+            pltpu.SemaphoreType.DMA((len(pieces),)),
             pltpu.SemaphoreType.DMA,
         ],
         compiler_params=pltpu.CompilerParams(vmem_limit_bytes=VMEM_BYTES),
-        cost_estimate=pl.CostEstimate(flops=pairs * HD * 8, bytes_accessed=8 << 20, transcendentals=pairs),
+        cost_estimate=pl.CostEstimate(flops=pairs * HD * 4, bytes_accessed=8 << 20, transcendentals=pairs),
         name="attend",
     )(*args)
 
@@ -341,23 +380,28 @@
     return swap(array, lambda core: (0, 0, 0, 1))
 
 
-STEPS = (1, 3, 2)
-
-
 def body(queries, keys, values, positions):
     shard = pack_kv(positions, keys, values)
-    near = [ring_first(shard, s) for s in STEPS]
+    near = [ring_first(shard, s) for s in (1, 3, 2)]
     packed, acc0 = pack_q(queries, shard)
-    others = [ring_x(packed, s) for s in STEPS]
+    near, packed, acc0 = lax.optimization_barrier((near, packed, acc0))
     line = jnp.concatenate([shard] + near, axis=0)
-    far = [ring_second(line, s) for s in STEPS]
-    plane = jnp.concatenate([line] + far, axis=0)
-    kv = jnp.concatenate([plane, cores(plane)], axis=0)
-    part1, part3 = attend(others[:2], kv)
-    back1, back3 = ring_x(part1, 1), ring_x(part3, 3)
-    (part2,) = attend(others[2:], kv)
+    q1, q3 = ring_x(packed, 1), ring_x(packed, 3)
+    far1, far3 = ring_second(line, 1), ring_second(line, 3)
+    far2 = ring_second(line, 2)
+    line_x = cores(line)
+    far1, far3, q1, q3, line_x = lax.optimization_barrier((far1, far3, q1, q3, line_x))
+    first = [line, line_x, far1, far3, cores(far1), cores(far3)]
+    (acc1,) = attend([q1], first, final=False)
+    q2 = ring_x(packed, 2)
+    last = [far2, cores(far2)]
+    (part1,) = attend([q1], last, first, acc=[acc1])
+    back1 = ring_x(part1, 1)
+    (part3,) = attend([q3], first + last)
+    back3 = ring_x(part3, 3)
+    (part2,) = attend([q2], first + last)
     back2 = ring_x(part2, 2)
-    (mine,) = attend([packed], kv, acc0)
+    (mine,) = attend([packed], first + last, base=acc0)
     return combine(mine, (back1, back3, back2))
 
 

time: 131 us -> 114 us (0.87)
  waiting for transfers between devices: 38.5 us -> 5.63 us
  Pallas kernels: 59.8 us -> 70.9 us
  starting transfers between devices: 22.5 us -> 32 us
  local copies, waits for them, and re-layouts: 8.4 us -> 4.29 us
    ppermute x13 -> x16, waiting for transfers between devices: 38.5 us -> 5.63 us  [swap(): return lax.ppermute(array, AXES, pairs)]
    pallas_call x3 -> x5, Pallas kernels: 51.9 us -> 63.1 us  [attend(): pl.pallas_call(functools.partial(attend_kernel, count, sizes, skip, acc i...]
    ppermute x13 -> x16, starting transfers between devices: 22.5 us -> 32 us  [swap(): return lax.ppermute(array, AXES, pairs)]
    unnamed x20 -> x30, local copies, waits for them, and re-layouts: 6.84 us -> 4.29 us
    concatenate x2 -> x0, local copies, waits for them, and re-layouts: 1.56 us -> none  [the longest x1 1.41 us: body(): kv = jnp.concatenate([plane, cores(plane)], axis=0)]
  transfers between devices with their start and end apart: 13 -> 16, of which waited for: 7 -> 5; matrix products, arithmetic and copies ran while one was open for 2% -> 0% of each run, Pallas kernels for 42% -> 58%
where the time goes in v2:
time: 114 us
  Pallas kernels  70.9 us (62%)
  starting transfers between devices  32 us (28%)
  waiting for transfers between devices  5.63 us (5%)
  local copies, waits for them, and re-layouts  4.29 us (4%)
    pallas_call x5, Pallas kernels, attend(): pl.pallas_call(functools.partial(attend_kernel, count, sizes, skip, acc i...  63.1 us
    ppermute x16, starting transfers between devices, swap(): return lax.ppermute(array, AXES, pairs)  32 us
    ppermute x16, waiting for transfers between devices, swap(): return lax.ppermute(array, AXES, pairs)  5.63 us
    unnamed x30, local copies, waits for them, and re-layouts  4.29 us
    pallas_call x1, Pallas kernels, combine(): pl.pallas_call(combine_kernel, out_shape=jax.ShapeDtypeStruct((2 * RUN, R...  3.16 us
    pallas_call x1, Pallas kernels, pack_q(): pl.pallas_call(pack_q_kernel, out_shape=(jax.ShapeDtypeStruct((QROWS, ROW...  3.03 us
  transfers between devices with their start and end apart: 16, of which 5 were waited for; matrix products, arithmetic and copies ran while one was open for 0% of the time, Pallas kernels for 58%

profile of v2, /device:TPU:1, one launch (start us, length us, event | category | flops | bytes accessed | tf_op | source)
XLA Modules:
  0.0 114.0 jit_solution(12421027447230354536)
XLA Ops:
  0.0 1.6 %pack_kv.1.shard_ref = bf16[528,128]{1,0:T(8,128)(2,1)} custom-call(s32[256]{0:T(256)} %pos_ref.1, bf16[256,128]{1,0:T(8,128)(2,1)} %key_ref.1, bf16[256,128]{1,0:T(8,128)(2,1)} %value_ref.1), custom_call_target="tpu_custom_call" | custom-call | tf_op jit(solution)/shard_map/pack_kv/pallas_call | solution.py:56
  1.6 2.1 %collective-permute-start = (bf16[528,128]{1,0:T(8,128)(2,1)}, bf16[528,128]{1,0:T(8,128)(2,1)S(1)}, u32[]{:S(2)}, u32[]{:S(2)}) collective-permute-start(bf16[528,128]{1,0:T(8,128)(2,1)} %pack_kv.1.shard_ref), channel_id=1, source_target_pairs={{0,2},{32,40},{2,0},{34,42},{4,6},{36,44},{6,4},{38,46},{8,10},{40... | collective-permute-start | bytes 405512 | tf_op jit(solution)/shard_map/ppermute | solution.py:364
  3.8 1.9 %collective-permute-start.1 = (bf16[528,128]{1,0:T(8,128)(2,1)}, bf16[528,128]{1,0:T(8,128)(2,1)S(1)}, u32[]{:S(2)}, u32[]{:S(2)}) collective-permute-start(bf16[528,128]{1,0:T(8,128)(2,1)} %pack_kv.1.shard_ref), channel_id=1, source_target_pairs={{0,6},{32,56},{2,4},{34,58},{4,2},{36,60},{6,0},{38,62},{8,14},{40... | collective-permute-start | bytes 405512 | tf_op jit(solution)/shard_map/ppermute | solution.py:364
  6.4 3.0 %pack_q.1 = (bf16[272,1024]{1,0:T(8,128)(2,1)}, f32[144,2048]{1,0:T(8,128)}) custom-call(bf16[256,1024]{1,0:T(8,128)(2,1)} %query_ref.1, bf16[528,128]{1,0:T(8,128)(2,1)} %pack_kv.1.shard_ref), custom_call_target="tpu_custom_call" | custom-call | tf_op jit(solution)/shard_map/pack_q/pallas_call | solution.py:93
  9.4 1.8 %collective-permute-done.2 = bf16[528,128]{1,0:T(8,128)(2,1)S(1)} collective-permute-done((bf16[528,128]{1,0:T(8,128)(2,1)}, bf16[528,128]{1,0:T(8,128)(2,1)S(1)}, u32[]{:S(2)}, u32[]{:S(2)}) %collective-permute-start.2) | collective-permute-done | bytes 135200 | tf_op jit(solution)/shard_map/ppermute | solution.py:364
  11.2 0.9 pad_maximum_fusion.refs_1_
  12.2 1.7 %collective-permute-start.3 = (bf16[2112,128]{1,0:T(8,128)(2,1)S(1)}, bf16[2112,128]{1,0:T(8,128)(2,1)S(1)}, u32[]{:S(2)}, u32[]{:S(2)}) collective-permute-start(bf16[2112,128]{1,0:T(8,128)(2,1)S(1)} %pad_maximum_fusion.refs_1_), channel_id=1, source_target_pairs={{0,8},{32,34},{2,10},{34,32},{4,12},{36,38},{6,14},{38,36},{8,0},{... | collective-permute-start | bytes 1622024 | tf_op jit(solution)/shard_map/ppermute | solution.py:364
  13.9 1.2 %collective-permute-start.5 = (bf16[272,1024]{1,0:T(8,128)(2,1)S(1)}, bf16[272,1024]{1,0:T(8,128)(2,1)S(1)}, u32[]{:S(2)}, u32[]{:S(2)}) collective-permute-start(bf16[272,1024]{1,0:T(8,128)(2,1)S(1)} %copy-done.12), channel_id=1, source_target_pairs={{0,1},{32,33},{2,3},{34,35},{4,5},{36,37},{6,7},{38,39},{8,9},{40,... | collective-permute-start | bytes 1671176 | tf_op jit(solution)/shard_map/ppermute | solution.py:364
  15.1 1.8 %collective-permute-start.6 = (bf16[272,1024]{1,0:T(8,128)(2,1)S(1)}, bf16[272,1024]{1,0:T(8,128)(2,1)S(1)}, u32[]{:S(2)}, u32[]{:S(2)}) collective-permute-start(bf16[272,1024]{1,0:T(8,128)(2,1)S(1)} %copy-done.12), channel_id=1, source_target_pairs={{0,65},{32,97},{2,67},{34,99},{4,69},{36,101},{6,71},{38,103},{8,7... | collective-permute-start | bytes 1671176 | tf_op jit(solution)/shard_map/ppermute | solution.py:364
  16.9 2.2 %collective-permute-start.4 = (bf16[2112,128]{1,0:T(8,128)(2,1)S(1)}, bf16[2112,128]{1,0:T(8,128)(2,1)S(1)}, u32[]{:S(2)}, u32[]{:S(2)}) collective-permute-start(bf16[2112,128]{1,0:T(8,128)(2,1)S(1)} %pad_maximum_fusion.refs_1_), channel_id=1, source_target_pairs={{0,24},{32,38},{2,26},{34,36},{4,28},{36,34},{6,30},{38,32},{8,16}... | collective-permute-start | bytes 1622024 | tf_op jit(solution)/shard_map/ppermute | solution.py:364
  19.2 3.5 %collective-permute-start.7 = (bf16[2112,128]{1,0:T(8,128)(2,1)S(1)}, bf16[2112,128]{1,0:T(8,128)(2,1)S(1)}, u32[]{:S(2)}, u32[]{:S(2)}) collective-permute-start(bf16[2112,128]{1,0:T(8,128)(2,1)S(1)} %pad_maximum_fusion.refs_1_), channel_id=1, source_target_pairs={{0,32},{32,0},{2,34},{34,2},{4,36},{36,4},{6,38},{38,6},{8,40},{40... | collective-permute-start | bytes 1622024 | tf_op jit(solution)/shard_map/ppermute | solution.py:364
  22.7 1.7 %collective-permute-start.10 = (bf16[2112,128]{1,0:T(8,128)(2,1)S(1)}, bf16[2112,128]{1,0:T(8,128)(2,1)S(1)}, u32[]{:S(2)}, u32[]{:S(2)}) collective-permute-start(bf16[2112,128]{1,0:T(8,128)(2,1)S(1)} %pad_maximum_fusion.refs_1_), channel_id=1, source_target_pairs={{0,16},{32,36},{2,18},{34,38},{4,20},{36,32},{6,22},{38,34},{8,24}... | collective-permute-start | bytes 1622024 | tf_op jit(solution)/shard_map/ppermute | solution.py:364
  24.4 2.3 %collective-permute-done.4.refs_4_ = bf16[2112,128]{1,0:T(8,128)(2,1)S(1)} collective-permute-done((bf16[2112,128]{1,0:T(8,128)(2,1)S(1)}, bf16[2112,128]{1,0:T(8,128)(2,1)S(1)}, u32[]{:S(2)}, u32[]{:S(2)}) %collective-permute-start.4) | collective-permute-done | bytes 540704 | tf_op jit(solution)/shard_map/ppermute | solution.py:364
  27.2 9.8 %collective-permute-start.8 = (bf16[2112,128]{1,0:T(8,128)(2,1)S(1)}, bf16[2112,128]{1,0:T(8,128)(2,1)S(1)}, u32[]{:S(2)}, u32[]{:S(2)}) collective-permute-start(bf16[2112,128]{1,0:T(8,128)(2,1)S(1)} %collective-permute-done.3.refs_3_), channel_id=1, source_target_pairs={{0,32},{32,0},{2,34},{34,2},{4,36},{36,4},{6,38},{38,6},{8,40},{40... | collective-permute-start | bytes 1622024 | tf_op jit(solution)/shard_map/ppermute | solution.py:364
  39.4 0.8 copy-done.10
  40.2 12.0 %attend.6.refs_9_ = f32[144,2048]{1,0:T(8,128)} custom-call(bf16[272,1024]{1,0:T(8,128)(2,1)} %copy-done.4, bf16[2112,128]{1,0:T(8,128)(2,1)} %copy-done, bf16[2112,128]{1,0:T(8,128)(2,1)} %copy-done.7, bf16[2112,128]{1,0:T(8,128)(2,1)} %copy-done.5, bf16[2112,128]{1,0:T(8,128)(2,1)} %copy-done.6, bf16[2112,128]{1,0:T(8,128)(2,1)} %copy-done.9, ...), custom_call_target="tpu_custom_call" | custom-call | flops 3221225472 | bytes 8388608 | tf_op jit(solution)/shard_map/attend/pallas_call | solution.py:296
  52.2 0.8 copy-done.11
  53.0 7.2 %attend.7 = bf16[144,2048]{1,0:T(8,128)(2,1)} custom-call(bf16[272,1024]{1,0:T(8,128)(2,1)} %copy-done.4, bf16[2112,128]{1,0:T(8,128)(2,1)} %copy-done, bf16[2112,128]{1,0:T(8,128)(2,1)} %copy-done.7, bf16[2112,128]{1,0:T(8,128)(2,1)} %copy-done.5, bf16[2112,128]{1,0:T(8,128)(2,1)} %copy-done.6, bf16[2112,128]{1,0:T(8,128)(2,1)} %copy-done.9, ...), custom_call_target="tpu_custom_call" | custom-call | flops 1073741824 | bytes 8388608 | tf_op jit(solution)/shard_map/attend/pallas_call | solution.py:296
  60.5 14.3 %attend.8 = bf16[144,2048]{1,0:T(8,128)(2,1)} custom-call(bf16[272,1024]{1,0:T(8,128)(2,1)} %copy-done.13, bf16[2112,128]{1,0:T(8,128)(2,1)} %copy-done, bf16[2112,128]{1,0:T(8,128)(2,1)} %copy-done.7, bf16[2112,128]{1,0:T(8,128)(2,1)} %copy-done.5, bf16[2112,128]{1,0:T(8,128)(2,1)} %copy-done.6, bf16[2112,128]{1,0:T(8,128)(2,1)} %copy-done.9, ...), custom_call_target="tpu_custom_call" | custom-call | flops 4294967296 | bytes 8388608 | tf_op jit(solution)/shard_map/attend/pallas_call | solution.py:296
  74.8 2.2 %collective-permute-start.13 = (bf16[144,2048]{1,0:T(8,128)(2,1)}, bf16[144,2048]{1,0:T(8,128)(2,1)S(1)}, u32[]{:S(2)}, u32[]{:S(2)}) collective-permute-start(bf16[144,2048]{1,0:T(8,128)(2,1)} %attend.8), channel_id=1, source_target_pairs={{0,65},{32,97},{2,67},{34,99},{4,69},{36,101},{6,71},{38,103},{8,7... | collective-permute-start | bytes 1769480 | tf_op jit(solution)/shard_map/ppermute | solution.py:364
  77.9 14.6 %attend.9 = bf16[144,2048]{1,0:T(8,128)(2,1)} custom-call(bf16[272,1024]{1,0:T(8,128)(2,1)} %copy-done.14, bf16[2112,128]{1,0:T(8,128)(2,1)} %copy-done, bf16[2112,128]{1,0:T(8,128)(2,1)} %copy-done.7, bf16[2112,128]{1,0:T(8,128)(2,1)} %copy-done.5, bf16[2112,128]{1,0:T(8,128)(2,1)} %copy-done.6, bf16[2112,128]{1,0:T(8,128)(2,1)} %copy-done.9, ...), custom_call_target="tpu_custom_call" | custom-call | flops 4294967296 | bytes 8388608 | tf_op jit(solution)/shard_map/attend/pallas_call | solution.py:296
  92.4 1.4 %collective-permute-start.15 = (bf16[144,2048]{1,0:T(8,128)(2,1)}, bf16[144,2048]{1,0:T(8,128)(2,1)S(1)}, u32[]{:S(2)}, u32[]{:S(2)}) collective-permute-start(bf16[144,2048]{1,0:T(8,128)(2,1)} %attend.9), channel_id=1, source_target_pairs={{0,64},{32,96},{2,66},{34,98},{4,68},{36,100},{6,70},{38,102},{8,7... | collective-permute-start | bytes 1769480 | tf_op jit(solution)/shard_map/ppermute | solution.py:364
  93.9 15.1 %attend.5.own_ref = f32[144,2048]{1,0:T(8,128)} custom-call(bf16[272,1024]{1,0:T(8,128)(2,1)} %get-tuple-element.19.refs_0_, bf16[2112,128]{1,0:T(8,128)(2,1)} %copy-done, bf16[2112,128]{1,0:T(8,128)(2,1)} %copy-done.7, bf16[2112,128]{1,0:T(8,128)(2,1)} %copy-done.5, bf16[2112,128]{1,0:T(8,128)(2,1)} %copy-done.6, bf16[2112,128]{1,0:T(8,128)(2,1)} %copy-done.9, ...), custom_call_target="tpu_custom_call" | custom-call | flops 4294967296 | bytes 8388608 | tf_op jit(solution)/shard_map/attend/pallas_call | solution.py:296
  110.9 3.2 %combine.1 = bf16[256,1024]{1,0:T(8,128)(2,1)} custom-call(f32[144,2048]{1,0:T(8,128)} %attend.5.own_ref, bf16[144,2048]{1,0:T(8,128)(2,1)} %copy-done.1, bf16[144,2048]{1,0:T(8,128)(2,1)} %copy-done.2, bf16[144,2048]{1,0:T(8,128)(2,1)} %copy-done.3), custom_call_target="tpu_custom_call" | custom-call | tf_op jit(solution)/shard_map/combine/pallas_call | solution.py:342
  (47 shorter events, 6.5 us)
Async XLA Ops:
  1.6 7.8 %collective-permute-start = (bf16[528,128]{1,0:T(8,128)(2,1)}, bf16[528,128]{1,0:T(8,128)(2,1)S(1)}, u32[]{:S(2)}, u32[]{:S(2)}) collective-permute-start(bf16[528,128]{1,0:T(8,128)(2,1)} %pack_kv.1.shard_ref), channel_id=1, source_target_pairs={{0,2},{32,40},{2,0},{34,42},{4,6},{36,44},{6,4},{38,46},{8,10},{40... | collective-permute-start | bytes 405512 | tf_op jit(solution)/shard_map/ppermute | solution.py:364
  3.8 5.7 %collective-permute-start.1 = (bf16[528,128]{1,0:T(8,128)(2,1)}, bf16[528,128]{1,0:T(8,128)(2,1)S(1)}, u32[]{:S(2)}, u32[]{:S(2)}) collective-permute-start(bf16[528,128]{1,0:T(8,128)(2,1)} %pack_kv.1.shard_ref), channel_id=1, source_target_pairs={{0,6},{32,56},{2,4},{34,58},{4,2},{36,60},{6,0},{38,62},{8,14},{40... | collective-permute-start | bytes 405512 | tf_op jit(solution)/shard_map/ppermute | solution.py:364
  5.7 5.6 %collective-permute-start.2 = (bf16[528,128]{1,0:T(8,128)(2,1)}, bf16[528,128]{1,0:T(8,128)(2,1)S(1)}, u32[]{:S(2)}, u32[]{:S(2)}) collective-permute-start(bf16[528,128]{1,0:T(8,128)(2,1)} %pack_kv.1.shard_ref), channel_id=1, source_target_pairs={{0,4},{32,48},{2,6},{34,50},{4,0},{36,52},{6,2},{38,54},{8,12},{40... | collective-permute-start | bytes 405512 | tf_op jit(solution)/shard_map/ppermute | solution.py:364
  9.4 4.5 %copy-start.12 = (bf16[272,1024]{1,0:T(8,128)(2,1)S(1)}, bf16[272,1024]{1,0:T(8,128)(2,1)}, u32[]{:S(2)}) copy-start(bf16[272,1024]{1,0:T(8,128)(2,1)} %get-tuple-element.19.refs_0_) | copy-start | bytes 1671172
  12.2 27.1 %copy-start = (bf16[2112,128]{1,0:T(8,128)(2,1)}, bf16[2112,128]{1,0:T(8,128)(2,1)S(1)}, u32[]{:S(2)}) copy-start(bf16[2112,128]{1,0:T(8,128)(2,1)S(1)} %pad_maximum_fusion.refs_1_) | copy-start | bytes 1622020
  12.2 10.5 %collective-permute-start.3 = (bf16[2112,128]{1,0:T(8,128)(2,1)S(1)}, bf16[2112,128]{1,0:T(8,128)(2,1)S(1)}, u32[]{:S(2)}, u32[]{:S(2)}) collective-permute-start(bf16[2112,128]{1,0:T(8,128)(2,1)S(1)} %pad_maximum_fusion.refs_1_), channel_id=1, source_target_pairs={{0,8},{32,34},{2,10},{34,32},{4,12},{36,38},{6,14},{38,36},{8,0},{... | collective-permute-start | bytes 1622024 | tf_op jit(solution)/shard_map/ppermute | solution.py:364
  13.9 12.8 %collective-permute-start.5 = (bf16[272,1024]{1,0:T(8,128)(2,1)S(1)}, bf16[272,1024]{1,0:T(8,128)(2,1)S(1)}, u32[]{:S(2)}, u32[]{:S(2)}) collective-permute-start(bf16[272,1024]{1,0:T(8,128)(2,1)S(1)} %copy-done.12), channel_id=1, source_target_pairs={{0,1},{32,33},{2,3},{34,35},{4,5},{36,37},{6,7},{38,39},{8,9},{40,... | collective-permute-start | bytes 1671176 | tf_op jit(solution)/shard_map/ppermute | solution.py:364
  15.1 12.0 %collective-permute-start.6 = (bf16[272,1024]{1,0:T(8,128)(2,1)S(1)}, bf16[272,1024]{1,0:T(8,128)(2,1)S(1)}, u32[]{:S(2)}, u32[]{:S(2)}) collective-permute-start(bf16[272,1024]{1,0:T(8,128)(2,1)S(1)} %copy-done.12), channel_id=1, source_target_pairs={{0,65},{32,97},{2,67},{34,99},{4,69},{36,101},{6,71},{38,103},{8,7... | collective-permute-start | bytes 1671176 | tf_op jit(solution)/shard_map/ppermute | solution.py:364
  16.9 9.7 %collective-permute-start.4 = (bf16[2112,128]{1,0:T(8,128)(2,1)S(1)}, bf16[2112,128]{1,0:T(8,128)(2,1)S(1)}, u32[]{:S(2)}, u32[]{:S(2)}) collective-permute-start(bf16[2112,128]{1,0:T(8,128)(2,1)S(1)} %pad_maximum_fusion.refs_1_), channel_id=1, source_target_pairs={{0,24},{32,38},{2,26},{34,36},{4,28},{36,34},{6,30},{38,32},{8,16}... | collective-permute-start | bytes 1622024 | tf_op jit(solution)/shard_map/ppermute | solution.py:364
  19.2 7.5 %collective-permute-start.7 = (bf16[2112,128]{1,0:T(8,128)(2,1)S(1)}, bf16[2112,128]{1,0:T(8,128)(2,1)S(1)}, u32[]{:S(2)}, u32[]{:S(2)}) collective-permute-start(bf16[2112,128]{1,0:T(8,128)(2,1)S(1)} %pad_maximum_fusion.refs_1_), channel_id=1, source_target_pairs={{0,32},{32,0},{2,34},{34,2},{4,36},{36,4},{6,38},{38,6},{8,40},{40... | collective-permute-start | bytes 1622024 | tf_op jit(solution)/shard_map/ppermute | solution.py:364
  22.7 16.6 %copy-start.5 = (bf16[2112,128]{1,0:T(8,128)(2,1)}, bf16[2112,128]{1,0:T(8,128)(2,1)S(1)}, u32[]{:S(2)}) copy-start(bf16[2112,128]{1,0:T(8,128)(2,1)S(1)} %collective-permute-done.3.refs_3_) | copy-start | bytes 1622020
  22.7 14.4 %collective-permute-start.10 = (bf16[2112,128]{1,0:T(8,128)(2,1)S(1)}, bf16[2112,128]{1,0:T(8,128)(2,1)S(1)}, u32[]{:S(2)}, u32[]{:S(2)}) collective-permute-start(bf16[2112,128]{1,0:T(8,128)(2,1)S(1)} %pad_maximum_fusion.refs_1_), channel_id=1, source_target_pairs={{0,16},{32,36},{2,18},{34,38},{4,20},{36,32},{6,22},{38,34},{8,24}... | collective-permute-start | bytes 1622024 | tf_op jit(solution)/shard_map/ppermute | solution.py:364
  26.7 12.7 %copy-start.6 = (bf16[2112,128]{1,0:T(8,128)(2,1)}, bf16[2112,128]{1,0:T(8,128)(2,1)S(1)}, u32[]{:S(2)}) copy-start(bf16[2112,128]{1,0:T(8,128)(2,1)S(1)} %collective-permute-done.4.refs_4_) | copy-start | bytes 1622020
  26.7 12.7 %copy-start.7 = (bf16[2112,128]{1,0:T(8,128)(2,1)}, bf16[2112,128]{1,0:T(8,128)(2,1)S(1)}, u32[]{:S(2)}) copy-start(bf16[2112,128]{1,0:T(8,128)(2,1)S(1)} %collective-permute-done.7.refs_2_) | copy-start | bytes 1622020
  26.7 12.7 %copy-start.4 = (bf16[272,1024]{1,0:T(8,128)(2,1)}, bf16[272,1024]{1,0:T(8,128)(2,1)S(1)}, u32[]{:S(2)}) copy-start(bf16[272,1024]{1,0:T(8,128)(2,1)S(1)} %collective-permute-done.5.refs_0_) | copy-start | bytes 1671172
  27.2 25.0 %copy-start.13 = (bf16[272,1024]{1,0:T(8,128)(2,1)}, bf16[272,1024]{1,0:T(8,128)(2,1)S(1)}, u32[]{:S(2)}) copy-start(bf16[272,1024]{1,0:T(8,128)(2,1)S(1)} %collective-permute-done.6.refs_0_) | copy-start | bytes 1671172
  27.2 11.4 %collective-permute-start.8 = (bf16[2112,128]{1,0:T(8,128)(2,1)S(1)}, bf16[2112,128]{1,0:T(8,128)(2,1)S(1)}, u32[]{:S(2)}, u32[]{:S(2)}) collective-permute-start(bf16[2112,128]{1,0:T(8,128)(2,1)S(1)} %collective-permute-done.3.refs_3_), channel_id=1, source_target_pairs={{0,32},{32,0},{2,34},{34,2},{4,36},{36,4},{6,38},{38,6},{8,40},{40... | collective-permute-start | bytes 1622024 | tf_op jit(solution)/shard_map/ppermute | solution.py:364
  37.0 2.3 %collective-permute-start.9 = (bf16[2112,128]{1,0:T(8,128)(2,1)S(1)}, bf16[2112,128]{1,0:T(8,128)(2,1)S(1)}, u32[]{:S(2)}, u32[]{:S(2)}) collective-permute-start(bf16[2112,128]{1,0:T(8,128)(2,1)S(1)} %collective-permute-done.4.refs_4_), channel_id=1, source_target_pairs={{0,32},{32,0},{2,34},{34,2},{4,36},{36,4},{6,38},{38,6},{8,40},{40... | collective-permute-start | bytes 1622024 | tf_op jit(solution)/shard_map/ppermute | solution.py:364
  37.1 15.1 %copy-start.8 = (bf16[2112,128]{1,0:T(8,128)(2,1)}, bf16[2112,128]{1,0:T(8,128)(2,1)S(1)}, u32[]{:S(2)}) copy-start(bf16[2112,128]{1,0:T(8,128)(2,1)S(1)} %collective-permute-done.10.refs_7_) | copy-start | bytes 1622020
  37.1 15.1 %collective-permute-start.11 = (bf16[2112,128]{1,0:T(8,128)(2,1)S(1)}, bf16[2112,128]{1,0:T(8,128)(2,1)S(1)}, u32[]{:S(2)}, u32[]{:S(2)}) collective-permute-start(bf16[2112,128]{1,0:T(8,128)(2,1)S(1)} %collective-permute-done.10.refs_7_), channel_id=1, source_target_pairs={{0,32},{32,0},{2,34},{34,2},{4,36},{36,4},{6,38},{38,6},{8,40},{40... | collective-permute-start | bytes 1622024 | tf_op jit(solution)/shard_map/ppermute | solution.py:364
  37.5 39.6 %collective-permute-start.14 = (bf16[272,1024]{1,0:T(8,128)(2,1)S(1)}, bf16[272,1024]{1,0:T(8,128)(2,1)S(1)}, u32[]{:S(2)}, u32[]{:S(2)}) collective-permute-start(bf16[272,1024]{1,0:T(8,128)(2,1)S(1)} %copy-done.12), channel_id=1, source_target_pairs={{0,64},{32,96},{2,66},{34,98},{4,68},{36,100},{6,70},{38,102},{8,7... | collective-permute-start | bytes 1671176 | tf_op jit(solution)/shard_map/ppermute | solution.py:364
  60.2 48.8 %collective-permute-start.12 = (bf16[144,2048]{1,0:T(8,128)(2,1)}, bf16[144,2048]{1,0:T(8,128)(2,1)S(1)}, u32[]{:S(2)}, u32[]{:S(2)}) collective-permute-start(bf16[144,2048]{1,0:T(8,128)(2,1)} %attend.7), channel_id=1, source_target_pairs={{0,1},{32,33},{2,3},{34,35},{4,5},{36,37},{6,7},{38,39},{8,9},{40,... | collective-permute-start | bytes 1769480 | tf_op jit(solution)/shard_map/ppermute | solution.py:364
  74.8 34.2 %collective-permute-start.13 = (bf16[144,2048]{1,0:T(8,128)(2,1)}, bf16[144,2048]{1,0:T(8,128)(2,1)S(1)}, u32[]{:S(2)}, u32[]{:S(2)}) collective-permute-start(bf16[144,2048]{1,0:T(8,128)(2,1)} %attend.8), channel_id=1, source_target_pairs={{0,65},{32,97},{2,67},{34,99},{4,69},{36,101},{6,71},{38,103},{8,7... | collective-permute-start | bytes 1769480 | tf_op jit(solution)/shard_map/ppermute | solution.py:364
  92.4 16.6 %collective-permute-start.15 = (bf16[144,2048]{1,0:T(8,128)(2,1)}, bf16[144,2048]{1,0:T(8,128)(2,1)S(1)}, u32[]{:S(2)}, u32[]{:S(2)}) collective-permute-start(bf16[144,2048]{1,0:T(8,128)(2,1)} %attend.9), channel_id=1, source_target_pairs={{0,64},{32,96},{2,66},{34,98},{4,68},{36,100},{6,70},{38,102},{8,7... | collective-permute-start | bytes 1769480 | tf_op jit(solution)/shard_map/ppermute | solution.py:364
  (7 other events, 5.9 us)

commit v3 on v2

--- a/solution.py
+++ b/solution.py
@@ -20,7 +20,7 @@
 COEF = HD**-0.5 * math.log2(math.e)
 NEG = -1e30
 LIMIT = 2.0**100
-VMEM_BYTES = 56 * 2**20
+VMEM_BYTES = 22 * 2**20
 
 
 def dot(a, b, ca, cb):
@@ -103,17 +103,28 @@
     )(queries, shard)
 
 
-def attend_kernel(count, sizes, old, have, base, final, *refs):
+def attend_kernel(count, sizes, old, have, base, final, keep, given, *refs):
     q_refs = refs[:count]
     at = count
-    piece_refs = refs[at : at + len(sizes)]
-    at += len(sizes)
+    piece_refs = () if given else refs[at : at + len(sizes)]
+    at += len(piece_refs)
+    if given:
+        kv_ref, numbers = refs[at : at + 2]
+        at += 2
     in_refs = refs[at : at + count] if have else None
     at += count if have else 0
     base_ref = refs[at] if base else None
     at += 1 if base else 0
     out_refs = refs[at : at + count]
-    kv_ref, q_buf, m_buf, acc_ref, ints, blocks, tasks, sems, sem = refs[at + count :]
+    at += count
+    if keep:
+        kv_ref, numbers = refs[at : at + 2]
+        at += 2
+    elif not given:
+        kv_ref, numbers = refs[at : at + 2]
+        at += 2
+    q_buf, m_buf, acc_ref, tasks = refs[at : at + 4]
+    ints, blocks, sems, sem = (None,) * 4 if given else refs[at + 4 :]
     starts = [sum(sizes[:i]) for i in range(len(sizes) + 1)]
     shards = starts[-1]
 
@@ -128,12 +139,12 @@
         copy = pltpu.make_async_copy(ints, blocks, sem)
         copy.start()
         copy.wait()
-
-    for i in range(old, len(sizes)):
-        piece_copy(i).start()
-    for j in range(count):
-        row = q_refs[j][2 * RUN : QROWS, 0:HD].astype(jnp.float32)[6:7]
-        ints[shards + j : shards + j + 1, :] = row.astype(jnp.int32)
+        for i in range(first, last):
+            numbers[i] = blocks[i, 0]
+
+    if not given:
+        for i in range(old, len(sizes)):
+            piece_copy(i).start()
 
     def key_block(task):
         shard = task // 2
@@ -150,7 +161,7 @@
 
         def place(i, ends):
             low, high = ends
-            block = blocks[i, 0]
+            block = numbers[i]
             tasks[high] = 2 * i
             high = high - 1
             later = block > here
@@ -186,11 +197,11 @@
                 acc_ref[half] = base_ref[:, span]
             else:
                 acc_ref[half] = jnp.zeros((ACC, ROWS), jnp.float32)
-        if j == 0:
+        here = jnp.max(tail[6:7, 0:HD]).astype(jnp.int32)
+        if j == 0 and not given:
             for i in range(old, len(sizes)):
                 piece_copy(i).wait()
             read_blocks(starts[old], shards)
-        here = blocks[shards + j, 0]
         low_end, high_start = list_tasks(here, starts[old], shards)
 
         def pure(first, half):
@@ -247,7 +258,8 @@
                 piece_copy(i).start()
             for i in range(old):
                 piece_copy(i).wait()
-            read_blocks(0, starts[old])
+            if old:
+                read_blocks(0, starts[old])
             low_all, high_all = list_tasks(here, 0, shards)
             for half in range(2):
                 if base:
@@ -281,34 +293,57 @@
                 )
 
 
-def attend(q_list, new, old=(), acc=None, base=None, final=True):
+def attend(q_list, new=(), old=(), acc=None, base=None, final=True, keep=False, given=None):
     count = len(q_list)
     pieces = (tuple(old) if final else ()) + tuple(new)
     skip = len(old) if final else 0
-    sizes = tuple(p.shape[0] // SHARD for p in pieces)
+    sizes = tuple(p.shape[0] // SHARD for p in pieces) if given is None else (given[0].shape[0] // SHARD,)
     shards = sum(sizes)
-    int_rows = -(-(shards + count) // 8) * 8
-    vmem = pl.BlockSpec(memory_space=pltpu.VMEM)
-    args = tuple(q_list) + pieces + (tuple(acc) if acc is not None else ()) + ((base,) if base is not None else ())
-    extra = len(args) - count - len(pieces)
+    int_rows = -(-shards // 8) * 8
+    vmem, smem = pl.BlockSpec(memory_space=pltpu.VMEM), pl.BlockSpec(memory_space=pltpu.SMEM)
+    args = list(q_list) + list(pieces)
+    in_specs = [vmem] * count + [pl.BlockSpec(memory_space=pl.ANY)] * len(pieces)
+    if given is not None:
+        args += given
+        in_specs += [vmem, smem]
+    if acc is not None:
+        args += acc
+        in_specs += [vmem] * count
+    if base is not None:
+        args.append(base)
+        in_specs.append(vmem)
     out = jax.ShapeDtypeStruct((ACC, 2 * ROWS), jnp.bfloat16 if final and base is None else jnp.float32)
-    pairs = count * 2 * sum(sizes[skip:]) * RUN * ROWS
-    return pl.pallas_call(
-        functools.partial(attend_kernel, count, sizes, skip, acc is not None, base is not None, final),
-        out_shape=(out,) * count,
-        in_specs=[vmem] * count + [pl.BlockSpec(memory_space=pl.ANY)] * len(pieces) + [vmem] * extra,
-        out_specs=(vmem,) * count,
-        scratch_shapes=[
-            pltpu.VMEM((shards * SHARD, HD), jnp.bfloat16),
-            pltpu.VMEM((2, ROWS, HD), jnp.bfloat16),
-            pltpu.VMEM((2, 8, ROWS), jnp.float32),
-            pltpu.VMEM((2, ACC, ROWS), jnp.float32),
+    outs, out_specs = [out] * count, [vmem] * count
+    scratch = []
+    if keep:
+        outs += [
+            jax.ShapeDtypeStruct((shards * SHARD, HD), jnp.bfloat16),
+            jax.ShapeDtypeStruct((int_rows,), jnp.int32),
+        ]
+        out_specs += [vmem, smem]
+    elif given is None:
+        scratch += [pltpu.VMEM((shards * SHARD, HD), jnp.bfloat16), pltpu.SMEM((int_rows,), jnp.int32)]
+    scratch += [
+        pltpu.VMEM((2, ROWS, HD), jnp.bfloat16),
+        pltpu.VMEM((2, 8, ROWS), jnp.float32),
+        pltpu.VMEM((2, ACC, ROWS), jnp.float32),
+        pltpu.SMEM((2 * shards + 8,), jnp.int32),
+    ]
+    if given is None:
+        scratch += [
             pltpu.VMEM((int_rows, HD), jnp.int32),
             pltpu.SMEM((int_rows, HD), jnp.int32),
-            pltpu.SMEM((2 * shards + 8,), jnp.int32),
             pltpu.SemaphoreType.DMA((len(pieces),)),
             pltpu.SemaphoreType.DMA,
-        ],
+        ]
+    pairs = count * 2 * sum(sizes[skip:]) * RUN * ROWS
+    flags = (count, sizes, skip, acc is not None, base is not None, final, keep, given is not None)
+    return pl.pallas_call(
+        functools.partial(attend_kernel, *flags),
+        out_shape=outs,
+        in_specs=in_specs,
+        out_specs=out_specs,
+        scratch_shapes=scratch,
         compiler_params=pltpu.CompilerParams(vmem_limit_bytes=VMEM_BYTES),
         cost_estimate=pl.CostEstimate(flops=pairs * HD * 4, bytes_accessed=8 << 20, transcendentals=pairs),
         name="attend",
@@ -396,12 +431,15 @@
     q2 = ring_x(packed, 2)
     last = [far2, cores(far2)]
     (part1,) = attend([q1], last, first, acc=[acc1])
+    q3, part1 = lax.optimization_barrier((q3, part1))
     back1 = ring_x(part1, 1)
-    (part3,) = attend([q3], first + last)
+    part3, *whole = attend([q3], first + last, keep=True)
+    q2, part3 = lax.optimization_barrier((q2, part3))
     back3 = ring_x(part3, 3)
-    (part2,) = attend([q2], first + last)
+    (part2,) = attend([q2], given=whole)
+    packed, part2 = lax.optimization_barrier((packed, part2))
     back2 = ring_x(part2, 2)
-    (mine,) = attend([packed], first + last, base=acc0)
+    (mine,) = attend([packed], given=whole, base=acc0)
     return combine(mine, (back1, back3, back2))
 
 

time: 114 us -> 104 us (0.912)
  Pallas kernels: 70.9 us -> 48.8 us
  waiting for transfers between devices: 5.63 us -> 22.4 us
  local copies, waits for them, and re-layouts: 4.29 us -> 1.98 us
  starting transfers between devices: 32 us -> 30.8 us
    pallas_call x5, Pallas kernels: 63.1 us -> 44.9 us  [attend(): pl.pallas_call(functools.partial(attend_kernel, *flags), out_shape=outs,...]
    ppermute x16, waiting for transfers between devices: 5.63 us -> 22.4 us  [swap(): return lax.ppermute(array, AXES, pairs)]
    unnamed x30 -> x4, local copies, waits for them, and re-layouts: 4.29 us -> 1.98 us
    pallas_call x1, Pallas kernels: 3.03 us -> 0.84 us  [pack_q(): pl.pallas_call(pack_q_kernel, out_shape=(jax.ShapeDtypeStruct((QROWS, ROW...]
    pallas_call x1, Pallas kernels: 3.16 us -> 1.41 us  [combine(): pl.pallas_call(combine_kernel, out_shape=jax.ShapeDtypeStruct((2 * RUN, R...]
    ppermute x16, starting transfers between devices: 32 us -> 30.8 us  [swap(): return lax.ppermute(array, AXES, pairs)]
  transfers between devices with their start and end apart: 16 -> 16, of which waited for: 5 -> 8; matrix products, arithmetic and copies ran while one was open for 0% -> 0% of each run, Pallas kernels for 58% -> 34%
where the time goes in v3:
time: 104 us
  Pallas kernels  48.8 us (47%)
  starting transfers between devices  30.8 us (30%)
  waiting for transfers between devices  22.4 us (22%)
  local copies, waits for them, and re-layouts  1.98 us (2%)
    pallas_call x5, Pallas kernels, attend(): pl.pallas_call(functools.partial(attend_kernel, *flags), out_shape=outs,...  44.9 us
    ppermute x16, starting transfers between devices, swap(): return lax.ppermute(array, AXES, pairs)  30.8 us
    ppermute x16, waiting for transfers between devices, swap(): return lax.ppermute(array, AXES, pairs)  22.4 us
  transfers between devices with their start and end apart: 16, of which 8 were waited for; matrix products, arithmetic and copies ran while one was open for 0% of the time, Pallas kernels for 34%

profile of v3, /device:TPU:1, one launch (start us, length us, event | category | flops | bytes accessed | tf_op | source)
XLA Modules:
  0.0 104.1 jit_solution(3406293689887994195)
XLA Ops:
  0.0 1.6 %pack_kv.1.shard_ref = bf16[528,128]{1,0:T(8,128)(2,1)} custom-call(s32[256]{0:T(256)} %pos_ref.1, bf16[256,128]{1,0:T(8,128)(2,1)} %key_ref.1, bf16[256,128]{1,0:T(8,128)(2,1)} %value_ref.1), custom_call_target="tpu_custom_call" | custom-call | tf_op jit(solution)/shard_map/pack_kv/pallas_call | solution.py:56
  1.6 2.1 %collective-permute-start = (bf16[528,128]{1,0:T(8,128)(2,1)}, bf16[528,128]{1,0:T(8,128)(2,1)S(1)}, u32[]{:S(2)}, u32[]{:S(2)}) collective-permute-start(bf16[528,128]{1,0:T(8,128)(2,1)} %pack_kv.1.shard_ref), channel_id=1, source_target_pairs={{0,2},{32,40},{2,0},{34,42},{4,6},{36,44},{6,4},{38,46},{8,10},{40... | collective-permute-start | bytes 405512 | tf_op jit(solution)/shard_map/ppermute | solution.py:399
  3.8 1.9 %collective-permute-start.1 = (bf16[528,128]{1,0:T(8,128)(2,1)}, bf16[528,128]{1,0:T(8,128)(2,1)S(1)}, u32[]{:S(2)}, u32[]{:S(2)}) collective-permute-start(bf16[528,128]{1,0:T(8,128)(2,1)} %pack_kv.1.shard_ref), channel_id=1, source_target_pairs={{0,6},{32,56},{2,4},{34,58},{4,2},{36,60},{6,0},{38,62},{8,14},{40... | collective-permute-start | bytes 405512 | tf_op jit(solution)/shard_map/ppermute | solution.py:399
  6.4 0.9 copy-done
  7.3 1.0 copy-done.1
  9.4 1.8 %collective-permute-done.2 = bf16[528,128]{1,0:T(8,128)(2,1)S(1)} collective-permute-done((bf16[528,128]{1,0:T(8,128)(2,1)}, bf16[528,128]{1,0:T(8,128)(2,1)S(1)}, u32[]{:S(2)}, u32[]{:S(2)}) %collective-permute-start.2) | collective-permute-done | bytes 135200 | tf_op jit(solution)/shard_map/ppermute | solution.py:399
  11.3 1.7 %collective-permute-start.4 = (bf16[2112,128]{1,0:T(8,128)(2,1)S(1)}, bf16[2112,128]{1,0:T(8,128)(2,1)S(1)}, u32[]{:S(2)}, u32[]{:S(2)}) collective-permute-start(bf16[2112,128]{1,0:T(8,128)(2,1)S(1)} %pad_maximum_fusion.refs_1_), channel_id=1, source_target_pairs={{0,8},{32,34},{2,10},{34,32},{4,12},{36,38},{6,14},{38,36},{8,0},{... | collective-permute-start | bytes 1622024 | tf_op jit(solution)/shard_map/ppermute | solution.py:399
  13.0 1.2 %collective-permute-start.6 = (bf16[272,1024]{1,0:T(8,128)(2,1)S(1)}, bf16[272,1024]{1,0:T(8,128)(2,1)S(1)}, u32[]{:S(2)}, u32[]{:S(2)}) collective-permute-start(bf16[272,1024]{1,0:T(8,128)(2,1)S(1)} %get-tuple-element.42.refs_0_), channel_id=1, source_target_pairs={{0,1},{32,33},{2,3},{34,35},{4,5},{36,37},{6,7},{38,39},{8,9},{40,... | collective-permute-start | bytes 1671176 | tf_op jit(solution)/shard_map/ppermute | solution.py:399
  14.2 1.8 %collective-permute-start.7 = (bf16[272,1024]{1,0:T(8,128)(2,1)S(1)}, bf16[272,1024]{1,0:T(8,128)(2,1)S(1)}, u32[]{:S(2)}, u32[]{:S(2)}) collective-permute-start(bf16[272,1024]{1,0:T(8,128)(2,1)S(1)} %get-tuple-element.42.refs_0_), channel_id=1, source_target_pairs={{0,65},{32,97},{2,67},{34,99},{4,69},{36,101},{6,71},{38,103},{8,7... | collective-permute-start | bytes 1671176 | tf_op jit(solution)/shard_map/ppermute | solution.py:399
  16.0 2.2 %collective-permute-start.5 = (bf16[2112,128]{1,0:T(8,128)(2,1)S(1)}, bf16[2112,128]{1,0:T(8,128)(2,1)S(1)}, u32[]{:S(2)}, u32[]{:S(2)}) collective-permute-start(bf16[2112,128]{1,0:T(8,128)(2,1)S(1)} %pad_maximum_fusion.refs_1_), channel_id=1, source_target_pairs={{0,24},{32,38},{2,26},{34,36},{4,28},{36,34},{6,30},{38,32},{8,16}... | collective-permute-start | bytes 1622024 | tf_op jit(solution)/shard_map/ppermute | solution.py:399
  18.3 3.5 %collective-permute-start.8 = (bf16[2112,128]{1,0:T(8,128)(2,1)S(1)}, bf16[2112,128]{1,0:T(8,128)(2,1)S(1)}, u32[]{:S(2)}, u32[]{:S(2)}) collective-permute-start(bf16[2112,128]{1,0:T(8,128)(2,1)S(1)} %pad_maximum_fusion.refs_1_), channel_id=1, source_target_pairs={{0,32},{32,0},{2,34},{34,2},{4,36},{36,4},{6,38},{38,6},{8,40},{40... | collective-permute-start | bytes 1622024 | tf_op jit(solution)/shard_map/ppermute | solution.py:399
  21.8 1.7 %collective-permute-start.11 = (bf16[2112,128]{1,0:T(8,128)(2,1)S(1)}, bf16[2112,128]{1,0:T(8,128)(2,1)S(1)}, u32[]{:S(2)}, u32[]{:S(2)}) collective-permute-start(bf16[2112,128]{1,0:T(8,128)(2,1)S(1)} %pad_maximum_fusion.refs_1_), channel_id=1, source_target_pairs={{0,16},{32,36},{2,18},{34,38},{4,20},{36,32},{6,22},{38,34},{8,24}... | collective-permute-start | bytes 1622024 | tf_op jit(solution)/shard_map/ppermute | solution.py:399
  23.5 2.3 %collective-permute-done.5.refs_4_ = bf16[2112,128]{1,0:T(8,128)(2,1)S(1)} collective-permute-done((bf16[2112,128]{1,0:T(8,128)(2,1)S(1)}, bf16[2112,128]{1,0:T(8,128)(2,1)S(1)}, u32[]{:S(2)}, u32[]{:S(2)}) %collective-permute-start.5) | collective-permute-done | bytes 540704 | tf_op jit(solution)/shard_map/ppermute | solution.py:399
  26.3 9.8 %collective-permute-start.10 = (bf16[2112,128]{1,0:T(8,128)(2,1)S(1)}, bf16[2112,128]{1,0:T(8,128)(2,1)S(1)}, u32[]{:S(2)}, u32[]{:S(2)}) collective-permute-start(bf16[2112,128]{1,0:T(8,128)(2,1)S(1)} %collective-permute-done.5.refs_4_), channel_id=1, source_target_pairs={{0,32},{32,0},{2,34},{34,2},{4,36},{36,4},{6,38},{38,6},{8,40},{40... | collective-permute-start | bytes 1622024 | tf_op jit(solution)/shard_map/ppermute | solution.py:399
  38.4 8.6 %attend.5.refs_9_ = f32[144,2048]{1,0:T(8,128)S(1)} custom-call(bf16[272,1024]{1,0:T(8,128)(2,1)S(1)} %collective-permute-done.6.refs_0_, bf16[2112,128]{1,0:T(8,128)(2,1)S(1)} %pad_maximum_fusion.refs_1_, bf16[2112,128]{1,0:T(8,128)(2,1)S(1)} %collective-permute-done.8.refs_2_, bf16[2112,128]{1,0:T(8,128)(2,1)S(1)} %collective-permute-done.4.refs_3_, ...), custom_call_target="tpu_custom_call" | custom-call | flops 3221225472 | bytes 8388608 | tf_op jit(solution)/shard_map/attend/pallas_call | solution.py:341
  47.0 4.2 %attend.6 = bf16[144,2048]{1,0:T(8,128)(2,1)S(1)} custom-call(bf16[272,1024]{1,0:T(8,128)(2,1)S(1)} %collective-permute-done.6.refs_0_, bf16[2112,128]{1,0:T(8,128)(2,1)S(1)} %pad_maximum_fusion.refs_1_, bf16[2112,128]{1,0:T(8,128)(2,1)S(1)} %collective-permute-done.8.refs_2_, bf16[2112,128]{1,0:T(8,128)(2,1)S(1)} %collective-permute-done.4.refs_3_, ...), custom_call_target="tpu_custom_call" | custom-call | flops 1073741824 | bytes 8388608 | tf_op jit(solution)/shard_map/attend/pallas_call | solution.py:341
  51.1 11.7 %attend.7 = (bf16[144,2048]{1,0:T(8,128)(2,1)S(1)}, bf16[16896,128]{1,0:T(8,128)(2,1)S(1)}, s32[32]{0:T(128)S(1)}) custom-call(bf16[272,1024]{1,0:T(8,128)(2,1)S(1)} %collective-permute-done.7.refs_0_, bf16[2112,128]{1,0:T(8,128)(2,1)S(1)} %pad_maximum_fusion.refs_1_, bf16[2112,128]{1,0:T(8,128)(2,1)S(1)} %collective-permute-done.8.refs_2_, ...), custom_call_target="tpu_custom_call" | custom-call | flops 4294967296 | bytes 8388608 | tf_op jit(solution)/shard_map/attend/pallas_call | solution.py:341
  62.8 10.3 %attend.8 = bf16[144,2048]{1,0:T(8,128)(2,1)S(1)} custom-call(bf16[272,1024]{1,0:T(8,128)(2,1)S(1)} %collective-permute-done.3.refs_0_, bf16[16896,128]{1,0:T(8,128)(2,1)S(1)} %get-tuple-element.40.refs_1_, s32[32]{0:T(128)S(1)} %get-tuple-element.41.refs_2_), custom_call_target="tpu_custom_call" | custom-call | flops 4294967296 | bytes 8388608 | tf_op jit(solution)/shard_map/attend/pallas_call | solution.py:341
  73.1 1.3 %collective-permute-start.15 = (bf16[144,2048]{1,0:T(8,128)(2,1)S(1)}, bf16[144,2048]{1,0:T(8,128)(2,1)S(1)}, u32[]{:S(2)}, u32[]{:S(2)}) collective-permute-start(bf16[144,2048]{1,0:T(8,128)(2,1)S(1)} %attend.8), channel_id=1, source_target_pairs={{0,64},{32,96},{2,66},{34,98},{4,68},{36,100},{6,70},{38,102},{8,7... | collective-permute-start | bytes 1769480 | tf_op jit(solution)/shard_map/ppermute | solution.py:399
  74.4 1.2 %collective-permute-start.14 = (bf16[144,2048]{1,0:T(8,128)(2,1)S(1)}, bf16[144,2048]{1,0:T(8,128)(2,1)S(1)}, u32[]{:S(2)}, u32[]{:S(2)}) collective-permute-start(bf16[144,2048]{1,0:T(8,128)(2,1)S(1)} %get-tuple-element.45), channel_id=1, source_target_pairs={{0,65},{32,97},{2,67},{34,99},{4,69},{36,101},{6,71},{38,103},{8,7... | collective-permute-start | bytes 1769480 | tf_op jit(solution)/shard_map/ppermute | solution.py:399
  75.9 10.2 %attend.9.own_ref = f32[144,2048]{1,0:T(8,128)S(1)} custom-call(bf16[272,1024]{1,0:T(8,128)(2,1)S(1)} %get-tuple-element.42.refs_0_, bf16[16896,128]{1,0:T(8,128)(2,1)S(1)} %get-tuple-element.40.refs_1_, s32[32]{0:T(128)S(1)} %get-tuple-element.41.refs_2_, f32[144,2048]{1,0:T(8,128)S(1)} %get-tuple-element.43.refs_3_), custom_call_target="tpu_custom_call" | custom-call | flops 4294967296 | bytes 8388608 | tf_op jit(solution)/shard_map/attend/pallas_call | solution.py:341
  86.1 3.6 %collective-permute-done.15.three_ref = bf16[144,2048]{1,0:T(8,128)(2,1)S(1)} collective-permute-done((bf16[144,2048]{1,0:T(8,128)(2,1)S(1)}, bf16[144,2048]{1,0:T(8,128)(2,1)S(1)}, u32[]{:S(2)}, u32[]{:S(2)}) %collective-permute-start.15) | collective-permute-done | bytes 589856 | tf_op jit(solution)/shard_map/ppermute | solution.py:399
  89.6 13.0 %collective-permute-done.14.two_ref = bf16[144,2048]{1,0:T(8,128)(2,1)S(1)} collective-permute-done((bf16[144,2048]{1,0:T(8,128)(2,1)S(1)}, bf16[144,2048]{1,0:T(8,128)(2,1)S(1)}, u32[]{:S(2)}, u32[]{:S(2)}) %collective-permute-start.14) | collective-permute-done | bytes 589856 | tf_op jit(solution)/shard_map/ppermute | solution.py:399
  102.7 1.4 %combine.1 = bf16[256,1024]{1,0:T(8,128)(2,1)} custom-call(f32[144,2048]{1,0:T(8,128)S(1)} %attend.9.own_ref, bf16[144,2048]{1,0:T(8,128)(2,1)S(1)} %collective-permute-done.13.one_ref, bf16[144,2048]{1,0:T(8,128)(2,1)S(1)} %collective-permute-done.14.two_ref, bf16[144,2048]{1,0:T(8,128)(2,1)S(1)} %collective-permute-done.15.three_ref), custom_call_target="tpu_custom_call" | custom-call | tf_op jit(solution)/shard_map/combine/pallas_call | solution.py:377
  (21 shorter events, 4.9 us)
Async XLA Ops:
  1.6 7.6 %collective-permute-start = (bf16[528,128]{1,0:T(8,128)(2,1)}, bf16[528,128]{1,0:T(8,128)(2,1)S(1)}, u32[]{:S(2)}, u32[]{:S(2)}) collective-permute-start(bf16[528,128]{1,0:T(8,128)(2,1)} %pack_kv.1.shard_ref), channel_id=1, source_target_pairs={{0,2},{32,40},{2,0},{34,42},{4,6},{36,44},{6,4},{38,46},{8,10},{40... | collective-permute-start | bytes 405512 | tf_op jit(solution)/shard_map/ppermute | solution.py:399
  3.8 5.7 %collective-permute-start.1 = (bf16[528,128]{1,0:T(8,128)(2,1)}, bf16[528,128]{1,0:T(8,128)(2,1)S(1)}, u32[]{:S(2)}, u32[]{:S(2)}) collective-permute-start(bf16[528,128]{1,0:T(8,128)(2,1)} %pack_kv.1.shard_ref), channel_id=1, source_target_pairs={{0,6},{32,56},{2,4},{34,58},{4,2},{36,60},{6,0},{38,62},{8,14},{40... | collective-permute-start | bytes 405512 | tf_op jit(solution)/shard_map/ppermute | solution.py:399
  5.7 5.6 %collective-permute-start.2 = (bf16[528,128]{1,0:T(8,128)(2,1)}, bf16[528,128]{1,0:T(8,128)(2,1)S(1)}, u32[]{:S(2)}, u32[]{:S(2)}) collective-permute-start(bf16[528,128]{1,0:T(8,128)(2,1)} %pack_kv.1.shard_ref), channel_id=1, source_target_pairs={{0,4},{32,48},{2,6},{34,50},{4,0},{36,52},{6,2},{38,54},{8,12},{40... | collective-permute-start | bytes 405512 | tf_op jit(solution)/shard_map/ppermute | solution.py:399
  6.4 0.9 copy-start
  7.3 1.0 %copy-start.1 = (bf16[256,1024]{1,0:T(8,128)(2,1)S(1)}, bf16[256,1024]{1,0:T(8,128)(2,1)}, u32[]{:S(2)}) copy-start(bf16[256,1024]{1,0:T(8,128)(2,1)} %query_ref.1) | copy-start | bytes 1572868
  11.3 10.5 %collective-permute-start.4 = (bf16[2112,128]{1,0:T(8,128)(2,1)S(1)}, bf16[2112,128]{1,0:T(8,128)(2,1)S(1)}, u32[]{:S(2)}, u32[]{:S(2)}) collective-permute-start(bf16[2112,128]{1,0:T(8,128)(2,1)S(1)} %pad_maximum_fusion.refs_1_), channel_id=1, source_target_pairs={{0,8},{32,34},{2,10},{34,32},{4,12},{36,38},{6,14},{38,36},{8,0},{... | collective-permute-start | bytes 1622024 | tf_op jit(solution)/shard_map/ppermute | solution.py:399
  13.0 12.7 %collective-permute-start.6 = (bf16[272,1024]{1,0:T(8,128)(2,1)S(1)}, bf16[272,1024]{1,0:T(8,128)(2,1)S(1)}, u32[]{:S(2)}, u32[]{:S(2)}) collective-permute-start(bf16[272,1024]{1,0:T(8,128)(2,1)S(1)} %get-tuple-element.42.refs_0_), channel_id=1, source_target_pairs={{0,1},{32,33},{2,3},{34,35},{4,5},{36,37},{6,7},{38,39},{8,9},{40,... | collective-permute-start | bytes 1671176 | tf_op jit(solution)/shard_map/ppermute | solution.py:399
  14.2 12.0 %collective-permute-start.7 = (bf16[272,1024]{1,0:T(8,128)(2,1)S(1)}, bf16[272,1024]{1,0:T(8,128)(2,1)S(1)}, u32[]{:S(2)}, u32[]{:S(2)}) collective-permute-start(bf16[272,1024]{1,0:T(8,128)(2,1)S(1)} %get-tuple-element.42.refs_0_), channel_id=1, source_target_pairs={{0,65},{32,97},{2,67},{34,99},{4,69},{36,101},{6,71},{38,103},{8,7... | collective-permute-start | bytes 1671176 | tf_op jit(solution)/shard_map/ppermute | solution.py:399
  16.0 9.7 %collective-permute-start.5 = (bf16[2112,128]{1,0:T(8,128)(2,1)S(1)}, bf16[2112,128]{1,0:T(8,128)(2,1)S(1)}, u32[]{:S(2)}, u32[]{:S(2)}) collective-permute-start(bf16[2112,128]{1,0:T(8,128)(2,1)S(1)} %pad_maximum_fusion.refs_1_), channel_id=1, source_target_pairs={{0,24},{32,38},{2,26},{34,36},{4,28},{36,34},{6,30},{38,32},{8,16}... | collective-permute-start | bytes 1622024 | tf_op jit(solution)/shard_map/ppermute | solution.py:399
  18.3 7.5 %collective-permute-start.8 = (bf16[2112,128]{1,0:T(8,128)(2,1)S(1)}, bf16[2112,128]{1,0:T(8,128)(2,1)S(1)}, u32[]{:S(2)}, u32[]{:S(2)}) collective-permute-start(bf16[2112,128]{1,0:T(8,128)(2,1)S(1)} %pad_maximum_fusion.refs_1_), channel_id=1, source_target_pairs={{0,32},{32,0},{2,34},{34,2},{4,36},{36,4},{6,38},{38,6},{8,40},{40... | collective-permute-start | bytes 1622024 | tf_op jit(solution)/shard_map/ppermute | solution.py:399
  21.8 14.4 %collective-permute-start.11 = (bf16[2112,128]{1,0:T(8,128)(2,1)S(1)}, bf16[2112,128]{1,0:T(8,128)(2,1)S(1)}, u32[]{:S(2)}, u32[]{:S(2)}) collective-permute-start(bf16[2112,128]{1,0:T(8,128)(2,1)S(1)} %pad_maximum_fusion.refs_1_), channel_id=1, source_target_pairs={{0,16},{32,36},{2,18},{34,38},{4,20},{36,32},{6,22},{38,34},{8,24}... | collective-permute-start | bytes 1622024 | tf_op jit(solution)/shard_map/ppermute | solution.py:399
  26.3 11.4 %collective-permute-start.10 = (bf16[2112,128]{1,0:T(8,128)(2,1)S(1)}, bf16[2112,128]{1,0:T(8,128)(2,1)S(1)}, u32[]{:S(2)}, u32[]{:S(2)}) collective-permute-start(bf16[2112,128]{1,0:T(8,128)(2,1)S(1)} %collective-permute-done.5.refs_4_), channel_id=1, source_target_pairs={{0,32},{32,0},{2,34},{34,2},{4,36},{36,4},{6,38},{38,6},{8,40},{40... | collective-permute-start | bytes 1622024 | tf_op jit(solution)/shard_map/ppermute | solution.py:399
  36.1 2.3 %collective-permute-start.9 = (bf16[2112,128]{1,0:T(8,128)(2,1)S(1)}, bf16[2112,128]{1,0:T(8,128)(2,1)S(1)}, u32[]{:S(2)}, u32[]{:S(2)}) collective-permute-start(bf16[2112,128]{1,0:T(8,128)(2,1)S(1)} %collective-permute-done.4.refs_3_), channel_id=1, source_target_pairs={{0,32},{32,0},{2,34},{34,2},{4,36},{36,4},{6,38},{38,6},{8,40},{40... | collective-permute-start | bytes 1622024 | tf_op jit(solution)/shard_map/ppermute | solution.py:399
  36.1 10.8 %collective-permute-start.12 = (bf16[2112,128]{1,0:T(8,128)(2,1)S(1)}, bf16[2112,128]{1,0:T(8,128)(2,1)S(1)}, u32[]{:S(2)}, u32[]{:S(2)}) collective-permute-start(bf16[2112,128]{1,0:T(8,128)(2,1)S(1)} %collective-permute-done.11.refs_7_), channel_id=1, source_target_pairs={{0,32},{32,0},{2,34},{34,2},{4,36},{36,4},{6,38},{38,6},{8,40},{40... | collective-permute-start | bytes 1622024 | tf_op jit(solution)/shard_map/ppermute | solution.py:399
  36.6 26.2 %collective-permute-start.3 = (bf16[272,1024]{1,0:T(8,128)(2,1)S(1)}, bf16[272,1024]{1,0:T(8,128)(2,1)S(1)}, u32[]{:S(2)}, u32[]{:S(2)}) collective-permute-start(bf16[272,1024]{1,0:T(8,128)(2,1)S(1)} %get-tuple-element.42.refs_0_), channel_id=1, source_target_pairs={{0,64},{32,96},{2,66},{34,98},{4,68},{36,100},{6,70},{38,102},{8,7... | collective-permute-start | bytes 1671176 | tf_op jit(solution)/shard_map/ppermute | solution.py:399
  73.1 16.5 %collective-permute-start.15 = (bf16[144,2048]{1,0:T(8,128)(2,1)S(1)}, bf16[144,2048]{1,0:T(8,128)(2,1)S(1)}, u32[]{:S(2)}, u32[]{:S(2)}) collective-permute-start(bf16[144,2048]{1,0:T(8,128)(2,1)S(1)} %attend.8), channel_id=1, source_target_pairs={{0,64},{32,96},{2,66},{34,98},{4,68},{36,100},{6,70},{38,102},{8,7... | collective-permute-start | bytes 1769480 | tf_op jit(solution)/shard_map/ppermute | solution.py:399
  74.4 28.3 %collective-permute-start.14 = (bf16[144,2048]{1,0:T(8,128)(2,1)S(1)}, bf16[144,2048]{1,0:T(8,128)(2,1)S(1)}, u32[]{:S(2)}, u32[]{:S(2)}) collective-permute-start(bf16[144,2048]{1,0:T(8,128)(2,1)S(1)} %get-tuple-element.45), channel_id=1, source_target_pairs={{0,65},{32,97},{2,67},{34,99},{4,69},{36,101},{6,71},{38,103},{8,7... | collective-permute-start | bytes 1769480 | tf_op jit(solution)/shard_map/ppermute | solution.py:399
  75.6 27.1 %collective-permute-start.13 = (bf16[144,2048]{1,0:T(8,128)(2,1)S(1)}, bf16[144,2048]{1,0:T(8,128)(2,1)S(1)}, u32[]{:S(2)}, u32[]{:S(2)}) collective-permute-start(bf16[144,2048]{1,0:T(8,128)(2,1)S(1)} %attend.6), channel_id=1, source_target_pairs={{0,1},{32,33},{2,3},{34,35},{4,5},{36,37},{6,7},{38,39},{8,9},{40,... | collective-permute-start | bytes 1769480 | tf_op jit(solution)/shard_map/ppermute | solution.py:399

commit v4 on v3

--- a/solution.py
+++ b/solution.py
@@ -16,7 +16,6 @@
 SHARD = 4 * RUN + 16
 QROWS = 2 * RUN + 16
 ACC = HD + 16
-GROUP = 8
 COEF = HD**-0.5 * math.log2(math.e)
 NEG = -1e30
 LIMIT = 2.0**100
@@ -103,7 +102,8 @@
     )(queries, shard)
 
 
-def attend_kernel(count, sizes, old, have, base, final, keep, given, *refs):
+def attend_kernel(count, sizes, old, done, only, have, base, final, keep, given, *refs):
+    halves = (0, 1) if only is None else (only,)
     q_refs = refs[:count]
     at = count
     piece_refs = () if given else refs[at : at + len(sizes)]
@@ -127,6 +127,7 @@
     ints, blocks, sems, sem = (None,) * 4 if given else refs[at + 4 :]
     starts = [sum(sizes[:i]) for i in range(len(sizes) + 1)]
     shards = starts[-1]
+    group = 16 if shards - done >= 24 and given and only is None else 8
 
     def piece_copy(i):
         there = kv_ref.at[pl.ds(starts[i] * SHARD, sizes[i] * SHARD), :]
@@ -143,7 +144,7 @@
             numbers[i] = blocks[i, 0]
 
     if not given:
-        for i in range(old, len(sizes)):
+        for i in list(range(old, len(sizes))) + (list(range(old)) if keep else []):
             piece_copy(i).start()
 
     def key_block(task):
@@ -177,12 +178,12 @@
         low_end, high_end = lax.fori_loop(first, last, place, (jnp.int32(0), jnp.int32(total - 1)))
         return low_end, high_end + 1
 
-    ones = jnp.ones((16, GROUP * RUN), jnp.bfloat16)
+    ones = jnp.ones((16, group * RUN), jnp.bfloat16)
 
     for j in range(count):
         q_ref = q_refs[j]
         tail = q_ref[2 * RUN : QROWS, :].astype(jnp.float32)
-        for half in range(2):
+        for half in halves:
             span = slice(half * ROWS, (half + 1) * ROWS)
             q_buf[half] = query_tile(q_ref, half)
             m_buf[half] = jnp.broadcast_to(
@@ -202,66 +203,75 @@
             for i in range(old, len(sizes)):
                 piece_copy(i).wait()
             read_blocks(starts[old], shards)
-        low_end, high_start = list_tasks(here, starts[old], shards)
+        low_end, high_start = list_tasks(here, done, shards)
 
         def pure(first, half):
             query = q_buf[half]
             shift = m_buf[half][0:1]
             parts = []
-            for b in range(0, GROUP, 2):
+            for b in range(0, group, 2):
                 keys = jnp.concatenate([key_block(tasks[first + b]), key_block(tasks[first + b + 1])], axis=0)
                 parts.append(jnp.exp2(dot(keys, query, 1, 1) * COEF - shift).astype(jnp.bfloat16))
             weights = jnp.concatenate(parts, axis=0)
-            vt = jnp.concatenate([value_block(tasks[first + b]) for b in range(GROUP)], axis=1)
+            vt = jnp.concatenate([value_block(tasks[first + b]) for b in range(group)], axis=1)
             vt = jnp.concatenate([vt, ones], axis=0)
             acc_ref[half] += dot(vt, weights, 1, 0)
 
         def mixed(first):
             parts = []
-            for b in range(GROUP):
-                half = (first + b >= high_start).astype(jnp.int32)
+            for b in range(group):
+                half = (first + b >= high_start).astype(jnp.int32) if only is None else only
                 scores = dot(key_block(tasks[first + b]), q_buf[half], 1, 1)
                 parts.append(jnp.exp2(scores * COEF - m_buf[half][0:1]).astype(jnp.bfloat16))
             weights = jnp.concatenate(parts, axis=0)
-            vt = jnp.concatenate([value_block(tasks[first + b]) for b in range(GROUP)], axis=1)
+            vt = jnp.concatenate([value_block(tasks[first + b]) for b in range(group)], axis=1)
             vt = jnp.concatenate([vt, ones], axis=0)
-            index = first + lax.broadcasted_iota(jnp.int32, (1, GROUP * RUN), 1) // RUN
+            index = first + lax.broadcasted_iota(jnp.int32, (1, group * RUN), 1) // RUN
             zero = jnp.zeros((), jnp.bfloat16)
-            acc_ref[0] += dot(jnp.where(index < low_end, vt, zero), weights, 1, 0)
-            acc_ref[1] += dot(jnp.where(index >= high_start, vt, zero), weights, 1, 0)
-
-        @pl.loop(0, 2 * (shards - starts[old]) // GROUP)
+            if 0 in halves:
+                acc_ref[0] += dot(jnp.where(index < low_end, vt, zero), weights, 1, 0)
+            if 1 in halves:
+                acc_ref[1] += dot(jnp.where(index >= high_start, vt, zero), weights, 1, 0)
+
+        steps = 2 * (shards - done) // group
+
+        @pl.loop(high_start // group if only == 1 else 0, (low_end + group - 1) // group if only == 0 else steps)
         def _(g):
-            first = g * GROUP
-            is_low = first + GROUP <= low_end
+            first = g * group
+            is_low = first + group <= low_end
             is_high = first >= high_start
 
             @pl.when(jnp.logical_or(is_low, is_high))
             def _():
-                pure(first, is_high.astype(jnp.int32))
+                pure(first, is_high.astype(jnp.int32) if only is None else only)
 
             @pl.when(jnp.logical_not(jnp.logical_or(is_low, is_high)))
             def _():
                 mixed(first)
+
+        if keep and old:
+            for i in range(old):
+                piece_copy(i).wait()
+            read_blocks(0, starts[old])
 
         if not final:
             for half in range(2):
                 out_refs[j][:, half * ROWS : (half + 1) * ROWS] = acc_ref[half]
             continue
 
-        sums = jnp.maximum(acc_ref[0][HD : HD + 8], acc_ref[1][HD : HD + 8])
+        sums = functools.reduce(jnp.maximum, [acc_ref[half][HD : HD + 8] for half in halves])
         fine = jnp.min(jnp.where(sums < LIMIT, 1.0, 0.0)) > 0.5
 
         @pl.when(jnp.logical_not(fine))
         def _():
-            for i in range(old):
-                piece_copy(i).start()
-            for i in range(old):
-                piece_copy(i).wait()
-            if old:
+            if old and not keep:
+                for i in range(old):
+                    piece_copy(i).start()
+                for i in range(old):
+                    piece_copy(i).wait()
                 read_blocks(0, starts[old])
             low_all, high_all = list_tasks(here, 0, shards)
-            for half in range(2):
+            for half in halves:
                 if base:
                     acc_ref[half] = base_ref[:, half * ROWS : (half + 1) * ROWS]
                 else:
@@ -269,9 +279,12 @@
 
             @pl.loop(0, 2 * shards)
             def _(t):
-                @pl.when(jnp.logical_or(t < low_all, t >= high_all))
+                in_low = jnp.logical_and(t < low_all, only != 1)
+                in_high = jnp.logical_and(t >= high_all, only != 0)
+
+                @pl.when(jnp.logical_or(in_low, in_high))
                 def _():
-                    half = (t >= high_all).astype(jnp.int32)
+                    half = (t >= high_all).astype(jnp.int32) if only is None else only
                     scores = dot(key_block(tasks[t]), q_buf[half], 1, 1) * COEF
                     before = m_buf[half][0:1]
                     new = jnp.maximum(before, jnp.max(scores, axis=0, keepdims=True))
@@ -280,8 +293,8 @@
                     acc_ref[half] = acc_ref[half] * jnp.exp2(before - new) + dot(vt, weights, 1, 0)
                     m_buf[half] = jnp.broadcast_to(new, (8, ROWS))
 
-        for half in range(2):
-            span = slice(half * ROWS, (half + 1) * ROWS)
+        for half in halves:
+            span = slice(half * ROWS, (half + 1) * ROWS) if only is None else slice(0, ROWS)
             if base:
                 out_refs[j][0 : HD + 8, span] = acc_ref[half][0 : HD + 8]
                 out_refs[j][HD + 8 : ACC, span] = m_buf[half]
@@ -293,12 +306,13 @@
                 )
 
 
-def attend(q_list, new=(), old=(), acc=None, base=None, final=True, keep=False, given=None):
+def attend(q_list, new=(), old=(), acc=None, base=None, final=True, keep=False, given=None, done=0, only=None):
     count = len(q_list)
     pieces = (tuple(old) if final else ()) + tuple(new)
     skip = len(old) if final else 0
     sizes = tuple(p.shape[0] // SHARD for p in pieces) if given is None else (given[0].shape[0] // SHARD,)
     shards = sum(sizes)
+    done = done if given is not None else sum(sizes[:skip])
     int_rows = -(-shards // 8) * 8
     vmem, smem = pl.BlockSpec(memory_space=pltpu.VMEM), pl.BlockSpec(memory_space=pltpu.SMEM)
     args = list(q_list) + list(pieces)
@@ -312,7 +326,7 @@
     if base is not None:
         args.append(base)
         in_specs.append(vmem)
-    out = jax.ShapeDtypeStruct((ACC, 2 * ROWS), jnp.bfloat16 if final and base is None else jnp.float32)
+    out = jax.ShapeDtypeStruct((ACC, (2 if only is None else 1) * ROWS), jnp.bfloat16 if final and base is None else jnp.float32)
     outs, out_specs = [out] * count, [vmem] * count
     scratch = []
     if keep:
@@ -336,8 +350,8 @@
             pltpu.SemaphoreType.DMA((len(pieces),)),
             pltpu.SemaphoreType.DMA,
         ]
-    pairs = count * 2 * sum(sizes[skip:]) * RUN * ROWS
-    flags = (count, sizes, skip, acc is not None, base is not None, final, keep, given is not None)
+    pairs = count * 2 * (shards - done) * RUN * ROWS
+    flags = (count, sizes, skip, done, only, acc is not None, base is not None, final, keep, given is not None)
     return pl.pallas_call(
         functools.partial(attend_kernel, *flags),
         out_shape=outs,
@@ -345,21 +359,22 @@
         out_specs=out_specs,
         scratch_shapes=scratch,
         compiler_params=pltpu.CompilerParams(vmem_limit_bytes=VMEM_BYTES),
-        cost_estimate=pl.CostEstimate(flops=pairs * HD * 4, bytes_accessed=8 << 20, transcendentals=pairs),
+        cost_estimate=pl.CostEstimate(flops=pairs, bytes_accessed=1 << 20, transcendentals=0),
         name="attend",
     )(*args)
 
 
-def combine_kernel(own_ref, one_ref, two_ref, three_ref, out_ref):
+def combine_kernel(own_ref, one_ref, two_ref, low_ref, high_ref, out_ref):
     for half in range(2):
         for h in range(HEADS):
             span = slice(half * ROWS + h * RUN, half * ROWS + (h + 1) * RUN)
             parts = [(own_ref[0:HD, span], own_ref[HD : HD + 1, span], own_ref[HD + 8 : HD + 9, span])]
-            for ref in (one_ref, two_ref, three_ref):
-                tail = ref[HD:ACC, span].astype(jnp.float32)
+            within = slice(h * RUN, (h + 1) * RUN)
+            for ref, at in ((one_ref, span), (two_ref, span), ((low_ref, high_ref)[half], within)):
+                tail = ref[HD:ACC, at].astype(jnp.float32)
                 parts.append(
                     (
-                        ref[0:HD, span].astype(jnp.float32),
+                        ref[0:HD, at].astype(jnp.float32),
                         tail[0:1] + tail[1:2] + tail[2:3],
                         tail[3:4] + tail[4:5] + tail[5:6],
                     )
@@ -377,7 +392,7 @@
     return pl.pallas_call(
         combine_kernel,
         out_shape=jax.ShapeDtypeStruct((2 * RUN, ROWS), jnp.bfloat16),
-        in_specs=[pl.BlockSpec(memory_space=pltpu.VMEM)] * 4,
+        in_specs=[pl.BlockSpec(memory_space=pltpu.VMEM)] * 5,
         out_specs=pl.BlockSpec(memory_space=pltpu.VMEM),
         compiler_params=pltpu.CompilerParams(vmem_limit_bytes=VMEM_BYTES),
         name="combine",
@@ -421,26 +436,34 @@
     packed, acc0 = pack_q(queries, shard)
     near, packed, acc0 = lax.optimization_barrier((near, packed, acc0))
     line = jnp.concatenate([shard] + near, axis=0)
+    q2 = ring_x(packed, 2)
+    far1, far3 = ring_second(line, 1), ring_second(line, 3)
+    line_x = cores(line)
+    (acc_own,) = attend([packed], [line, line_x], base=acc0, final=False)
+    far1, far3, q2, line_x, line, packed, acc_own = lax.optimization_barrier(
+        (far1, far3, q2, line_x, line, packed, acc_own)
+    )
+    far2 = ring_second(line, 2)
     q1, q3 = ring_x(packed, 1), ring_x(packed, 3)
-    far1, far3 = ring_second(line, 1), ring_second(line, 3)
-    far2 = ring_second(line, 2)
-    line_x = cores(line)
-    far1, far3, q1, q3, line_x = lax.optimization_barrier((far1, far3, q1, q3, line_x))
     first = [line, line_x, far1, far3, cores(far1), cores(far3)]
-    (acc1,) = attend([q1], first, final=False)
-    q2 = ring_x(packed, 2)
+    (acc2,) = attend([q2], first, final=False)
+    far2, acc2 = lax.optimization_barrier((far2, acc2))
     last = [far2, cores(far2)]
-    (part1,) = attend([q1], last, first, acc=[acc1])
+    part2, *whole = attend([q2], last, first, acc=[acc2], keep=True)
+    q1, q3, part2 = lax.optimization_barrier((q1, q3, part2))
+    back2 = ring_x(part2, 2)
+    (part1,) = attend([q1], given=whole)
     q3, part1 = lax.optimization_barrier((q3, part1))
     back1 = ring_x(part1, 1)
-    part3, *whole = attend([q3], first + last, keep=True)
-    q2, part3 = lax.optimization_barrier((q2, part3))
-    back3 = ring_x(part3, 3)
-    (part2,) = attend([q2], given=whole)
-    packed, part2 = lax.optimization_barrier((packed, part2))
-    back2 = ring_x(part2, 2)
-    (mine,) = attend([packed], given=whole, base=acc0)
-    return combine(mine, (back1, back3, back2))
+    (low3,) = attend([q3], given=whole, only=0)
+    q3, low3, back2 = lax.optimization_barrier((q3, low3, back2))
+    back_low = ring_x(low3, 3)
+    (high3,) = attend([q3], given=whole, only=1)
+    packed, high3 = lax.optimization_barrier((packed, high3))
+    back_high = ring_x(high3, 3)
+    packed, back_low = lax.optimization_barrier((packed, back_low))
+    (mine,) = attend([packed], given=whole, acc=[acc_own], base=acc0, done=8)
+    return combine(mine, (back1, back2, back_low, back_high))
 
 
 def solution(mesh):

time: 104 us -> 89.2 us (0.86)
  the two profiles are of different devices: /device:TPU:1 before, /device:TPU:8 now
where the time goes in v4:
time: 89.2 us; the launch traced here: 88.4 us
  Pallas kernels  50.7 us (57%)
  starting transfers between devices  23.2 us (26%)
  waiting for transfers between devices  12.3 us (14%)
  local copies, waits for them, and re-layouts  1.98 us (2%)
    pallas_call x7, Pallas kernels, attend(): pl.pallas_call(functools.partial(attend_kernel, *flags), out_shape=outs,...  46.9 us
    ppermute x17, starting transfers between devices, swap(): return lax.ppermute(array, AXES, pairs)  23.2 us
    ppermute x17, waiting for transfers between devices, swap(): return lax.ppermute(array, AXES, pairs)  12.3 us
    unnamed x4, local copies, waits for them, and re-layouts  1.98 us
  transfers between devices with their start and end apart: 17, of which 7 were waited for; matrix products, arithmetic and copies ran while one was open for 0% of the time, Pallas kernels for 54%

profile of v4, /device:TPU:8, one launch (start us, length us, event | category | flops | bytes accessed | tf_op | source)
XLA Modules:
  0.0 88.4 jit_solution(3371749043488606673)
XLA Ops:
  0.0 1.6 %pack_kv.1.shard_ref = bf16[528,128]{1,0:T(8,128)(2,1)} custom-call(s32[256]{0:T(256)} %pos_ref.1, bf16[256,128]{1,0:T(8,128)(2,1)} %key_ref.1, bf16[256,128]{1,0:T(8,128)(2,1)} %value_ref.1), custom_call_target="tpu_custom_call" | custom-call | tf_op jit(solution)/shard_map/pack_kv/pallas_call | solution.py:55
  1.6 1.9 %collective-permute-start = (bf16[528,128]{1,0:T(8,128)(2,1)}, bf16[528,128]{1,0:T(8,128)(2,1)S(1)}, u32[]{:S(2)}, u32[]{:S(2)}) collective-permute-start(bf16[528,128]{1,0:T(8,128)(2,1)} %pack_kv.1.shard_ref), channel_id=1, source_target_pairs={{0,2},{32,40},{2,0},{34,42},{4,6},{36,44},{6,4},{38,46},{8,10},{40... | collective-permute-start | bytes 405512 | tf_op jit(solution)/shard_map/ppermute | solution.py:414
  3.6 2.5 %collective-permute-start.1 = (bf16[528,128]{1,0:T(8,128)(2,1)}, bf16[528,128]{1,0:T(8,128)(2,1)S(1)}, u32[]{:S(2)}, u32[]{:S(2)}) collective-permute-start(bf16[528,128]{1,0:T(8,128)(2,1)} %pack_kv.1.shard_ref), channel_id=1, source_target_pairs={{0,6},{32,56},{2,4},{34,58},{4,2},{36,60},{6,0},{38,62},{8,14},{40... | collective-permute-start | bytes 405512 | tf_op jit(solution)/shard_map/ppermute | solution.py:414
  6.1 1.1 %collective-permute-start.2 = (bf16[528,128]{1,0:T(8,128)(2,1)}, bf16[528,128]{1,0:T(8,128)(2,1)S(1)}, u32[]{:S(2)}, u32[]{:S(2)}) collective-permute-start(bf16[528,128]{1,0:T(8,128)(2,1)} %pack_kv.1.shard_ref), channel_id=1, source_target_pairs={{0,4},{32,48},{2,6},{34,50},{4,0},{36,52},{6,2},{38,54},{8,12},{40... | collective-permute-start | bytes 405512 | tf_op jit(solution)/shard_map/ppermute | solution.py:414
  7.1 0.9 %copy-done = bf16[528,128]{1,0:T(8,128)(2,1)S(1)} copy-done((bf16[528,128]{1,0:T(8,128)(2,1)S(1)}, bf16[528,128]{1,0:T(8,128)(2,1)}, u32[]{:S(2)}) %copy-start) | copy-done | bytes 135192
  8.1 1.0 %copy-done.1 = bf16[256,1024]{1,0:T(8,128)(2,1)S(1)} copy-done((bf16[256,1024]{1,0:T(8,128)(2,1)S(1)}, bf16[256,1024]{1,0:T(8,128)(2,1)}, u32[]{:S(2)}) %copy-start.1) | copy-done | bytes 524312
  10.4 2.4 %collective-permute-done.2 = bf16[528,128]{1,0:T(8,128)(2,1)S(1)} collective-permute-done((bf16[528,128]{1,0:T(8,128)(2,1)}, bf16[528,128]{1,0:T(8,128)(2,1)S(1)}, u32[]{:S(2)}, u32[]{:S(2)}) %collective-permute-start.2) | collective-permute-done | bytes 135200 | tf_op jit(solution)/shard_map/ppermute | solution.py:414
  12.8 3.0 %collective-permute-start.5 = (bf16[272,1024]{1,0:T(8,128)(2,1)S(1)}, bf16[272,1024]{1,0:T(8,128)(2,1)S(1)}, u32[]{:S(2)}, u32[]{:S(2)}) collective-permute-start(bf16[272,1024]{1,0:T(8,128)(2,1)S(1)} %get-tuple-element.61.refs_0_), channel_id=1, source_target_pairs={{0,64},{32,96},{2,66},{34,98},{4,68},{36,100},{6,70},{38,102},{8,7... | collective-permute-start | bytes 1671176 | tf_op jit(solution)/shard_map/ppermute | solution.py:414
  16.5 2.4 %collective-permute-start.4 = (bf16[2112,128]{1,0:T(8,128)(2,1)S(1)}, bf16[2112,128]{1,0:T(8,128)(2,1)S(1)}, u32[]{:S(2)}, u32[]{:S(2)}) collective-permute-start(bf16[2112,128]{1,0:T(8,128)(2,1)S(1)} %pad_maximum_fusion.refs_1_), channel_id=1, source_target_pairs={{0,24},{32,38},{2,26},{34,36},{4,28},{36,34},{6,30},{38,32},{8,16}... | collective-permute-start | bytes 1622024 | tf_op jit(solution)/shard_map/ppermute | solution.py:414
  18.9 3.6 %attend.7.refs_3_ = f32[144,2048]{1,0:T(8,128)S(1)} custom-call(bf16[272,1024]{1,0:T(8,128)(2,1)S(1)} %get-tuple-element.61.refs_0_, bf16[2112,128]{1,0:T(8,128)(2,1)S(1)} %pad_maximum_fusion.refs_1_, bf16[2112,128]{1,0:T(8,128)(2,1)S(1)} %collective-permute-done.6.refs_2_, f32[144,2048]{1,0:T(8,128)S(1)} %get-tuple-element.42.refs_3_.refs_4_), custom_call_target="tpu_custom_call" | custom-call | flops 2097152 | bytes 1048576 | tf_op jit(solution)/shard_map/attend/pallas_call | solution.py:355
  22.5 2.9 %collective-permute-done.3.refs_3_ = bf16[2112,128]{1,0:T(8,128)(2,1)S(1)} collective-permute-done((bf16[2112,128]{1,0:T(8,128)(2,1)S(1)}, bf16[2112,128]{1,0:T(8,128)(2,1)S(1)}, u32[]{:S(2)}, u32[]{:S(2)}) %collective-permute-start.3) | collective-permute-done | bytes 540704 | tf_op jit(solution)/shard_map/ppermute | solution.py:414
  26.8 3.4 %collective-permute-start.11 = (bf16[2112,128]{1,0:T(8,128)(2,1)S(1)}, bf16[2112,128]{1,0:T(8,128)(2,1)S(1)}, u32[]{:S(2)}, u32[]{:S(2)}) collective-permute-start(bf16[2112,128]{1,0:T(8,128)(2,1)S(1)} %pad_maximum_fusion.refs_1_), channel_id=1, source_target_pairs={{0,16},{32,36},{2,18},{34,38},{4,20},{36,32},{6,22},{38,34},{8,24}... | collective-permute-start | bytes 1622024 | tf_op jit(solution)/shard_map/ppermute | solution.py:414
  31.4 8.6 %attend.8.refs_9_ = f32[144,2048]{1,0:T(8,128)S(1)} custom-call(bf16[272,1024]{1,0:T(8,128)(2,1)S(1)} %collective-permute-done.5.refs_0_, bf16[2112,128]{1,0:T(8,128)(2,1)S(1)} %pad_maximum_fusion.refs_1_, bf16[2112,128]{1,0:T(8,128)(2,1)S(1)} %collective-permute-done.6.refs_2_, bf16[2112,128]{1,0:T(8,128)(2,1)S(1)} %collective-permute-done.3.refs_3_, ...), custom_call_target="tpu_custom_call" | custom-call | flops 6291456 | bytes 1048576 | tf_op jit(solution)/shard_map/attend/pallas_call | solution.py:355
  40.0 1.7 %collective-permute-start.12 = (bf16[2112,128]{1,0:T(8,128)(2,1)S(1)}, bf16[2112,128]{1,0:T(8,128)(2,1)S(1)}, u32[]{:S(2)}, u32[]{:S(2)}) collective-permute-start(bf16[2112,128]{1,0:T(8,128)(2,1)S(1)} %collective-permute-done.11.refs_7_), channel_id=1, source_target_pairs={{0,32},{32,0},{2,34},{34,2},{4,36},{36,4},{6,38},{38,6},{8,40},{40... | collective-permute-start | bytes 1622024 | tf_op jit(solution)/shard_map/ppermute | solution.py:414
  41.7 1.6 %collective-permute-done.12.refs_8_ = bf16[2112,128]{1,0:T(8,128)(2,1)S(1)} collective-permute-done((bf16[2112,128]{1,0:T(8,128)(2,1)S(1)}, bf16[2112,128]{1,0:T(8,128)(2,1)S(1)}, u32[]{:S(2)}, u32[]{:S(2)}) %collective-permute-start.12) | collective-permute-done | bytes 540704 | tf_op jit(solution)/shard_map/ppermute | solution.py:414
  43.2 5.6 %attend.9 = (bf16[144,2048]{1,0:T(8,128)(2,1)S(1)}, bf16[16896,128]{1,0:T(8,128)(2,1)S(1)}, s32[32]{0:T(128)S(1)}) custom-call(bf16[272,1024]{1,0:T(8,128)(2,1)S(1)} %collective-permute-done.5.refs_0_, bf16[2112,128]{1,0:T(8,128)(2,1)S(1)} %pad_maximum_fusion.refs_1_, bf16[2112,128]{1,0:T(8,128)(2,1)S(1)} %collective-permute-done.6.refs_2_, ...), custom_call_target="tpu_custom_call" | custom-call | flops 2097152 | bytes 1048576 | tf_op jit(solution)/shard_map/attend/pallas_call | solution.py:355
  48.9 1.9 %collective-permute-start.13 = (bf16[144,2048]{1,0:T(8,128)(2,1)S(1)}, bf16[144,2048]{1,0:T(8,128)(2,1)S(1)}, u32[]{:S(2)}, u32[]{:S(2)}) collective-permute-start(bf16[144,2048]{1,0:T(8,128)(2,1)S(1)} %get-tuple-element.57), channel_id=1, source_target_pairs={{0,64},{32,96},{2,66},{34,98},{4,68},{36,100},{6,70},{38,102},{8,7... | collective-permute-start | bytes 1769480 | tf_op jit(solution)/shard_map/ppermute | solution.py:414
  50.8 9.9 %attend.10 = bf16[144,2048]{1,0:T(8,128)(2,1)S(1)} custom-call(bf16[272,1024]{1,0:T(8,128)(2,1)S(1)} %collective-permute-done.7.refs_0_, bf16[16896,128]{1,0:T(8,128)(2,1)S(1)} %get-tuple-element.54.refs_1_, s32[32]{0:T(128)S(1)} %get-tuple-element.55.refs_2_), custom_call_target="tpu_custom_call" | custom-call | flops 8388608 | bytes 1048576 | tf_op jit(solution)/shard_map/attend/pallas_call | solution.py:355
  61.4 1.2 %attend.11 = bf16[144,1024]{1,0:T(8,128)(2,1)S(1)} custom-call(bf16[272,1024]{1,0:T(8,128)(2,1)S(1)} %collective-permute-done.8.refs_0_, bf16[16896,128]{1,0:T(8,128)(2,1)S(1)} %get-tuple-element.54.refs_1_, s32[32]{0:T(128)S(1)} %get-tuple-element.55.refs_2_), custom_call_target="tpu_custom_call" | custom-call | flops 8388608 | bytes 1048576 | tf_op jit(solution)/shard_map/attend/pallas_call | solution.py:355
  62.6 4.0 %collective-permute-done.13.two_ref = bf16[144,2048]{1,0:T(8,128)(2,1)S(1)} collective-permute-done((bf16[144,2048]{1,0:T(8,128)(2,1)S(1)}, bf16[144,2048]{1,0:T(8,128)(2,1)S(1)}, u32[]{:S(2)}, u32[]{:S(2)}) %collective-permute-start.13) | collective-permute-done | bytes 589856 | tf_op jit(solution)/shard_map/ppermute | solution.py:414
  66.6 2.2 %collective-permute-start.14 = (bf16[144,1024]{1,0:T(8,128)(2,1)S(1)}, bf16[144,1024]{1,0:T(8,128)(2,1)S(1)}, u32[]{:S(2)}, u32[]{:S(2)}) collective-permute-start(bf16[144,1024]{1,0:T(8,128)(2,1)S(1)} %attend.11), channel_id=1, source_target_pairs={{0,65},{32,97},{2,67},{34,99},{4,69},{36,101},{6,71},{38,103},{8,7... | collective-permute-start | bytes 884744 | tf_op jit(solution)/shard_map/ppermute | solution.py:414
  68.8 10.2 %attend.12 = bf16[144,1024]{1,0:T(8,128)(2,1)S(1)} custom-call(bf16[272,1024]{1,0:T(8,128)(2,1)S(1)} %collective-permute-done.8.refs_0_, bf16[16896,128]{1,0:T(8,128)(2,1)S(1)} %get-tuple-element.54.refs_1_, s32[32]{0:T(128)S(1)} %get-tuple-element.55.refs_2_), custom_call_target="tpu_custom_call" | custom-call | flops 8388608 | bytes 1048576 | tf_op jit(solution)/shard_map/attend/pallas_call | solution.py:355
  79.1 7.7 %attend.13.own_ref = f32[144,2048]{1,0:T(8,128)S(1)} custom-call(bf16[272,1024]{1,0:T(8,128)(2,1)S(1)} %get-tuple-element.61.refs_0_, bf16[16896,128]{1,0:T(8,128)(2,1)S(1)} %get-tuple-element.54.refs_1_, s32[32]{0:T(128)S(1)} %get-tuple-element.55.refs_2_, f32[144,2048]{1,0:T(8,128)S(1)} %attend.7.refs_3_, f32[144,2048]{1,0:T(8,128)S(1)} %get-tuple-element.42.refs_3_.refs_4_), custom_call_target="tpu_custom_call" | custom-call | flops 6291456 | bytes 1048576 | tf_op jit(solution)/shard_map/attend/pallas_call | solution.py:355
  87.0 1.4 %combine.1 = bf16[256,1024]{1,0:T(8,128)(2,1)} custom-call(f32[144,2048]{1,0:T(8,128)S(1)} %attend.13.own_ref, bf16[144,2048]{1,0:T(8,128)(2,1)S(1)} %collective-permute-done.15.one_ref, bf16[144,2048]{1,0:T(8,128)(2,1)S(1)} %collective-permute-done.13.two_ref, bf16[144,1024]{1,0:T(8,128)(2,1)S(1)} %collective-permute-done.14.low_ref, ...), custom_call_target="tpu_custom_call" | custom-call | tf_op jit(solution)/shard_map/combine/pallas_call | solution.py:392
  (25 shorter events, 5.4 us)
Async XLA Ops:
  1.6 8.3 %collective-permute-start = (bf16[528,128]{1,0:T(8,128)(2,1)}, bf16[528,128]{1,0:T(8,128)(2,1)S(1)}, u32[]{:S(2)}, u32[]{:S(2)}) collective-permute-start(bf16[528,128]{1,0:T(8,128)(2,1)} %pack_kv.1.shard_ref), channel_id=1, source_target_pairs={{0,2},{32,40},{2,0},{34,42},{4,6},{36,44},{6,4},{38,46},{8,10},{40... | collective-permute-start | bytes 405512 | tf_op jit(solution)/shard_map/ppermute | solution.py:414
  3.6 6.8 %collective-permute-start.1 = (bf16[528,128]{1,0:T(8,128)(2,1)}, bf16[528,128]{1,0:T(8,128)(2,1)S(1)}, u32[]{:S(2)}, u32[]{:S(2)}) collective-permute-start(bf16[528,128]{1,0:T(8,128)(2,1)} %pack_kv.1.shard_ref), channel_id=1, source_target_pairs={{0,6},{32,56},{2,4},{34,58},{4,2},{36,60},{6,0},{38,62},{8,14},{40... | collective-permute-start | bytes 405512 | tf_op jit(solution)/shard_map/ppermute | solution.py:414
  6.1 6.7 %collective-permute-start.2 = (bf16[528,128]{1,0:T(8,128)(2,1)}, bf16[528,128]{1,0:T(8,128)(2,1)S(1)}, u32[]{:S(2)}, u32[]{:S(2)}) collective-permute-start(bf16[528,128]{1,0:T(8,128)(2,1)} %pack_kv.1.shard_ref), channel_id=1, source_target_pairs={{0,4},{32,48},{2,6},{34,50},{4,0},{36,52},{6,2},{38,54},{8,12},{40... | collective-permute-start | bytes 405512 | tf_op jit(solution)/shard_map/ppermute | solution.py:414
  7.1 0.9 %copy-start = (bf16[528,128]{1,0:T(8,128)(2,1)S(1)}, bf16[528,128]{1,0:T(8,128)(2,1)}, u32[]{:S(2)}) copy-start(bf16[528,128]{1,0:T(8,128)(2,1)} %pack_kv.1.shard_ref) | copy-start | bytes 405508
  8.1 1.0 %copy-start.1 = (bf16[256,1024]{1,0:T(8,128)(2,1)S(1)}, bf16[256,1024]{1,0:T(8,128)(2,1)}, u32[]{:S(2)}) copy-start(bf16[256,1024]{1,0:T(8,128)(2,1)} %query_ref.1) | copy-start | bytes 1572868
  12.8 13.4 %collective-permute-start.5 = (bf16[272,1024]{1,0:T(8,128)(2,1)S(1)}, bf16[272,1024]{1,0:T(8,128)(2,1)S(1)}, u32[]{:S(2)}, u32[]{:S(2)}) collective-permute-start(bf16[272,1024]{1,0:T(8,128)(2,1)S(1)} %get-tuple-element.61.refs_0_), channel_id=1, source_target_pairs={{0,64},{32,96},{2,66},{34,98},{4,68},{36,100},{6,70},{38,102},{8,7... | collective-permute-start | bytes 1671176 | tf_op jit(solution)/shard_map/ppermute | solution.py:414
  15.9 3.0 %collective-permute-start.6 = (bf16[2112,128]{1,0:T(8,128)(2,1)S(1)}, bf16[2112,128]{1,0:T(8,128)(2,1)S(1)}, u32[]{:S(2)}, u32[]{:S(2)}) collective-permute-start(bf16[2112,128]{1,0:T(8,128)(2,1)S(1)} %pad_maximum_fusion.refs_1_), channel_id=1, source_target_pairs={{0,32},{32,0},{2,34},{34,2},{4,36},{36,4},{6,38},{38,6},{8,40},{40... | collective-permute-start | bytes 1622024 | tf_op jit(solution)/shard_map/ppermute | solution.py:414
  16.0 9.4 %collective-permute-start.3 = (bf16[2112,128]{1,0:T(8,128)(2,1)S(1)}, bf16[2112,128]{1,0:T(8,128)(2,1)S(1)}, u32[]{:S(2)}, u32[]{:S(2)}) collective-permute-start(bf16[2112,128]{1,0:T(8,128)(2,1)S(1)} %pad_maximum_fusion.refs_1_), channel_id=1, source_target_pairs={{0,8},{32,34},{2,10},{34,32},{4,12},{36,38},{6,14},{38,36},{8,0},{... | collective-permute-start | bytes 1622024 | tf_op jit(solution)/shard_map/ppermute | solution.py:414
  16.5 9.7 %collective-permute-start.4 = (bf16[2112,128]{1,0:T(8,128)(2,1)S(1)}, bf16[2112,128]{1,0:T(8,128)(2,1)S(1)}, u32[]{:S(2)}, u32[]{:S(2)}) collective-permute-start(bf16[2112,128]{1,0:T(8,128)(2,1)S(1)} %pad_maximum_fusion.refs_1_), channel_id=1, source_target_pairs={{0,24},{32,38},{2,26},{34,36},{4,28},{36,34},{6,30},{38,32},{8,16}... | collective-permute-start | bytes 1622024 | tf_op jit(solution)/shard_map/ppermute | solution.py:414
  26.2 5.2 %collective-permute-start.10 = (bf16[2112,128]{1,0:T(8,128)(2,1)S(1)}, bf16[2112,128]{1,0:T(8,128)(2,1)S(1)}, u32[]{:S(2)}, u32[]{:S(2)}) collective-permute-start(bf16[2112,128]{1,0:T(8,128)(2,1)S(1)} %collective-permute-done.4.refs_4_), channel_id=1, source_target_pairs={{0,32},{32,0},{2,34},{34,2},{4,36},{36,4},{6,38},{38,6},{8,40},{40... | collective-permute-start | bytes 1622024 | tf_op jit(solution)/shard_map/ppermute | solution.py:414
  26.6 4.8 %collective-permute-start.9 = (bf16[2112,128]{1,0:T(8,128)(2,1)S(1)}, bf16[2112,128]{1,0:T(8,128)(2,1)S(1)}, u32[]{:S(2)}, u32[]{:S(2)}) collective-permute-start(bf16[2112,128]{1,0:T(8,128)(2,1)S(1)} %collective-permute-done.3.refs_3_), channel_id=1, source_target_pairs={{0,32},{32,0},{2,34},{34,2},{4,36},{36,4},{6,38},{38,6},{8,40},{40... | collective-permute-start | bytes 1622024 | tf_op jit(solution)/shard_map/ppermute | solution.py:414
  26.8 13.2 %collective-permute-start.11 = (bf16[2112,128]{1,0:T(8,128)(2,1)S(1)}, bf16[2112,128]{1,0:T(8,128)(2,1)S(1)}, u32[]{:S(2)}, u32[]{:S(2)}) collective-permute-start(bf16[2112,128]{1,0:T(8,128)(2,1)S(1)} %pad_maximum_fusion.refs_1_), channel_id=1, source_target_pairs={{0,16},{32,36},{2,18},{34,38},{4,20},{36,32},{6,22},{38,34},{8,24}... | collective-permute-start | bytes 1622024 | tf_op jit(solution)/shard_map/ppermute | solution.py:414
  30.2 18.7 %collective-permute-start.7 = (bf16[272,1024]{1,0:T(8,128)(2,1)S(1)}, bf16[272,1024]{1,0:T(8,128)(2,1)S(1)}, u32[]{:S(2)}, u32[]{:S(2)}) collective-permute-start(bf16[272,1024]{1,0:T(8,128)(2,1)S(1)} %get-tuple-element.61.refs_0_), channel_id=1, source_target_pairs={{0,1},{32,33},{2,3},{34,35},{4,5},{36,37},{6,7},{38,39},{8,9},{40,... | collective-permute-start | bytes 1671176 | tf_op jit(solution)/shard_map/ppermute | solution.py:414
  30.8 18.1 %collective-permute-start.8 = (bf16[272,1024]{1,0:T(8,128)(2,1)S(1)}, bf16[272,1024]{1,0:T(8,128)(2,1)S(1)}, u32[]{:S(2)}, u32[]{:S(2)}) collective-permute-start(bf16[272,1024]{1,0:T(8,128)(2,1)S(1)} %get-tuple-element.61.refs_0_), channel_id=1, source_target_pairs={{0,65},{32,97},{2,67},{34,99},{4,69},{36,101},{6,71},{38,103},{8,7... | collective-permute-start | bytes 1671176 | tf_op jit(solution)/shard_map/ppermute | solution.py:414
  40.0 3.2 %collective-permute-start.12 = (bf16[2112,128]{1,0:T(8,128)(2,1)S(1)}, bf16[2112,128]{1,0:T(8,128)(2,1)S(1)}, u32[]{:S(2)}, u32[]{:S(2)}) collective-permute-start(bf16[2112,128]{1,0:T(8,128)(2,1)S(1)} %collective-permute-done.11.refs_7_), channel_id=1, source_target_pairs={{0,32},{32,0},{2,34},{34,2},{4,36},{36,4},{6,38},{38,6},{8,40},{40... | collective-permute-start | bytes 1622024 | tf_op jit(solution)/shard_map/ppermute | solution.py:414
  48.9 17.7 %collective-permute-start.13 = (bf16[144,2048]{1,0:T(8,128)(2,1)S(1)}, bf16[144,2048]{1,0:T(8,128)(2,1)S(1)}, u32[]{:S(2)}, u32[]{:S(2)}) collective-permute-start(bf16[144,2048]{1,0:T(8,128)(2,1)S(1)} %get-tuple-element.57), channel_id=1, source_target_pairs={{0,64},{32,96},{2,66},{34,98},{4,68},{36,100},{6,70},{38,102},{8,7... | collective-permute-start | bytes 1769480 | tf_op jit(solution)/shard_map/ppermute | solution.py:414
  60.7 26.2 %collective-permute-start.15 = (bf16[144,2048]{1,0:T(8,128)(2,1)S(1)}, bf16[144,2048]{1,0:T(8,128)(2,1)S(1)}, u32[]{:S(2)}, u32[]{:S(2)}) collective-permute-start(bf16[144,2048]{1,0:T(8,128)(2,1)S(1)} %attend.10), channel_id=1, source_target_pairs={{0,1},{32,33},{2,3},{34,35},{4,5},{36,37},{6,7},{38,39},{8,9},{40,... | collective-permute-start | bytes 1769480 | tf_op jit(solution)/shard_map/ppermute | solution.py:414
  66.6 12.5 %collective-permute-start.14 = (bf16[144,1024]{1,0:T(8,128)(2,1)S(1)}, bf16[144,1024]{1,0:T(8,128)(2,1)S(1)}, u32[]{:S(2)}, u32[]{:S(2)}) collective-permute-start(bf16[144,1024]{1,0:T(8,128)(2,1)S(1)} %attend.11), channel_id=1, source_target_pairs={{0,65},{32,97},{2,67},{34,99},{4,69},{36,101},{6,71},{38,103},{8,7... | collective-permute-start | bytes 884744 | tf_op jit(solution)/shard_map/ppermute | solution.py:414
  79.0 8.0 %collective-permute-start.16 = (bf16[144,1024]{1,0:T(8,128)(2,1)S(1)}, bf16[144,1024]{1,0:T(8,128)(2,1)S(1)}, u32[]{:S(2)}, u32[]{:S(2)}) collective-permute-start(bf16[144,1024]{1,0:T(8,128)(2,1)S(1)} %attend.12), channel_id=1, source_target_pairs={{0,65},{32,97},{2,67},{34,99},{4,69},{36,101},{6,71},{38,103},{8,7... | collective-permute-start | bytes 884744 | tf_op jit(solution)/shard_map/ppermute | solution.py:414

commit v5 on v4

--- a/solution.py
+++ b/solution.py
@@ -103,7 +103,7 @@
 
 
 def attend_kernel(count, sizes, old, done, only, have, base, final, keep, given, *refs):
-    halves = (0, 1) if only is None else (only,)
+    whole_only = only
     q_refs = refs[:count]
     at = count
     piece_refs = () if given else refs[at : at + len(sizes)]
@@ -127,7 +127,7 @@
     ints, blocks, sems, sem = (None,) * 4 if given else refs[at + 4 :]
     starts = [sum(sizes[:i]) for i in range(len(sizes) + 1)]
     shards = starts[-1]
-    group = 16 if shards - done >= 24 and given and only is None else 8
+    group = 16 if shards - done >= 24 and given and only[-1] != 1 else 8
 
     def piece_copy(i):
         there = kv_ref.at[pl.ds(starts[i] * SHARD, sizes[i] * SHARD), :]
@@ -181,6 +181,8 @@
     ones = jnp.ones((16, group * RUN), jnp.bfloat16)
 
     for j in range(count):
+        only = whole_only[j]
+        halves = (0, 1) if only is None else (only,)
         q_ref = q_refs[j]
         tail = q_ref[2 * RUN : QROWS, :].astype(jnp.float32)
         for half in halves:
@@ -307,6 +309,7 @@
 
 
 def attend(q_list, new=(), old=(), acc=None, base=None, final=True, keep=False, given=None, done=0, only=None):
+    only = only or (None,) * len(q_list)
     count = len(q_list)
     pieces = (tuple(old) if final else ()) + tuple(new)
     skip = len(old) if final else 0
@@ -326,8 +329,9 @@
     if base is not None:
         args.append(base)
         in_specs.append(vmem)
-    out = jax.ShapeDtypeStruct((ACC, (2 if only is None else 1) * ROWS), jnp.bfloat16 if final and base is None else jnp.float32)
-    outs, out_specs = [out] * count, [vmem] * count
+    kind = jnp.bfloat16 if final and base is None else jnp.float32
+    outs = [jax.ShapeDtypeStruct((ACC, (2 if run is None else 1) * ROWS), kind) for run in only]
+    out_specs = [vmem] * count
     scratch = []
     if keep:
         outs += [
@@ -434,7 +438,7 @@
     shard = pack_kv(positions, keys, values)
     near = [ring_first(shard, s) for s in (1, 3, 2)]
     packed, acc0 = pack_q(queries, shard)
-    near, packed, acc0 = lax.optimization_barrier((near, packed, acc0))
+    near, _ = lax.optimization_barrier((near, packed))
     line = jnp.concatenate([shard] + near, axis=0)
     q2 = ring_x(packed, 2)
     far1, far3 = ring_second(line, 1), ring_second(line, 3)
@@ -452,13 +456,11 @@
     part2, *whole = attend([q2], last, first, acc=[acc2], keep=True)
     q1, q3, part2 = lax.optimization_barrier((q1, q3, part2))
     back2 = ring_x(part2, 2)
-    (part1,) = attend([q1], given=whole)
-    q3, part1 = lax.optimization_barrier((q3, part1))
-    back1 = ring_x(part1, 1)
-    (low3,) = attend([q3], given=whole, only=0)
-    q3, low3, back2 = lax.optimization_barrier((q3, low3, back2))
-    back_low = ring_x(low3, 3)
-    (high3,) = attend([q3], given=whole, only=1)
+    part1, low3 = attend([q1, q3], given=whole, only=(None, 0))
+    q3, part1, low3 = lax.optimization_barrier((q3, part1, low3))
+    back1, back_low = ring_x(part1, 1), ring_x(low3, 3)
+    (high3,) = attend([q3], given=whole, only=(1,))
+    high3, back2 = lax.optimization_barrier((high3, back2))
     packed, high3 = lax.optimization_barrier((packed, high3))
     back_high = ring_x(high3, 3)
     packed, back_low = lax.optimization_barrier((packed, back_low))

time: 89.2 us -> 87.6 us (0.982)
  the two profiles are of different devices: /device:TPU:8 before, /device:TPU:1 now
where the time goes in v5:
time: 87.6 us; the launch traced here: 87.2 us
  Pallas kernels  50.7 us (58%)
  starting transfers between devices  26.8 us (31%)
  waiting for transfers between devices  7.54 us (9%)
  local copies, waits for them, and re-layouts  1.98 us (2%)
    pallas_call x6, Pallas kernels, attend(): pl.pallas_call(functools.partial(attend_kernel, *flags), out_shape=outs,...  46.9 us
    ppermute x17, starting transfers between devices, swap(): return lax.ppermute(array, AXES, pairs)  26.8 us
    ppermute x17, waiting for transfers between devices, swap(): return lax.ppermute(array, AXES, pairs)  7.54 us
    unnamed x4, local copies, waits for them, and re-layouts  1.98 us
  transfers between devices with their start and end apart: 17, of which 5 were waited for; matrix products, arithmetic and copies ran while one was open for 0% of the time, Pallas kernels for 55%

profile of v5, /device:TPU:1, one launch (start us, length us, event | category | flops | bytes accessed | tf_op | source)
XLA Modules:
  0.0 87.2 jit_solution(6570271385002914306)
XLA Ops:
  0.0 1.6 %pack_kv.1.shard_ref = bf16[528,128]{1,0:T(8,128)(2,1)} custom-call(s32[256]{0:T(256)} %pos_ref.1, bf16[256,128]{1,0:T(8,128)(2,1)} %key_ref.1, bf16[256,128]{1,0:T(8,128)(2,1)} %value_ref.1), custom_call_target="tpu_custom_call" | custom-call | tf_op jit(solution)/shard_map/pack_kv/pallas_call | solution.py:55
  1.6 2.1 %collective-permute-start = (bf16[528,128]{1,0:T(8,128)(2,1)}, bf16[528,128]{1,0:T(8,128)(2,1)S(1)}, u32[]{:S(2)}, u32[]{:S(2)}) collective-permute-start(bf16[528,128]{1,0:T(8,128)(2,1)} %pack_kv.1.shard_ref), channel_id=1, source_target_pairs={{0,2},{32,40},{2,0},{34,42},{4,6},{36,44},{6,4},{38,46},{8,10},{40... | collective-permute-start | bytes 405512 | tf_op jit(solution)/shard_map/ppermute | solution.py:418
  3.8 1.9 %collective-permute-start.1 = (bf16[528,128]{1,0:T(8,128)(2,1)}, bf16[528,128]{1,0:T(8,128)(2,1)S(1)}, u32[]{:S(2)}, u32[]{:S(2)}) collective-permute-start(bf16[528,128]{1,0:T(8,128)(2,1)} %pack_kv.1.shard_ref), channel_id=1, source_target_pairs={{0,6},{32,56},{2,4},{34,58},{4,2},{36,60},{6,0},{38,62},{8,14},{40... | collective-permute-start | bytes 405512 | tf_op jit(solution)/shard_map/ppermute | solution.py:418
  9.2 2.8 %collective-permute-start.5 = (bf16[272,1024]{1,0:T(8,128)(2,1)S(1)}, bf16[272,1024]{1,0:T(8,128)(2,1)S(1)}, u32[]{:S(2)}, u32[]{:S(2)}) collective-permute-start(bf16[272,1024]{1,0:T(8,128)(2,1)S(1)} %get-tuple-element.61.refs_0_), channel_id=1, source_target_pairs={{0,64},{32,96},{2,66},{34,98},{4,68},{36,100},{6,70},{38,102},{8,7... | collective-permute-start | bytes 1671176 | tf_op jit(solution)/shard_map/ppermute | solution.py:418
  12.1 2.6 %collective-permute-start.6 = (bf16[2112,128]{1,0:T(8,128)(2,1)S(1)}, bf16[2112,128]{1,0:T(8,128)(2,1)S(1)}, u32[]{:S(2)}, u32[]{:S(2)}) collective-permute-start(bf16[2112,128]{1,0:T(8,128)(2,1)S(1)} %pad_maximum_fusion.refs_1_), channel_id=1, source_target_pairs={{0,32},{32,0},{2,34},{34,2},{4,36},{36,4},{6,38},{38,6},{8,40},{40... | collective-permute-start | bytes 1622024 | tf_op jit(solution)/shard_map/ppermute | solution.py:418
  15.2 2.0 %collective-permute-start.4 = (bf16[2112,128]{1,0:T(8,128)(2,1)S(1)}, bf16[2112,128]{1,0:T(8,128)(2,1)S(1)}, u32[]{:S(2)}, u32[]{:S(2)}) collective-permute-start(bf16[2112,128]{1,0:T(8,128)(2,1)S(1)} %pad_maximum_fusion.refs_1_), channel_id=1, source_target_pairs={{0,24},{32,38},{2,26},{34,36},{4,28},{36,34},{6,30},{38,32},{8,16}... | collective-permute-start | bytes 1622024 | tf_op jit(solution)/shard_map/ppermute | solution.py:418
  17.2 3.5 %attend.6.refs_3_ = f32[144,2048]{1,0:T(8,128)S(1)} custom-call(bf16[272,1024]{1,0:T(8,128)(2,1)S(1)} %get-tuple-element.61.refs_0_, bf16[2112,128]{1,0:T(8,128)(2,1)S(1)} %pad_maximum_fusion.refs_1_, bf16[2112,128]{1,0:T(8,128)(2,1)S(1)} %collective-permute-done.6.refs_2_, f32[144,2048]{1,0:T(8,128)S(1)} %get-tuple-element.40.refs_3_.refs_4_), custom_call_target="tpu_custom_call" | custom-call | flops 2097152 | bytes 1048576 | tf_op jit(solution)/shard_map/attend/pallas_call | solution.py:359
  20.8 1.9 %collective-permute-done.5.refs_0_ = bf16[272,1024]{1,0:T(8,128)(2,1)S(1)} collective-permute-done((bf16[272,1024]{1,0:T(8,128)(2,1)S(1)}, bf16[272,1024]{1,0:T(8,128)(2,1)S(1)}, u32[]{:S(2)}, u32[]{:S(2)}) %collective-permute-start.5) | collective-permute-done | bytes 557088 | tf_op jit(solution)/shard_map/ppermute | solution.py:418
  23.2 1.7 %collective-permute-done.4.refs_4_ = bf16[2112,128]{1,0:T(8,128)(2,1)S(1)} collective-permute-done((bf16[2112,128]{1,0:T(8,128)(2,1)S(1)}, bf16[2112,128]{1,0:T(8,128)(2,1)S(1)}, u32[]{:S(2)}, u32[]{:S(2)}) %collective-permute-start.4) | collective-permute-done | bytes 540704 | tf_op jit(solution)/shard_map/ppermute | solution.py:418
  24.9 2.1 %collective-permute-start.10 = (bf16[2112,128]{1,0:T(8,128)(2,1)S(1)}, bf16[2112,128]{1,0:T(8,128)(2,1)S(1)}, u32[]{:S(2)}, u32[]{:S(2)}) collective-permute-start(bf16[2112,128]{1,0:T(8,128)(2,1)S(1)} %collective-permute-done.4.refs_4_), channel_id=1, source_target_pairs={{0,32},{32,0},{2,34},{34,2},{4,36},{36,4},{6,38},{38,6},{8,40},{40... | collective-permute-start | bytes 1622024 | tf_op jit(solution)/shard_map/ppermute | solution.py:418
  27.0 2.6 %collective-permute-start.11 = (bf16[2112,128]{1,0:T(8,128)(2,1)S(1)}, bf16[2112,128]{1,0:T(8,128)(2,1)S(1)}, u32[]{:S(2)}, u32[]{:S(2)}) collective-permute-start(bf16[2112,128]{1,0:T(8,128)(2,1)S(1)} %pad_maximum_fusion.refs_1_), channel_id=1, source_target_pairs={{0,16},{32,36},{2,18},{34,38},{4,20},{36,32},{6,22},{38,34},{8,24}... | collective-permute-start | bytes 1622024 | tf_op jit(solution)/shard_map/ppermute | solution.py:418
  29.5 1.2 %collective-permute-start.7 = (bf16[272,1024]{1,0:T(8,128)(2,1)S(1)}, bf16[272,1024]{1,0:T(8,128)(2,1)S(1)}, u32[]{:S(2)}, u32[]{:S(2)}) collective-permute-start(bf16[272,1024]{1,0:T(8,128)(2,1)S(1)} %get-tuple-element.61.refs_0_), channel_id=1, source_target_pairs={{0,1},{32,33},{2,3},{34,35},{4,5},{36,37},{6,7},{38,39},{8,9},{40,... | collective-permute-start | bytes 1671176 | tf_op jit(solution)/shard_map/ppermute | solution.py:418
  30.7 1.8 %collective-permute-start.8 = (bf16[272,1024]{1,0:T(8,128)(2,1)S(1)}, bf16[272,1024]{1,0:T(8,128)(2,1)S(1)}, u32[]{:S(2)}, u32[]{:S(2)}) collective-permute-start(bf16[272,1024]{1,0:T(8,128)(2,1)S(1)} %get-tuple-element.61.refs_0_), channel_id=1, source_target_pairs={{0,65},{32,97},{2,67},{34,99},{4,69},{36,101},{6,71},{38,103},{8,7... | collective-permute-start | bytes 1671176 | tf_op jit(solution)/shard_map/ppermute | solution.py:418
  32.6 8.3 %attend.7.refs_9_ = f32[144,2048]{1,0:T(8,128)S(1)} custom-call(bf16[272,1024]{1,0:T(8,128)(2,1)S(1)} %collective-permute-done.5.refs_0_, bf16[2112,128]{1,0:T(8,128)(2,1)S(1)} %pad_maximum_fusion.refs_1_, bf16[2112,128]{1,0:T(8,128)(2,1)S(1)} %collective-permute-done.6.refs_2_, bf16[2112,128]{1,0:T(8,128)(2,1)S(1)} %collective-permute-done.3.refs_3_, ...), custom_call_target="tpu_custom_call" | custom-call | flops 6291456 | bytes 1048576 | tf_op jit(solution)/shard_map/attend/pallas_call | solution.py:359
  41.3 1.7 %collective-permute-done.12.refs_8_ = bf16[2112,128]{1,0:T(8,128)(2,1)S(1)} collective-permute-done((bf16[2112,128]{1,0:T(8,128)(2,1)S(1)}, bf16[2112,128]{1,0:T(8,128)(2,1)S(1)}, u32[]{:S(2)}, u32[]{:S(2)}) %collective-permute-start.12) | collective-permute-done | bytes 540704 | tf_op jit(solution)/shard_map/ppermute | solution.py:418
  43.0 5.3 %attend.8 = (bf16[144,2048]{1,0:T(8,128)(2,1)S(1)}, bf16[16896,128]{1,0:T(8,128)(2,1)S(1)}, s32[32]{0:T(128)S(1)}) custom-call(bf16[272,1024]{1,0:T(8,128)(2,1)S(1)} %collective-permute-done.5.refs_0_, bf16[2112,128]{1,0:T(8,128)(2,1)S(1)} %pad_maximum_fusion.refs_1_, bf16[2112,128]{1,0:T(8,128)(2,1)S(1)} %collective-permute-done.6.refs_2_, ...), custom_call_target="tpu_custom_call" | custom-call | flops 2097152 | bytes 1048576 | tf_op jit(solution)/shard_map/attend/pallas_call | solution.py:359
  48.4 1.3 %collective-permute-start.13 = (bf16[144,2048]{1,0:T(8,128)(2,1)S(1)}, bf16[144,2048]{1,0:T(8,128)(2,1)S(1)}, u32[]{:S(2)}, u32[]{:S(2)}) collective-permute-start(bf16[144,2048]{1,0:T(8,128)(2,1)S(1)} %get-tuple-element.57), channel_id=1, source_target_pairs={{0,64},{32,96},{2,66},{34,98},{4,68},{36,100},{6,70},{38,102},{8,7... | collective-permute-start | bytes 1769480 | tf_op jit(solution)/shard_map/ppermute | solution.py:418
  49.7 13.1 %attend.9 = (bf16[144,2048]{1,0:T(8,128)(2,1)S(1)}, bf16[144,1024]{1,0:T(8,128)(2,1)S(1)}) custom-call(bf16[272,1024]{1,0:T(8,128)(2,1)S(1)} %collective-permute-done.7.refs_0_, bf16[272,1024]{1,0:T(8,128)(2,1)S(1)} %collective-permute-done.8.refs_1_.refs_0_, bf16[16896,128]{1,0:T(8,128)(2,1)S(1)} %get-tuple-element.52.refs_2_.refs_1_, ...), custom_call_target="tpu_custom_call" | custom-call | flops 16777216 | bytes 1048576 | tf_op jit(solution)/shard_map/attend/pallas_call | solution.py:359
  62.8 2.6 %collective-permute-start.15 = (bf16[144,2048]{1,0:T(8,128)(2,1)S(1)}, bf16[144,2048]{1,0:T(8,128)(2,1)S(1)}, u32[]{:S(2)}, u32[]{:S(2)}) collective-permute-start(bf16[144,2048]{1,0:T(8,128)(2,1)S(1)} %get-tuple-element.63), channel_id=1, source_target_pairs={{0,1},{32,33},{2,3},{34,35},{4,5},{36,37},{6,7},{38,39},{8,9},{40,... | collective-permute-start | bytes 1769480 | tf_op jit(solution)/shard_map/ppermute | solution.py:418
  65.4 1.7 %collective-permute-start.14 = (bf16[144,1024]{1,0:T(8,128)(2,1)S(1)}, bf16[144,1024]{1,0:T(8,128)(2,1)S(1)}, u32[]{:S(2)}, u32[]{:S(2)}) collective-permute-start(bf16[144,1024]{1,0:T(8,128)(2,1)S(1)} %get-tuple-element.60), channel_id=1, source_target_pairs={{0,65},{32,97},{2,67},{34,99},{4,69},{36,101},{6,71},{38,103},{8,7... | collective-permute-start | bytes 884744 | tf_op jit(solution)/shard_map/ppermute | solution.py:418
  67.1 8.9 %attend.10 = bf16[144,1024]{1,0:T(8,128)(2,1)S(1)} custom-call(bf16[272,1024]{1,0:T(8,128)(2,1)S(1)} %collective-permute-done.8.refs_1_.refs_0_, bf16[16896,128]{1,0:T(8,128)(2,1)S(1)} %get-tuple-element.52.refs_2_.refs_1_, s32[32]{0:T(128)S(1)} %get-tuple-element.53.refs_3_.refs_2_), custom_call_target="tpu_custom_call" | custom-call | flops 8388608 | bytes 1048576 | tf_op jit(solution)/shard_map/attend/pallas_call | solution.py:359
  76.4 7.7 %attend.11.own_ref = f32[144,2048]{1,0:T(8,128)S(1)} custom-call(bf16[272,1024]{1,0:T(8,128)(2,1)S(1)} %get-tuple-element.61.refs_0_, bf16[16896,128]{1,0:T(8,128)(2,1)S(1)} %get-tuple-element.52.refs_2_.refs_1_, s32[32]{0:T(128)S(1)} %get-tuple-element.53.refs_3_.refs_2_, f32[144,2048]{1,0:T(8,128)S(1)} %attend.6.refs_3_, ...), custom_call_target="tpu_custom_call" | custom-call | flops 6291456 | bytes 1048576 | tf_op jit(solution)/shard_map/attend/pallas_call | solution.py:359
  84.1 1.6 %collective-permute-done.16.high_ref = bf16[144,1024]{1,0:T(8,128)(2,1)S(1)} collective-permute-done((bf16[144,1024]{1,0:T(8,128)(2,1)S(1)}, bf16[144,1024]{1,0:T(8,128)(2,1)S(1)}, u32[]{:S(2)}, u32[]{:S(2)}) %collective-permute-start.16) | collective-permute-done | bytes 294944 | tf_op jit(solution)/shard_map/ppermute | solution.py:418
  85.8 1.4 %combine.1 = bf16[256,1024]{1,0:T(8,128)(2,1)} custom-call(f32[144,2048]{1,0:T(8,128)S(1)} %attend.11.own_ref, bf16[144,2048]{1,0:T(8,128)(2,1)S(1)} %collective-permute-done.15.one_ref, bf16[144,2048]{1,0:T(8,128)(2,1)S(1)} %collective-permute-done.13.two_ref, bf16[144,1024]{1,0:T(8,128)(2,1)S(1)} %collective-permute-done.14.low_ref, ...), custom_call_target="tpu_custom_call" | custom-call | tf_op jit(solution)/shard_map/combine/pallas_call | solution.py:396
  (24 shorter events, 5.4 us)
Async XLA Ops:
  1.6 10.4 %collective-permute-start = (bf16[528,128]{1,0:T(8,128)(2,1)}, bf16[528,128]{1,0:T(8,128)(2,1)S(1)}, u32[]{:S(2)}, u32[]{:S(2)}) collective-permute-start(bf16[528,128]{1,0:T(8,128)(2,1)} %pack_kv.1.shard_ref), channel_id=1, source_target_pairs={{0,2},{32,40},{2,0},{34,42},{4,6},{36,44},{6,4},{38,46},{8,10},{40... | collective-permute-start | bytes 405512 | tf_op jit(solution)/shard_map/ppermute | solution.py:418
  3.8 8.3 %collective-permute-start.1 = (bf16[528,128]{1,0:T(8,128)(2,1)}, bf16[528,128]{1,0:T(8,128)(2,1)S(1)}, u32[]{:S(2)}, u32[]{:S(2)}) collective-permute-start(bf16[528,128]{1,0:T(8,128)(2,1)} %pack_kv.1.shard_ref), channel_id=1, source_target_pairs={{0,6},{32,56},{2,4},{34,58},{4,2},{36,60},{6,0},{38,62},{8,14},{40... | collective-permute-start | bytes 405512 | tf_op jit(solution)/shard_map/ppermute | solution.py:418
  5.7 6.4 %collective-permute-start.2 = (bf16[528,128]{1,0:T(8,128)(2,1)}, bf16[528,128]{1,0:T(8,128)(2,1)S(1)}, u32[]{:S(2)}, u32[]{:S(2)}) collective-permute-start(bf16[528,128]{1,0:T(8,128)(2,1)} %pack_kv.1.shard_ref), channel_id=1, source_target_pairs={{0,4},{32,48},{2,6},{34,50},{4,0},{36,52},{6,2},{38,54},{8,12},{40... | collective-permute-start | bytes 405512 | tf_op jit(solution)/shard_map/ppermute | solution.py:418
  6.4 0.9 %copy-start = (bf16[528,128]{1,0:T(8,128)(2,1)S(1)}, bf16[528,128]{1,0:T(8,128)(2,1)}, u32[]{:S(2)}) copy-start(bf16[528,128]{1,0:T(8,128)(2,1)} %pack_kv.1.shard_ref) | copy-start | bytes 405508
  7.3 1.0 %copy-start.1 = (bf16[256,1024]{1,0:T(8,128)(2,1)S(1)}, bf16[256,1024]{1,0:T(8,128)(2,1)}, u32[]{:S(2)}) copy-start(bf16[256,1024]{1,0:T(8,128)(2,1)} %query_ref.1) | copy-start | bytes 1572868
  9.2 13.4 %collective-permute-start.5 = (bf16[272,1024]{1,0:T(8,128)(2,1)S(1)}, bf16[272,1024]{1,0:T(8,128)(2,1)S(1)}, u32[]{:S(2)}, u32[]{:S(2)}) collective-permute-start(bf16[272,1024]{1,0:T(8,128)(2,1)S(1)} %get-tuple-element.61.refs_0_), channel_id=1, source_target_pairs={{0,64},{32,96},{2,66},{34,98},{4,68},{36,100},{6,70},{38,102},{8,7... | collective-permute-start | bytes 1671176 | tf_op jit(solution)/shard_map/ppermute | solution.py:418
  12.1 5.1 %collective-permute-start.6 = (bf16[2112,128]{1,0:T(8,128)(2,1)S(1)}, bf16[2112,128]{1,0:T(8,128)(2,1)S(1)}, u32[]{:S(2)}, u32[]{:S(2)}) collective-permute-start(bf16[2112,128]{1,0:T(8,128)(2,1)S(1)} %pad_maximum_fusion.refs_1_), channel_id=1, source_target_pairs={{0,32},{32,0},{2,34},{34,2},{4,36},{36,4},{6,38},{38,6},{8,40},{40... | collective-permute-start | bytes 1622024 | tf_op jit(solution)/shard_map/ppermute | solution.py:418
  14.7 8.5 %collective-permute-start.3 = (bf16[2112,128]{1,0:T(8,128)(2,1)S(1)}, bf16[2112,128]{1,0:T(8,128)(2,1)S(1)}, u32[]{:S(2)}, u32[]{:S(2)}) collective-permute-start(bf16[2112,128]{1,0:T(8,128)(2,1)S(1)} %pad_maximum_fusion.refs_1_), channel_id=1, source_target_pairs={{0,8},{32,34},{2,10},{34,32},{4,12},{36,38},{6,14},{38,36},{8,0},{... | collective-permute-start | bytes 1622024 | tf_op jit(solution)/shard_map/ppermute | solution.py:418
  15.2 9.7 %collective-permute-start.4 = (bf16[2112,128]{1,0:T(8,128)(2,1)S(1)}, bf16[2112,128]{1,0:T(8,128)(2,1)S(1)}, u32[]{:S(2)}, u32[]{:S(2)}) collective-permute-start(bf16[2112,128]{1,0:T(8,128)(2,1)S(1)} %pad_maximum_fusion.refs_1_), channel_id=1, source_target_pairs={{0,24},{32,38},{2,26},{34,36},{4,28},{36,34},{6,30},{38,32},{8,16}... | collective-permute-start | bytes 1622024 | tf_op jit(solution)/shard_map/ppermute | solution.py:418
  24.9 7.7 %collective-permute-start.10 = (bf16[2112,128]{1,0:T(8,128)(2,1)S(1)}, bf16[2112,128]{1,0:T(8,128)(2,1)S(1)}, u32[]{:S(2)}, u32[]{:S(2)}) collective-permute-start(bf16[2112,128]{1,0:T(8,128)(2,1)S(1)} %collective-permute-done.4.refs_4_), channel_id=1, source_target_pairs={{0,32},{32,0},{2,34},{34,2},{4,36},{36,4},{6,38},{38,6},{8,40},{40... | collective-permute-start | bytes 1622024 | tf_op jit(solution)/shard_map/ppermute | solution.py:418
  27.0 5.6 %collective-permute-start.9 = (bf16[2112,128]{1,0:T(8,128)(2,1)S(1)}, bf16[2112,128]{1,0:T(8,128)(2,1)S(1)}, u32[]{:S(2)}, u32[]{:S(2)}) collective-permute-start(bf16[2112,128]{1,0:T(8,128)(2,1)S(1)} %collective-permute-done.3.refs_3_), channel_id=1, source_target_pairs={{0,32},{32,0},{2,34},{34,2},{4,36},{36,4},{6,38},{38,6},{8,40},{40... | collective-permute-start | bytes 1622024 | tf_op jit(solution)/shard_map/ppermute | solution.py:418
  27.0 13.9 %collective-permute-start.11 = (bf16[2112,128]{1,0:T(8,128)(2,1)S(1)}, bf16[2112,128]{1,0:T(8,128)(2,1)S(1)}, u32[]{:S(2)}, u32[]{:S(2)}) collective-permute-start(bf16[2112,128]{1,0:T(8,128)(2,1)S(1)} %pad_maximum_fusion.refs_1_), channel_id=1, source_target_pairs={{0,16},{32,36},{2,18},{34,38},{4,20},{36,32},{6,22},{38,34},{8,24}... | collective-permute-start | bytes 1622024 | tf_op jit(solution)/shard_map/ppermute | solution.py:418
  29.5 18.8 %collective-permute-start.7 = (bf16[272,1024]{1,0:T(8,128)(2,1)S(1)}, bf16[272,1024]{1,0:T(8,128)(2,1)S(1)}, u32[]{:S(2)}, u32[]{:S(2)}) collective-permute-start(bf16[272,1024]{1,0:T(8,128)(2,1)S(1)} %get-tuple-element.61.refs_0_), channel_id=1, source_target_pairs={{0,1},{32,33},{2,3},{34,35},{4,5},{36,37},{6,7},{38,39},{8,9},{40,... | collective-permute-start | bytes 1671176 | tf_op jit(solution)/shard_map/ppermute | solution.py:418
  30.7 17.6 %collective-permute-start.8 = (bf16[272,1024]{1,0:T(8,128)(2,1)S(1)}, bf16[272,1024]{1,0:T(8,128)(2,1)S(1)}, u32[]{:S(2)}, u32[]{:S(2)}) collective-permute-start(bf16[272,1024]{1,0:T(8,128)(2,1)S(1)} %get-tuple-element.61.refs_0_), channel_id=1, source_target_pairs={{0,65},{32,97},{2,67},{34,99},{4,69},{36,101},{6,71},{38,103},{8,7... | collective-permute-start | bytes 1671176 | tf_op jit(solution)/shard_map/ppermute | solution.py:418
  40.9 2.2 %collective-permute-start.12 = (bf16[2112,128]{1,0:T(8,128)(2,1)S(1)}, bf16[2112,128]{1,0:T(8,128)(2,1)S(1)}, u32[]{:S(2)}, u32[]{:S(2)}) collective-permute-start(bf16[2112,128]{1,0:T(8,128)(2,1)S(1)} %collective-permute-done.11.refs_7_), channel_id=1, source_target_pairs={{0,32},{32,0},{2,34},{34,2},{4,36},{36,4},{6,38},{38,6},{8,40},{40... | collective-permute-start | bytes 1622024 | tf_op jit(solution)/shard_map/ppermute | solution.py:418
  48.4 27.6 %collective-permute-start.13 = (bf16[144,2048]{1,0:T(8,128)(2,1)S(1)}, bf16[144,2048]{1,0:T(8,128)(2,1)S(1)}, u32[]{:S(2)}, u32[]{:S(2)}) collective-permute-start(bf16[144,2048]{1,0:T(8,128)(2,1)S(1)} %get-tuple-element.57), channel_id=1, source_target_pairs={{0,64},{32,96},{2,66},{34,98},{4,68},{36,100},{6,70},{38,102},{8,7... | collective-permute-start | bytes 1769480 | tf_op jit(solution)/shard_map/ppermute | solution.py:418
  62.8 21.3 %collective-permute-start.15 = (bf16[144,2048]{1,0:T(8,128)(2,1)S(1)}, bf16[144,2048]{1,0:T(8,128)(2,1)S(1)}, u32[]{:S(2)}, u32[]{:S(2)}) collective-permute-start(bf16[144,2048]{1,0:T(8,128)(2,1)S(1)} %get-tuple-element.63), channel_id=1, source_target_pairs={{0,1},{32,33},{2,3},{34,35},{4,5},{36,37},{6,7},{38,39},{8,9},{40,... | collective-permute-start | bytes 1769480 | tf_op jit(solution)/shard_map/ppermute | solution.py:418
  65.4 11.0 %collective-permute-start.14 = (bf16[144,1024]{1,0:T(8,128)(2,1)S(1)}, bf16[144,1024]{1,0:T(8,128)(2,1)S(1)}, u32[]{:S(2)}, u32[]{:S(2)}) collective-permute-start(bf16[144,1024]{1,0:T(8,128)(2,1)S(1)} %get-tuple-element.60), channel_id=1, source_target_pairs={{0,65},{32,97},{2,67},{34,99},{4,69},{36,101},{6,71},{38,103},{8,7... | collective-permute-start | bytes 884744 | tf_op jit(solution)/shard_map/ppermute | solution.py:418
  76.0 9.8 %collective-permute-start.16 = (bf16[144,1024]{1,0:T(8,128)(2,1)S(1)}, bf16[144,1024]{1,0:T(8,128)(2,1)S(1)}, u32[]{:S(2)}, u32[]{:S(2)}) collective-permute-start(bf16[144,1024]{1,0:T(8,128)(2,1)S(1)} %attend.10), channel_id=1, source_target_pairs={{0,65},{32,97},{2,67},{34,99},{4,69},{36,101},{6,71},{38,103},{8,7... | collective-permute-start | bytes 884744 | tf_op jit(solution)/shard_map/ppermute | solution.py:418

commit v6 on v5

--- a/solution.py
+++ b/solution.py
@@ -115,8 +115,12 @@
     at += count if have else 0
     base_ref = refs[at] if base else None
     at += 1 if base else 0
+    carry_in = refs[at] if 1 in only else None
+    at += 1 if 1 in only else 0
     out_refs = refs[at : at + count]
     at += count
+    carry_out = refs[at] if 0 in only else None
+    at += 1 if 0 in only else 0
     if keep:
         kv_ref, numbers = refs[at : at + 2]
         at += 2
@@ -127,7 +131,7 @@
     ints, blocks, sems, sem = (None,) * 4 if given else refs[at + 4 :]
     starts = [sum(sizes[:i]) for i in range(len(sizes) + 1)]
     shards = starts[-1]
-    group = 16 if shards - done >= 24 and given and only[-1] != 1 else 8
+    group = 16 if shards - done >= 24 else 8
 
     def piece_copy(i):
         there = kv_ref.at[pl.ds(starts[i] * SHARD, sizes[i] * SHARD), :]
@@ -183,9 +187,10 @@
     for j in range(count):
         only = whole_only[j]
         halves = (0, 1) if only is None else (only,)
+        touched = (1,) if only == 1 else (0, 1)
         q_ref = q_refs[j]
         tail = q_ref[2 * RUN : QROWS, :].astype(jnp.float32)
-        for half in halves:
+        for half in touched:
             span = slice(half * ROWS, (half + 1) * ROWS)
             q_buf[half] = query_tile(q_ref, half)
             m_buf[half] = jnp.broadcast_to(
@@ -198,6 +203,8 @@
                 acc_ref[half] = in_refs[j][:, span]
             elif base:
                 acc_ref[half] = base_ref[:, span]
+            elif only == 1:
+                acc_ref[half] = carry_in[...]
             else:
                 acc_ref[half] = jnp.zeros((ACC, ROWS), jnp.float32)
         here = jnp.max(tail[6:7, 0:HD]).astype(jnp.int32)
@@ -207,7 +214,7 @@
             read_blocks(starts[old], shards)
         low_end, high_start = list_tasks(here, done, shards)
 
-        def pure(first, half):
+        def pure(first, half, group):
             query = q_buf[half]
             shift = m_buf[half][0:1]
             parts = []
@@ -216,40 +223,58 @@
                 parts.append(jnp.exp2(dot(keys, query, 1, 1) * COEF - shift).astype(jnp.bfloat16))
             weights = jnp.concatenate(parts, axis=0)
             vt = jnp.concatenate([value_block(tasks[first + b]) for b in range(group)], axis=1)
-            vt = jnp.concatenate([vt, ones], axis=0)
+            vt = jnp.concatenate([vt, ones[:, : group * RUN]], axis=0)
             acc_ref[half] += dot(vt, weights, 1, 0)
 
-        def mixed(first):
+        def mixed(first, group):
             parts = []
             for b in range(group):
-                half = (first + b >= high_start).astype(jnp.int32) if only is None else only
+                half = (first + b >= high_start).astype(jnp.int32)
                 scores = dot(key_block(tasks[first + b]), q_buf[half], 1, 1)
                 parts.append(jnp.exp2(scores * COEF - m_buf[half][0:1]).astype(jnp.bfloat16))
             weights = jnp.concatenate(parts, axis=0)
             vt = jnp.concatenate([value_block(tasks[first + b]) for b in range(group)], axis=1)
-            vt = jnp.concatenate([vt, ones], axis=0)
+            vt = jnp.concatenate([vt, ones[:, : group * RUN]], axis=0)
             index = first + lax.broadcasted_iota(jnp.int32, (1, group * RUN), 1) // RUN
             zero = jnp.zeros((), jnp.bfloat16)
-            if 0 in halves:
-                acc_ref[0] += dot(jnp.where(index < low_end, vt, zero), weights, 1, 0)
-            if 1 in halves:
-                acc_ref[1] += dot(jnp.where(index >= high_start, vt, zero), weights, 1, 0)
+            acc_ref[0] += dot(jnp.where(index < low_end, vt, zero), weights, 1, 0)
+            acc_ref[1] += dot(jnp.where(index >= high_start, vt, zero), weights, 1, 0)
 
         steps = 2 * (shards - done) // group
 
-        @pl.loop(high_start // group if only == 1 else 0, (low_end + group - 1) // group if only == 0 else steps)
+        @pl.loop(steps // 2 if only == 1 else 0, steps // 2 if only == 0 else steps)
         def _(g):
             first = g * group
             is_low = first + group <= low_end
             is_high = first >= high_start
 
+            if only == 1:
+                pure(first, 1, group)
+                return
+
             @pl.when(jnp.logical_or(is_low, is_high))
             def _():
-                pure(first, is_high.astype(jnp.int32) if only is None else only)
+                pure(first, is_high.astype(jnp.int32), group)
 
             @pl.when(jnp.logical_not(jnp.logical_or(is_low, is_high)))
             def _():
-                mixed(first)
+                @pl.loop(0, group // 8)
+                def _(part):
+                    begin = first + part * 8
+                    low_8 = begin + 8 <= low_end
+                    high_8 = begin >= high_start
+                    pure_8 = jnp.logical_or(low_8, high_8)
+
+                    @pl.when(pure_8)
+                    def _():
+                        pure(begin, high_8.astype(jnp.int32), 8)
+
+                    @pl.when(jnp.logical_not(pure_8))
+                    def _():
+                        mixed(begin, 8)
+
+        if only == 0:
+            carry_out[...] = acc_ref[1]
 
         if keep and old:
             for i in range(old):
@@ -308,7 +333,7 @@
                 )
 
 
-def attend(q_list, new=(), old=(), acc=None, base=None, final=True, keep=False, given=None, done=0, only=None):
+def attend(q_list, new=(), old=(), acc=None, base=None, final=True, keep=False, given=None, done=0, only=None, carry=None):
     only = only or (None,) * len(q_list)
     count = len(q_list)
     pieces = (tuple(old) if final else ()) + tuple(new)
@@ -329,9 +354,15 @@
     if base is not None:
         args.append(base)
         in_specs.append(vmem)
+    if carry is not None:
+        args.append(carry)
+        in_specs.append(vmem)
     kind = jnp.bfloat16 if final and base is None else jnp.float32
     outs = [jax.ShapeDtypeStruct((ACC, (2 if run is None else 1) * ROWS), kind) for run in only]
     out_specs = [vmem] * count
+    if 0 in only:
+        outs.append(jax.ShapeDtypeStruct((ACC, ROWS), jnp.float32))
+        out_specs.append(vmem)
     scratch = []
     if keep:
         outs += [
@@ -436,7 +467,7 @@
 
 def body(queries, keys, values, positions):
     shard = pack_kv(positions, keys, values)
-    near = [ring_first(shard, s) for s in (1, 3, 2)]
+    near = [ring_first(shard, s) for s in (2, 3, 1)]
     packed, acc0 = pack_q(queries, shard)
     near, _ = lax.optimization_barrier((near, packed))
     line = jnp.concatenate([shard] + near, axis=0)
@@ -456,10 +487,10 @@
     part2, *whole = attend([q2], last, first, acc=[acc2], keep=True)
     q1, q3, part2 = lax.optimization_barrier((q1, q3, part2))
     back2 = ring_x(part2, 2)
-    part1, low3 = attend([q1, q3], given=whole, only=(None, 0))
-    q3, part1, low3 = lax.optimization_barrier((q3, part1, low3))
+    part1, low3, carry = attend([q1, q3], given=whole, only=(None, 0))
+    q3, part1, low3, carry = lax.optimization_barrier((q3, part1, low3, carry))
     back1, back_low = ring_x(part1, 1), ring_x(low3, 3)
-    (high3,) = attend([q3], given=whole, only=(1,))
+    (high3,) = attend([q3], given=whole, only=(1,), carry=carry)
     high3, back2 = lax.optimization_barrier((high3, back2))
     packed, high3 = lax.optimization_barrier((packed, high3))
     back_high = ring_x(high3, 3)

time: 87.6 us -> 84.1 us (0.960)
  Pallas kernels: 50.7 us -> 49.5 us
  waiting for transfers between devices: 7.54 us -> 6.38 us
  starting transfers between devices: 26.8 us -> 25.7 us
    pallas_call x6, Pallas kernels: 46.9 us -> 45.6 us  [attend(): pl.pallas_call(functools.partial(attend_kernel, *flags), out_shape=outs,...]
    ppermute x17, waiting for transfers between devices: 7.54 us -> 6.38 us  [swap(): return lax.ppermute(array, AXES, pairs)]
    ppermute x17, starting transfers between devices: 26.8 us -> 25.7 us  [swap(): return lax.ppermute(array, AXES, pairs)]
  transfers between devices with their start and end apart: 17 -> 17, of which waited for: 5 -> 4; matrix products, arithmetic and copies ran while one was open for 0% -> 0% of each run, Pallas kernels for 55% -> 55%
where the time goes in v6:
time: 84.1 us; the launch traced here: 83.8 us
  Pallas kernels  49.5 us (59%)
  starting transfers between devices  25.7 us (31%)
  waiting for transfers between devices  6.38 us (8%)
  local copies, waits for them, and re-layouts  2.01 us (2%)
    pallas_call x6, Pallas kernels, attend(): pl.pallas_call(functools.partial(attend_kernel, *flags), out_shape=outs,...  45.6 us
    ppermute x17, starting transfers between devices, swap(): return lax.ppermute(array, AXES, pairs)  25.7 us
    ppermute x17, waiting for transfers between devices, swap(): return lax.ppermute(array, AXES, pairs)  6.38 us
    unnamed x4, local copies, waits for them, and re-layouts  2.01 us
  transfers between devices with their start and end apart: 17, of which 4 were waited for; matrix products, arithmetic and copies ran while one was open for 0% of the time, Pallas kernels for 55%

profile of v6, /device:TPU:1, one launch (start us, length us, event | category | flops | bytes accessed | tf_op | source)
XLA Modules:
  0.0 83.8 jit_solution(12789975167019176122)
XLA Ops:
  0.0 1.6 %pack_kv.1.shard_ref = bf16[528,128]{1,0:T(8,128)(2,1)} custom-call(s32[256]{0:T(256)} %pos_ref.1, bf16[256,128]{1,0:T(8,128)(2,1)} %key_ref.1, bf16[256,128]{1,0:T(8,128)(2,1)} %value_ref.1), custom_call_target="tpu_custom_call" | custom-call | tf_op jit(solution)/shard_map/pack_kv/pallas_call | solution.py:55
  1.6 3.7 %collective-permute-start = (bf16[528,128]{1,0:T(8,128)(2,1)}, bf16[528,128]{1,0:T(8,128)(2,1)S(1)}, u32[]{:S(2)}, u32[]{:S(2)}) collective-permute-start(bf16[528,128]{1,0:T(8,128)(2,1)} %pack_kv.1.shard_ref), channel_id=1, source_target_pairs={{0,4},{32,48},{2,6},{34,50},{4,0},{36,52},{6,2},{38,54},{8,12},{40... | collective-permute-start | bytes 405512 | tf_op jit(solution)/shard_map/ppermute | solution.py:449
  6.2 1.0 %copy-done = bf16[528,128]{1,0:T(8,128)(2,1)S(1)} copy-done((bf16[528,128]{1,0:T(8,128)(2,1)S(1)}, bf16[528,128]{1,0:T(8,128)(2,1)}, u32[]{:S(2)}) %copy-start) | copy-done | bytes 135192
  7.1 1.0 %copy-done.1 = bf16[256,1024]{1,0:T(8,128)(2,1)S(1)} copy-done((bf16[256,1024]{1,0:T(8,128)(2,1)S(1)}, bf16[256,1024]{1,0:T(8,128)(2,1)}, u32[]{:S(2)}) %copy-start.1) | copy-done | bytes 524312
  9.0 2.8 %collective-permute-start.5 = (bf16[272,1024]{1,0:T(8,128)(2,1)S(1)}, bf16[272,1024]{1,0:T(8,128)(2,1)S(1)}, u32[]{:S(2)}, u32[]{:S(2)}) collective-permute-start(bf16[272,1024]{1,0:T(8,128)(2,1)S(1)} %get-tuple-element.65.refs_0_), channel_id=1, source_target_pairs={{0,64},{32,96},{2,66},{34,98},{4,68},{36,100},{6,70},{38,102},{8,7... | collective-permute-start | bytes 1671176 | tf_op jit(solution)/shard_map/ppermute | solution.py:449
  11.9 2.2 %collective-permute-start.6 = (bf16[2112,128]{1,0:T(8,128)(2,1)S(1)}, bf16[2112,128]{1,0:T(8,128)(2,1)S(1)}, u32[]{:S(2)}, u32[]{:S(2)}) collective-permute-start(bf16[2112,128]{1,0:T(8,128)(2,1)S(1)} %pad_maximum_fusion.refs_1_), channel_id=1, source_target_pairs={{0,32},{32,0},{2,34},{34,2},{4,36},{36,4},{6,38},{38,6},{8,40},{40... | collective-permute-start | bytes 1622024 | tf_op jit(solution)/shard_map/ppermute | solution.py:449
  14.1 1.4 %collective-permute-start.3 = (bf16[2112,128]{1,0:T(8,128)(2,1)S(1)}, bf16[2112,128]{1,0:T(8,128)(2,1)S(1)}, u32[]{:S(2)}, u32[]{:S(2)}) collective-permute-start(bf16[2112,128]{1,0:T(8,128)(2,1)S(1)} %pad_maximum_fusion.refs_1_), channel_id=1, source_target_pairs={{0,8},{32,34},{2,10},{34,32},{4,12},{36,38},{6,14},{38,36},{8,0},{... | collective-permute-start | bytes 1622024 | tf_op jit(solution)/shard_map/ppermute | solution.py:449
  15.6 2.2 %collective-permute-start.4 = (bf16[2112,128]{1,0:T(8,128)(2,1)S(1)}, bf16[2112,128]{1,0:T(8,128)(2,1)S(1)}, u32[]{:S(2)}, u32[]{:S(2)}) collective-permute-start(bf16[2112,128]{1,0:T(8,128)(2,1)S(1)} %pad_maximum_fusion.refs_1_), channel_id=1, source_target_pairs={{0,24},{32,38},{2,26},{34,36},{4,28},{36,34},{6,30},{38,32},{8,16}... | collective-permute-start | bytes 1622024 | tf_op jit(solution)/shard_map/ppermute | solution.py:449
  17.8 3.6 %attend.6.refs_3_ = f32[144,2048]{1,0:T(8,128)S(1)} custom-call(bf16[272,1024]{1,0:T(8,128)(2,1)S(1)} %get-tuple-element.65.refs_0_, bf16[2112,128]{1,0:T(8,128)(2,1)S(1)} %pad_maximum_fusion.refs_1_, bf16[2112,128]{1,0:T(8,128)(2,1)S(1)} %collective-permute-done.6.refs_2_, f32[144,2048]{1,0:T(8,128)S(1)} %get-tuple-element.42.refs_3_.refs_4_), custom_call_target="tpu_custom_call" | custom-call | flops 2097152 | bytes 1048576 | tf_op jit(solution)/shard_map/attend/pallas_call | solution.py:390
  21.4 1.5 %collective-permute-done.5.refs_0_ = bf16[272,1024]{1,0:T(8,128)(2,1)S(1)} collective-permute-done((bf16[272,1024]{1,0:T(8,128)(2,1)S(1)}, bf16[272,1024]{1,0:T(8,128)(2,1)S(1)}, u32[]{:S(2)}, u32[]{:S(2)}) %collective-permute-start.5) | collective-permute-done | bytes 557088 | tf_op jit(solution)/shard_map/ppermute | solution.py:449
  22.9 2.4 %collective-permute-done.4.refs_4_ = bf16[2112,128]{1,0:T(8,128)(2,1)S(1)} collective-permute-done((bf16[2112,128]{1,0:T(8,128)(2,1)S(1)}, bf16[2112,128]{1,0:T(8,128)(2,1)S(1)}, u32[]{:S(2)}, u32[]{:S(2)}) %collective-permute-start.4) | collective-permute-done | bytes 540704 | tf_op jit(solution)/shard_map/ppermute | solution.py:449
  25.3 1.1 %collective-permute-start.10 = (bf16[2112,128]{1,0:T(8,128)(2,1)S(1)}, bf16[2112,128]{1,0:T(8,128)(2,1)S(1)}, u32[]{:S(2)}, u32[]{:S(2)}) collective-permute-start(bf16[2112,128]{1,0:T(8,128)(2,1)S(1)} %collective-permute-done.4.refs_4_), channel_id=1, source_target_pairs={{0,32},{32,0},{2,34},{34,2},{4,36},{36,4},{6,38},{38,6},{8,40},{40... | collective-permute-start | bytes 1622024 | tf_op jit(solution)/shard_map/ppermute | solution.py:449
  26.4 3.4 %collective-permute-start.11 = (bf16[2112,128]{1,0:T(8,128)(2,1)S(1)}, bf16[2112,128]{1,0:T(8,128)(2,1)S(1)}, u32[]{:S(2)}, u32[]{:S(2)}) collective-permute-start(bf16[2112,128]{1,0:T(8,128)(2,1)S(1)} %pad_maximum_fusion.refs_1_), channel_id=1, source_target_pairs={{0,16},{32,36},{2,18},{34,38},{4,20},{36,32},{6,22},{38,34},{8,24}... | collective-permute-start | bytes 1622024 | tf_op jit(solution)/shard_map/ppermute | solution.py:449
  30.6 1.8 %collective-permute-start.8 = (bf16[272,1024]{1,0:T(8,128)(2,1)S(1)}, bf16[272,1024]{1,0:T(8,128)(2,1)S(1)}, u32[]{:S(2)}, u32[]{:S(2)}) collective-permute-start(bf16[272,1024]{1,0:T(8,128)(2,1)S(1)} %get-tuple-element.65.refs_0_), channel_id=1, source_target_pairs={{0,65},{32,97},{2,67},{34,99},{4,69},{36,101},{6,71},{38,103},{8,7... | collective-permute-start | bytes 1671176 | tf_op jit(solution)/shard_map/ppermute | solution.py:449
  32.4 8.2 %attend.7.refs_9_ = f32[144,2048]{1,0:T(8,128)S(1)} custom-call(bf16[272,1024]{1,0:T(8,128)(2,1)S(1)} %collective-permute-done.5.refs_0_, bf16[2112,128]{1,0:T(8,128)(2,1)S(1)} %pad_maximum_fusion.refs_1_, bf16[2112,128]{1,0:T(8,128)(2,1)S(1)} %collective-permute-done.6.refs_2_, bf16[2112,128]{1,0:T(8,128)(2,1)S(1)} %collective-permute-done.3.refs_3_, ...), custom_call_target="tpu_custom_call" | custom-call | flops 6291456 | bytes 1048576 | tf_op jit(solution)/shard_map/attend/pallas_call | solution.py:390
  41.4 1.6 %collective-permute-done.12.refs_8_ = bf16[2112,128]{1,0:T(8,128)(2,1)S(1)} collective-permute-done((bf16[2112,128]{1,0:T(8,128)(2,1)S(1)}, bf16[2112,128]{1,0:T(8,128)(2,1)S(1)}, u32[]{:S(2)}, u32[]{:S(2)}) %collective-permute-start.12) | collective-permute-done | bytes 540704 | tf_op jit(solution)/shard_map/ppermute | solution.py:449
  43.0 5.6 %attend.8 = (bf16[144,2048]{1,0:T(8,128)(2,1)S(1)}, bf16[16896,128]{1,0:T(8,128)(2,1)S(1)}, s32[32]{0:T(128)S(1)}) custom-call(bf16[272,1024]{1,0:T(8,128)(2,1)S(1)} %collective-permute-done.5.refs_0_, bf16[2112,128]{1,0:T(8,128)(2,1)S(1)} %pad_maximum_fusion.refs_1_, bf16[2112,128]{1,0:T(8,128)(2,1)S(1)} %collective-permute-done.6.refs_2_, ...), custom_call_target="tpu_custom_call" | custom-call | flops 2097152 | bytes 1048576 | tf_op jit(solution)/shard_map/attend/pallas_call | solution.py:390
  49.3 15.1 %attend.9 = (bf16[144,2048]{1,0:T(8,128)(2,1)S(1)}, bf16[144,1024]{1,0:T(8,128)(2,1)S(1)}, f32[144,1024]{1,0:T(8,128)S(1)}) custom-call(bf16[272,1024]{1,0:T(8,128)(2,1)S(1)} %collective-permute-done.7.refs_0_, bf16[272,1024]{1,0:T(8,128)(2,1)S(1)} %collective-permute-done.8.refs_1_.refs_0_, bf16[16896,128]{1,0:T(8,128)(2,1)S(1)} %get-tuple-element.54.refs_2_.refs_1_, ...), custom_call_target="tpu_custom_call" | custom-call | flops 16777216 | bytes 1048576 | tf_op jit(solution)/shard_map/attend/pallas_call | solution.py:390
  64.5 1.1 %collective-permute-start.15 = (bf16[144,2048]{1,0:T(8,128)(2,1)S(1)}, bf16[144,2048]{1,0:T(8,128)(2,1)S(1)}, u32[]{:S(2)}, u32[]{:S(2)}) collective-permute-start(bf16[144,2048]{1,0:T(8,128)(2,1)S(1)} %get-tuple-element.67), channel_id=1, source_target_pairs={{0,1},{32,33},{2,3},{34,35},{4,5},{36,37},{6,7},{38,39},{8,9},{40,... | collective-permute-start | bytes 1769480 | tf_op jit(solution)/shard_map/ppermute | solution.py:449
  65.6 1.4 %collective-permute-start.14 = (bf16[144,1024]{1,0:T(8,128)(2,1)S(1)}, bf16[144,1024]{1,0:T(8,128)(2,1)S(1)}, u32[]{:S(2)}, u32[]{:S(2)}) collective-permute-start(bf16[144,1024]{1,0:T(8,128)(2,1)S(1)} %get-tuple-element.64), channel_id=1, source_target_pairs={{0,65},{32,97},{2,67},{34,99},{4,69},{36,101},{6,71},{38,103},{8,7... | collective-permute-start | bytes 884744 | tf_op jit(solution)/shard_map/ppermute | solution.py:449
  66.9 5.5 %attend.10 = bf16[144,1024]{1,0:T(8,128)(2,1)S(1)} custom-call(bf16[272,1024]{1,0:T(8,128)(2,1)S(1)} %collective-permute-done.8.refs_1_.refs_0_, bf16[16896,128]{1,0:T(8,128)(2,1)S(1)} %get-tuple-element.54.refs_2_.refs_1_, s32[32]{0:T(128)S(1)} %get-tuple-element.55.refs_3_.refs_2_, f32[144,1024]{1,0:T(8,128)S(1)} %get-tuple-element.60.refs_3_), custom_call_target="tpu_custom_call" | custom-call | flops 8388608 | bytes 1048576 | tf_op jit(solution)/shard_map/attend/pallas_call | solution.py:390
  72.4 1.4 %collective-permute-start.16 = (bf16[144,1024]{1,0:T(8,128)(2,1)S(1)}, bf16[144,1024]{1,0:T(8,128)(2,1)S(1)}, u32[]{:S(2)}, u32[]{:S(2)}) collective-permute-start(bf16[144,1024]{1,0:T(8,128)(2,1)S(1)} %attend.10), channel_id=1, source_target_pairs={{0,65},{32,97},{2,67},{34,99},{4,69},{36,101},{6,71},{38,103},{8,7... | collective-permute-start | bytes 884744 | tf_op jit(solution)/shard_map/ppermute | solution.py:449
  74.7 7.6 %attend.11.own_ref = f32[144,2048]{1,0:T(8,128)S(1)} custom-call(bf16[272,1024]{1,0:T(8,128)(2,1)S(1)} %get-tuple-element.65.refs_0_, bf16[16896,128]{1,0:T(8,128)(2,1)S(1)} %get-tuple-element.54.refs_2_.refs_1_, s32[32]{0:T(128)S(1)} %get-tuple-element.55.refs_3_.refs_2_, f32[144,2048]{1,0:T(8,128)S(1)} %attend.6.refs_3_, ...), custom_call_target="tpu_custom_call" | custom-call | flops 6291456 | bytes 1048576 | tf_op jit(solution)/shard_map/attend/pallas_call | solution.py:390
  82.4 1.4 %combine.1 = bf16[256,1024]{1,0:T(8,128)(2,1)} custom-call(f32[144,2048]{1,0:T(8,128)S(1)} %attend.11.own_ref, bf16[144,2048]{1,0:T(8,128)(2,1)S(1)} %collective-permute-done.15.one_ref, bf16[144,2048]{1,0:T(8,128)(2,1)S(1)} %collective-permute-done.13.two_ref, bf16[144,1024]{1,0:T(8,128)(2,1)S(1)} %collective-permute-done.14.low_ref, ...), custom_call_target="tpu_custom_call" | custom-call | tf_op jit(solution)/shard_map/combine/pallas_call | solution.py:427
  (24 shorter events, 4.9 us)
Async XLA Ops:
  1.6 10.2 %collective-permute-start = (bf16[528,128]{1,0:T(8,128)(2,1)}, bf16[528,128]{1,0:T(8,128)(2,1)S(1)}, u32[]{:S(2)}, u32[]{:S(2)}) collective-permute-start(bf16[528,128]{1,0:T(8,128)(2,1)} %pack_kv.1.shard_ref), channel_id=1, source_target_pairs={{0,4},{32,48},{2,6},{34,50},{4,0},{36,52},{6,2},{38,54},{8,12},{40... | collective-permute-start | bytes 405512 | tf_op jit(solution)/shard_map/ppermute | solution.py:449
  5.4 6.5 %collective-permute-start.1 = (bf16[528,128]{1,0:T(8,128)(2,1)}, bf16[528,128]{1,0:T(8,128)(2,1)S(1)}, u32[]{:S(2)}, u32[]{:S(2)}) collective-permute-start(bf16[528,128]{1,0:T(8,128)(2,1)} %pack_kv.1.shard_ref), channel_id=1, source_target_pairs={{0,6},{32,56},{2,4},{34,58},{4,2},{36,60},{6,0},{38,62},{8,14},{40... | collective-permute-start | bytes 405512 | tf_op jit(solution)/shard_map/ppermute | solution.py:449
  6.2 5.7 %collective-permute-start.2 = (bf16[528,128]{1,0:T(8,128)(2,1)}, bf16[528,128]{1,0:T(8,128)(2,1)S(1)}, u32[]{:S(2)}, u32[]{:S(2)}) collective-permute-start(bf16[528,128]{1,0:T(8,128)(2,1)} %pack_kv.1.shard_ref), channel_id=1, source_target_pairs={{0,2},{32,40},{2,0},{34,42},{4,6},{36,44},{6,4},{38,46},{8,10},{40... | collective-permute-start | bytes 405512 | tf_op jit(solution)/shard_map/ppermute | solution.py:449
  6.2 1.0 %copy-start = (bf16[528,128]{1,0:T(8,128)(2,1)S(1)}, bf16[528,128]{1,0:T(8,128)(2,1)}, u32[]{:S(2)}) copy-start(bf16[528,128]{1,0:T(8,128)(2,1)} %pack_kv.1.shard_ref) | copy-start | bytes 405508
  7.1 1.0 %copy-start.1 = (bf16[256,1024]{1,0:T(8,128)(2,1)S(1)}, bf16[256,1024]{1,0:T(8,128)(2,1)}, u32[]{:S(2)}) copy-start(bf16[256,1024]{1,0:T(8,128)(2,1)} %query_ref.1) | copy-start | bytes 1572868
  9.0 13.8 %collective-permute-start.5 = (bf16[272,1024]{1,0:T(8,128)(2,1)S(1)}, bf16[272,1024]{1,0:T(8,128)(2,1)S(1)}, u32[]{:S(2)}, u32[]{:S(2)}) collective-permute-start(bf16[272,1024]{1,0:T(8,128)(2,1)S(1)} %get-tuple-element.65.refs_0_), channel_id=1, source_target_pairs={{0,64},{32,96},{2,66},{34,98},{4,68},{36,100},{6,70},{38,102},{8,7... | collective-permute-start | bytes 1671176 | tf_op jit(solution)/shard_map/ppermute | solution.py:449
  11.9 5.9 %collective-permute-start.6 = (bf16[2112,128]{1,0:T(8,128)(2,1)S(1)}, bf16[2112,128]{1,0:T(8,128)(2,1)S(1)}, u32[]{:S(2)}, u32[]{:S(2)}) collective-permute-start(bf16[2112,128]{1,0:T(8,128)(2,1)S(1)} %pad_maximum_fusion.refs_1_), channel_id=1, source_target_pairs={{0,32},{32,0},{2,34},{34,2},{4,36},{36,4},{6,38},{38,6},{8,40},{40... | collective-permute-start | bytes 1622024 | tf_op jit(solution)/shard_map/ppermute | solution.py:449
  14.1 8.8 %collective-permute-start.3 = (bf16[2112,128]{1,0:T(8,128)(2,1)S(1)}, bf16[2112,128]{1,0:T(8,128)(2,1)S(1)}, u32[]{:S(2)}, u32[]{:S(2)}) collective-permute-start(bf16[2112,128]{1,0:T(8,128)(2,1)S(1)} %pad_maximum_fusion.refs_1_), channel_id=1, source_target_pairs={{0,8},{32,34},{2,10},{34,32},{4,12},{36,38},{6,14},{38,36},{8,0},{... | collective-permute-start | bytes 1622024 | tf_op jit(solution)/shard_map/ppermute | solution.py:449
  15.6 9.7 %collective-permute-start.4 = (bf16[2112,128]{1,0:T(8,128)(2,1)S(1)}, bf16[2112,128]{1,0:T(8,128)(2,1)S(1)}, u32[]{:S(2)}, u32[]{:S(2)}) collective-permute-start(bf16[2112,128]{1,0:T(8,128)(2,1)S(1)} %pad_maximum_fusion.refs_1_), channel_id=1, source_target_pairs={{0,24},{32,38},{2,26},{34,36},{4,28},{36,34},{6,30},{38,32},{8,16}... | collective-permute-start | bytes 1622024 | tf_op jit(solution)/shard_map/ppermute | solution.py:449
  25.3 7.1 %collective-permute-start.10 = (bf16[2112,128]{1,0:T(8,128)(2,1)S(1)}, bf16[2112,128]{1,0:T(8,128)(2,1)S(1)}, u32[]{:S(2)}, u32[]{:S(2)}) collective-permute-start(bf16[2112,128]{1,0:T(8,128)(2,1)S(1)} %collective-permute-done.4.refs_4_), channel_id=1, source_target_pairs={{0,32},{32,0},{2,34},{34,2},{4,36},{36,4},{6,38},{38,6},{8,40},{40... | collective-permute-start | bytes 1622024 | tf_op jit(solution)/shard_map/ppermute | solution.py:449
  26.4 6.0 %collective-permute-start.9 = (bf16[2112,128]{1,0:T(8,128)(2,1)S(1)}, bf16[2112,128]{1,0:T(8,128)(2,1)S(1)}, u32[]{:S(2)}, u32[]{:S(2)}) collective-permute-start(bf16[2112,128]{1,0:T(8,128)(2,1)S(1)} %collective-permute-done.3.refs_3_), channel_id=1, source_target_pairs={{0,32},{32,0},{2,34},{34,2},{4,36},{36,4},{6,38},{38,6},{8,40},{40... | collective-permute-start | bytes 1622024 | tf_op jit(solution)/shard_map/ppermute | solution.py:449
  26.4 14.3 %collective-permute-start.11 = (bf16[2112,128]{1,0:T(8,128)(2,1)S(1)}, bf16[2112,128]{1,0:T(8,128)(2,1)S(1)}, u32[]{:S(2)}, u32[]{:S(2)}) collective-permute-start(bf16[2112,128]{1,0:T(8,128)(2,1)S(1)} %pad_maximum_fusion.refs_1_), channel_id=1, source_target_pairs={{0,16},{32,36},{2,18},{34,38},{4,20},{36,32},{6,22},{38,34},{8,24}... | collective-permute-start | bytes 1622024 | tf_op jit(solution)/shard_map/ppermute | solution.py:449
  29.8 18.9 %collective-permute-start.7 = (bf16[272,1024]{1,0:T(8,128)(2,1)S(1)}, bf16[272,1024]{1,0:T(8,128)(2,1)S(1)}, u32[]{:S(2)}, u32[]{:S(2)}) collective-permute-start(bf16[272,1024]{1,0:T(8,128)(2,1)S(1)} %get-tuple-element.65.refs_0_), channel_id=1, source_target_pairs={{0,1},{32,33},{2,3},{34,35},{4,5},{36,37},{6,7},{38,39},{8,9},{40,... | collective-permute-start | bytes 1671176 | tf_op jit(solution)/shard_map/ppermute | solution.py:449
  30.6 18.1 %collective-permute-start.8 = (bf16[272,1024]{1,0:T(8,128)(2,1)S(1)}, bf16[272,1024]{1,0:T(8,128)(2,1)S(1)}, u32[]{:S(2)}, u32[]{:S(2)}) collective-permute-start(bf16[272,1024]{1,0:T(8,128)(2,1)S(1)} %get-tuple-element.65.refs_0_), channel_id=1, source_target_pairs={{0,65},{32,97},{2,67},{34,99},{4,69},{36,101},{6,71},{38,103},{8,7... | collective-permute-start | bytes 1671176 | tf_op jit(solution)/shard_map/ppermute | solution.py:449
  40.6 2.4 %collective-permute-start.12 = (bf16[2112,128]{1,0:T(8,128)(2,1)S(1)}, bf16[2112,128]{1,0:T(8,128)(2,1)S(1)}, u32[]{:S(2)}, u32[]{:S(2)}) collective-permute-start(bf16[2112,128]{1,0:T(8,128)(2,1)S(1)} %collective-permute-done.11.refs_7_), channel_id=1, source_target_pairs={{0,32},{32,0},{2,34},{34,2},{4,36},{36,4},{6,38},{38,6},{8,40},{40... | collective-permute-start | bytes 1622024 | tf_op jit(solution)/shard_map/ppermute | solution.py:449
  48.6 23.8 %collective-permute-start.13 = (bf16[144,2048]{1,0:T(8,128)(2,1)S(1)}, bf16[144,2048]{1,0:T(8,128)(2,1)S(1)}, u32[]{:S(2)}, u32[]{:S(2)}) collective-permute-start(bf16[144,2048]{1,0:T(8,128)(2,1)S(1)} %get-tuple-element.61), channel_id=1, source_target_pairs={{0,64},{32,96},{2,66},{34,98},{4,68},{36,100},{6,70},{38,102},{8,7... | collective-permute-start | bytes 1769480 | tf_op jit(solution)/shard_map/ppermute | solution.py:449
  64.5 17.9 %collective-permute-start.15 = (bf16[144,2048]{1,0:T(8,128)(2,1)S(1)}, bf16[144,2048]{1,0:T(8,128)(2,1)S(1)}, u32[]{:S(2)}, u32[]{:S(2)}) collective-permute-start(bf16[144,2048]{1,0:T(8,128)(2,1)S(1)} %get-tuple-element.67), channel_id=1, source_target_pairs={{0,1},{32,33},{2,3},{34,35},{4,5},{36,37},{6,7},{38,39},{8,9},{40,... | collective-permute-start | bytes 1769480 | tf_op jit(solution)/shard_map/ppermute | solution.py:449
  65.6 9.1 %collective-permute-start.14 = (bf16[144,1024]{1,0:T(8,128)(2,1)S(1)}, bf16[144,1024]{1,0:T(8,128)(2,1)S(1)}, u32[]{:S(2)}, u32[]{:S(2)}) collective-permute-start(bf16[144,1024]{1,0:T(8,128)(2,1)S(1)} %get-tuple-element.64), channel_id=1, source_target_pairs={{0,65},{32,97},{2,67},{34,99},{4,69},{36,101},{6,71},{38,103},{8,7... | collective-permute-start | bytes 884744 | tf_op jit(solution)/shard_map/ppermute | solution.py:449
  72.4 9.9 %collective-permute-start.16 = (bf16[144,1024]{1,0:T(8,128)(2,1)S(1)}, bf16[144,1024]{1,0:T(8,128)(2,1)S(1)}, u32[]{:S(2)}, u32[]{:S(2)}) collective-permute-start(bf16[144,1024]{1,0:T(8,128)(2,1)S(1)} %attend.10), channel_id=1, source_target_pairs={{0,65},{32,97},{2,67},{34,99},{4,69},{36,101},{6,71},{38,103},{8,7... | collective-permute-start | bytes 884744 | tf_op jit(solution)/shard_map/ppermute | solution.py:449

commit v7 on v6

--- a/solution.py
+++ b/solution.py
@@ -179,7 +179,7 @@
 
         for i in range(total):
             tasks[i] = 2 * first
-        low_end, high_end = lax.fori_loop(first, last, place, (jnp.int32(0), jnp.int32(total - 1)))
+        low_end, high_end = lax.fori_loop(first, last, place, (jnp.int32(0), jnp.int32(total - 1)), unroll=4)
         return low_end, high_end + 1
 
     ones = jnp.ones((16, group * RUN), jnp.bfloat16)
@@ -472,24 +472,24 @@
     near, _ = lax.optimization_barrier((near, packed))
     line = jnp.concatenate([shard] + near, axis=0)
     q2 = ring_x(packed, 2)
-    far1, far3 = ring_second(line, 1), ring_second(line, 3)
+    far3, far1 = ring_second(line, 3), ring_second(line, 1)
     line_x = cores(line)
     (acc_own,) = attend([packed], [line, line_x], base=acc0, final=False)
-    far1, far3, q2, line_x, line, packed, acc_own = lax.optimization_barrier(
-        (far1, far3, q2, line_x, line, packed, acc_own)
+    far3, far1, q2, line_x, line, packed, acc_own = lax.optimization_barrier(
+        (far3, far1, q2, line_x, line, packed, acc_own)
     )
     far2 = ring_second(line, 2)
-    q1, q3 = ring_x(packed, 1), ring_x(packed, 3)
+    q3, q1 = ring_x(packed, 3), ring_x(packed, 1)
     first = [line, line_x, far1, far3, cores(far1), cores(far3)]
     (acc2,) = attend([q2], first, final=False)
     far2, acc2 = lax.optimization_barrier((far2, acc2))
     last = [far2, cores(far2)]
     part2, *whole = attend([q2], last, first, acc=[acc2], keep=True)
-    q1, q3, part2 = lax.optimization_barrier((q1, q3, part2))
+    q3, q1, part2 = lax.optimization_barrier((q3, q1, part2))
     back2 = ring_x(part2, 2)
     part1, low3, carry = attend([q1, q3], given=whole, only=(None, 0))
     q3, part1, low3, carry = lax.optimization_barrier((q3, part1, low3, carry))
-    back1, back_low = ring_x(part1, 1), ring_x(low3, 3)
+    back_low, back1 = ring_x(low3, 3), ring_x(part1, 1)
     (high3,) = attend([q3], given=whole, only=(1,), carry=carry)
     high3, back2 = lax.optimization_barrier((high3, back2))
     packed, high3 = lax.optimization_barrier((packed, high3))

time: 84.1 us -> 83.5 us (level)
  Pallas kernels: 49.5 us -> 48.2 us
  waiting for transfers between devices: 6.38 us -> 7.47 us
    pallas_call x6, Pallas kernels: 45.6 us -> 44.3 us  [attend(): pl.pallas_call(functools.partial(attend_kernel, *flags), out_shape=outs,...]
    ppermute x17, waiting for transfers between devices: 6.38 us -> 7.47 us  [swap(): return lax.ppermute(array, AXES, pairs)]
  transfers between devices with their start and end apart: 17 -> 17, of which waited for: 4 -> 5; matrix products, arithmetic and copies ran while one was open for 0% -> 0% of each run, Pallas kernels for 55% -> 54%
where the time goes in v7:
time: 83.5 us
  Pallas kernels  48.2 us (58%)
  starting transfers between devices  25.7 us (31%)
  waiting for transfers between devices  7.47 us (9%)
  local copies, waits for them, and re-layouts  2.01 us (2%)
    pallas_call x6, Pallas kernels, attend(): pl.pallas_call(functools.partial(attend_kernel, *flags), out_shape=outs,...  44.3 us
    ppermute x17, starting transfers between devices, swap(): return lax.ppermute(array, AXES, pairs)  25.7 us
    ppermute x17, waiting for transfers between devices, swap(): return lax.ppermute(array, AXES, pairs)  7.47 us
    unnamed x4, local copies, waits for them, and re-layouts  2.01 us
  transfers between devices with their start and end apart: 17, of which 5 were waited for; matrix products, arithmetic and copies ran while one was open for 0% of the time, Pallas kernels for 54%

profile of v7, /device:TPU:1, one launch (start us, length us, event | category | flops | bytes accessed | tf_op | source)
XLA Modules:
  0.0 83.5 jit_solution(13174326100574010812)
XLA Ops:
  0.0 1.6 %pack_kv.1.shard_ref = bf16[528,128]{1,0:T(8,128)(2,1)} custom-call(s32[256]{0:T(256)} %pos_ref.1, bf16[256,128]{1,0:T(8,128)(2,1)} %key_ref.1, bf16[256,128]{1,0:T(8,128)(2,1)} %value_ref.1), custom_call_target="tpu_custom_call" | custom-call | tf_op jit(solution)/shard_map/pack_kv/pallas_call | solution.py:55
  1.6 3.7 %collective-permute-start = (bf16[528,128]{1,0:T(8,128)(2,1)}, bf16[528,128]{1,0:T(8,128)(2,1)S(1)}, u32[]{:S(2)}, u32[]{:S(2)}) collective-permute-start(bf16[528,128]{1,0:T(8,128)(2,1)} %pack_kv.1.shard_ref), channel_id=1, source_target_pairs={{0,4},{32,48},{2,6},{34,50},{4,0},{36,52},{6,2},{38,54},{8,12},{40... | collective-permute-start | bytes 405512 | tf_op jit(solution)/shard_map/ppermute | solution.py:449
  6.2 1.0 %copy-done = bf16[528,128]{1,0:T(8,128)(2,1)S(1)} copy-done((bf16[528,128]{1,0:T(8,128)(2,1)S(1)}, bf16[528,128]{1,0:T(8,128)(2,1)}, u32[]{:S(2)}) %copy-start) | copy-done | bytes 135192
  7.1 1.0 %copy-done.1 = bf16[256,1024]{1,0:T(8,128)(2,1)S(1)} copy-done((bf16[256,1024]{1,0:T(8,128)(2,1)S(1)}, bf16[256,1024]{1,0:T(8,128)(2,1)}, u32[]{:S(2)}) %copy-start.1) | copy-done | bytes 524312
  9.0 2.8 %collective-permute-start.5 = (bf16[272,1024]{1,0:T(8,128)(2,1)S(1)}, bf16[272,1024]{1,0:T(8,128)(2,1)S(1)}, u32[]{:S(2)}, u32[]{:S(2)}) collective-permute-start(bf16[272,1024]{1,0:T(8,128)(2,1)S(1)} %get-tuple-element.65.refs_0_), channel_id=1, source_target_pairs={{0,64},{32,96},{2,66},{34,98},{4,68},{36,100},{6,70},{38,102},{8,7... | collective-permute-start | bytes 1671176 | tf_op jit(solution)/shard_map/ppermute | solution.py:449
  11.9 2.2 %collective-permute-start.6 = (bf16[2112,128]{1,0:T(8,128)(2,1)S(1)}, bf16[2112,128]{1,0:T(8,128)(2,1)S(1)}, u32[]{:S(2)}, u32[]{:S(2)}) collective-permute-start(bf16[2112,128]{1,0:T(8,128)(2,1)S(1)} %pad_maximum_fusion.refs_1_), channel_id=1, source_target_pairs={{0,32},{32,0},{2,34},{34,2},{4,36},{36,4},{6,38},{38,6},{8,40},{40... | collective-permute-start | bytes 1622024 | tf_op jit(solution)/shard_map/ppermute | solution.py:449
  14.1 2.3 %collective-permute-start.3 = (bf16[2112,128]{1,0:T(8,128)(2,1)S(1)}, bf16[2112,128]{1,0:T(8,128)(2,1)S(1)}, u32[]{:S(2)}, u32[]{:S(2)}) collective-permute-start(bf16[2112,128]{1,0:T(8,128)(2,1)S(1)} %pad_maximum_fusion.refs_1_), channel_id=1, source_target_pairs={{0,24},{32,38},{2,26},{34,36},{4,28},{36,34},{6,30},{38,32},{8,16}... | collective-permute-start | bytes 1622024 | tf_op jit(solution)/shard_map/ppermute | solution.py:449
  17.2 3.5 %attend.6.refs_3_ = f32[144,2048]{1,0:T(8,128)S(1)} custom-call(bf16[272,1024]{1,0:T(8,128)(2,1)S(1)} %get-tuple-element.65.refs_0_, bf16[2112,128]{1,0:T(8,128)(2,1)S(1)} %pad_maximum_fusion.refs_1_, bf16[2112,128]{1,0:T(8,128)(2,1)S(1)} %collective-permute-done.6.refs_2_, f32[144,2048]{1,0:T(8,128)S(1)} %get-tuple-element.42.refs_3_.refs_4_), custom_call_target="tpu_custom_call" | custom-call | flops 2097152 | bytes 1048576 | tf_op jit(solution)/shard_map/attend/pallas_call | solution.py:390
  20.7 2.1 %collective-permute-done.5.refs_0_ = bf16[272,1024]{1,0:T(8,128)(2,1)S(1)} collective-permute-done((bf16[272,1024]{1,0:T(8,128)(2,1)S(1)}, bf16[272,1024]{1,0:T(8,128)(2,1)S(1)}, u32[]{:S(2)}, u32[]{:S(2)}) %collective-permute-start.5) | collective-permute-done | bytes 557088 | tf_op jit(solution)/shard_map/ppermute | solution.py:449
  23.8 1.1 %collective-permute-done.4.refs_3_ = bf16[2112,128]{1,0:T(8,128)(2,1)S(1)} collective-permute-done((bf16[2112,128]{1,0:T(8,128)(2,1)S(1)}, bf16[2112,128]{1,0:T(8,128)(2,1)S(1)}, u32[]{:S(2)}, u32[]{:S(2)}) %collective-permute-start.4) | collective-permute-done | bytes 540704 | tf_op jit(solution)/shard_map/ppermute | solution.py:449
  25.0 1.6 %collective-permute-start.10 = (bf16[2112,128]{1,0:T(8,128)(2,1)S(1)}, bf16[2112,128]{1,0:T(8,128)(2,1)S(1)}, u32[]{:S(2)}, u32[]{:S(2)}) collective-permute-start(bf16[2112,128]{1,0:T(8,128)(2,1)S(1)} %collective-permute-done.3.refs_4_), channel_id=1, source_target_pairs={{0,32},{32,0},{2,34},{34,2},{4,36},{36,4},{6,38},{38,6},{8,40},{40... | collective-permute-start | bytes 1622024 | tf_op jit(solution)/shard_map/ppermute | solution.py:449
  26.6 3.4 %collective-permute-start.11 = (bf16[2112,128]{1,0:T(8,128)(2,1)S(1)}, bf16[2112,128]{1,0:T(8,128)(2,1)S(1)}, u32[]{:S(2)}, u32[]{:S(2)}) collective-permute-start(bf16[2112,128]{1,0:T(8,128)(2,1)S(1)} %pad_maximum_fusion.refs_1_), channel_id=1, source_target_pairs={{0,16},{32,36},{2,18},{34,38},{4,20},{36,32},{6,22},{38,34},{8,24}... | collective-permute-start | bytes 1622024 | tf_op jit(solution)/shard_map/ppermute | solution.py:449
  30.0 1.8 %collective-permute-start.7 = (bf16[272,1024]{1,0:T(8,128)(2,1)S(1)}, bf16[272,1024]{1,0:T(8,128)(2,1)S(1)}, u32[]{:S(2)}, u32[]{:S(2)}) collective-permute-start(bf16[272,1024]{1,0:T(8,128)(2,1)S(1)} %get-tuple-element.65.refs_0_), channel_id=1, source_target_pairs={{0,65},{32,97},{2,67},{34,99},{4,69},{36,101},{6,71},{38,103},{8,7... | collective-permute-start | bytes 1671176 | tf_op jit(solution)/shard_map/ppermute | solution.py:449
  31.8 7.6 %attend.7.refs_9_ = f32[144,2048]{1,0:T(8,128)S(1)} custom-call(bf16[272,1024]{1,0:T(8,128)(2,1)S(1)} %collective-permute-done.5.refs_0_, bf16[2112,128]{1,0:T(8,128)(2,1)S(1)} %pad_maximum_fusion.refs_1_, bf16[2112,128]{1,0:T(8,128)(2,1)S(1)} %collective-permute-done.6.refs_2_, bf16[2112,128]{1,0:T(8,128)(2,1)S(1)} %collective-permute-done.4.refs_3_, ...), custom_call_target="tpu_custom_call" | custom-call | flops 6291456 | bytes 1048576 | tf_op jit(solution)/shard_map/attend/pallas_call | solution.py:390
  39.5 1.2 %collective-permute-start.12 = (bf16[2112,128]{1,0:T(8,128)(2,1)S(1)}, bf16[2112,128]{1,0:T(8,128)(2,1)S(1)}, u32[]{:S(2)}, u32[]{:S(2)}) collective-permute-start(bf16[2112,128]{1,0:T(8,128)(2,1)S(1)} %collective-permute-done.11.refs_7_), channel_id=1, source_target_pairs={{0,32},{32,0},{2,34},{34,2},{4,36},{36,4},{6,38},{38,6},{8,40},{40... | collective-permute-start | bytes 1622024 | tf_op jit(solution)/shard_map/ppermute | solution.py:449
  40.7 1.6 %collective-permute-done.12.refs_8_ = bf16[2112,128]{1,0:T(8,128)(2,1)S(1)} collective-permute-done((bf16[2112,128]{1,0:T(8,128)(2,1)S(1)}, bf16[2112,128]{1,0:T(8,128)(2,1)S(1)}, u32[]{:S(2)}, u32[]{:S(2)}) %collective-permute-start.12) | collective-permute-done | bytes 540704 | tf_op jit(solution)/shard_map/ppermute | solution.py:449
  42.2 5.6 %attend.8 = (bf16[144,2048]{1,0:T(8,128)(2,1)S(1)}, bf16[16896,128]{1,0:T(8,128)(2,1)S(1)}, s32[32]{0:T(128)S(1)}) custom-call(bf16[272,1024]{1,0:T(8,128)(2,1)S(1)} %collective-permute-done.5.refs_0_, bf16[2112,128]{1,0:T(8,128)(2,1)S(1)} %pad_maximum_fusion.refs_1_, bf16[2112,128]{1,0:T(8,128)(2,1)S(1)} %collective-permute-done.6.refs_2_, ...), custom_call_target="tpu_custom_call" | custom-call | flops 2097152 | bytes 1048576 | tf_op jit(solution)/shard_map/attend/pallas_call | solution.py:390
  47.8 2.0 %collective-permute-start.13 = (bf16[144,2048]{1,0:T(8,128)(2,1)S(1)}, bf16[144,2048]{1,0:T(8,128)(2,1)S(1)}, u32[]{:S(2)}, u32[]{:S(2)}) collective-permute-start(bf16[144,2048]{1,0:T(8,128)(2,1)S(1)} %get-tuple-element.61), channel_id=1, source_target_pairs={{0,64},{32,96},{2,66},{34,98},{4,68},{36,100},{6,70},{38,102},{8,7... | collective-permute-start | bytes 1769480 | tf_op jit(solution)/shard_map/ppermute | solution.py:449
  49.9 14.8 %attend.9 = (bf16[144,2048]{1,0:T(8,128)(2,1)S(1)}, bf16[144,1024]{1,0:T(8,128)(2,1)S(1)}, f32[144,1024]{1,0:T(8,128)S(1)}) custom-call(bf16[272,1024]{1,0:T(8,128)(2,1)S(1)} %collective-permute-done.8.refs_0_, bf16[272,1024]{1,0:T(8,128)(2,1)S(1)} %collective-permute-done.7.refs_1_.refs_0_, bf16[16896,128]{1,0:T(8,128)(2,1)S(1)} %get-tuple-element.54.refs_2_.refs_1_, ...), custom_call_target="tpu_custom_call" | custom-call | flops 16777216 | bytes 1048576 | tf_op jit(solution)/shard_map/attend/pallas_call | solution.py:390
  64.7 1.9 %collective-permute-start.14 = (bf16[144,1024]{1,0:T(8,128)(2,1)S(1)}, bf16[144,1024]{1,0:T(8,128)(2,1)S(1)}, u32[]{:S(2)}, u32[]{:S(2)}) collective-permute-start(bf16[144,1024]{1,0:T(8,128)(2,1)S(1)} %get-tuple-element.64), channel_id=1, source_target_pairs={{0,65},{32,97},{2,67},{34,99},{4,69},{36,101},{6,71},{38,103},{8,7... | collective-permute-start | bytes 884744 | tf_op jit(solution)/shard_map/ppermute | solution.py:449
  66.6 5.4 %attend.10 = bf16[144,1024]{1,0:T(8,128)(2,1)S(1)} custom-call(bf16[272,1024]{1,0:T(8,128)(2,1)S(1)} %collective-permute-done.7.refs_1_.refs_0_, bf16[16896,128]{1,0:T(8,128)(2,1)S(1)} %get-tuple-element.54.refs_2_.refs_1_, s32[32]{0:T(128)S(1)} %get-tuple-element.55.refs_3_.refs_2_, f32[144,1024]{1,0:T(8,128)S(1)} %get-tuple-element.60.refs_3_), custom_call_target="tpu_custom_call" | custom-call | flops 8388608 | bytes 1048576 | tf_op jit(solution)/shard_map/attend/pallas_call | solution.py:390
  73.0 1.6 %collective-permute-done.14.low_ref = bf16[144,1024]{1,0:T(8,128)(2,1)S(1)} collective-permute-done((bf16[144,1024]{1,0:T(8,128)(2,1)S(1)}, bf16[144,1024]{1,0:T(8,128)(2,1)S(1)}, u32[]{:S(2)}, u32[]{:S(2)}) %collective-permute-start.14) | collective-permute-done | bytes 294944 | tf_op jit(solution)/shard_map/ppermute | solution.py:449
  74.6 7.5 %attend.11.own_ref = f32[144,2048]{1,0:T(8,128)S(1)} custom-call(bf16[272,1024]{1,0:T(8,128)(2,1)S(1)} %get-tuple-element.65.refs_0_, bf16[16896,128]{1,0:T(8,128)(2,1)S(1)} %get-tuple-element.54.refs_2_.refs_1_, s32[32]{0:T(128)S(1)} %get-tuple-element.55.refs_3_.refs_2_, f32[144,2048]{1,0:T(8,128)S(1)} %attend.6.refs_3_, ...), custom_call_target="tpu_custom_call" | custom-call | flops 6291456 | bytes 1048576 | tf_op jit(solution)/shard_map/attend/pallas_call | solution.py:390
  82.1 1.4 %combine.1 = bf16[256,1024]{1,0:T(8,128)(2,1)} custom-call(f32[144,2048]{1,0:T(8,128)S(1)} %attend.11.own_ref, bf16[144,2048]{1,0:T(8,128)(2,1)S(1)} %collective-permute-done.15.one_ref, bf16[144,2048]{1,0:T(8,128)(2,1)S(1)} %collective-permute-done.13.two_ref, bf16[144,1024]{1,0:T(8,128)(2,1)S(1)} %collective-permute-done.14.low_ref, ...), custom_call_target="tpu_custom_call" | custom-call | tf_op jit(solution)/shard_map/combine/pallas_call | solution.py:427
  (24 shorter events, 4.4 us)
Async XLA Ops:
  1.6 10.2 %collective-permute-start = (bf16[528,128]{1,0:T(8,128)(2,1)}, bf16[528,128]{1,0:T(8,128)(2,1)S(1)}, u32[]{:S(2)}, u32[]{:S(2)}) collective-permute-start(bf16[528,128]{1,0:T(8,128)(2,1)} %pack_kv.1.shard_ref), channel_id=1, source_target_pairs={{0,4},{32,48},{2,6},{34,50},{4,0},{36,52},{6,2},{38,54},{8,12},{40... | collective-permute-start | bytes 405512 | tf_op jit(solution)/shard_map/ppermute | solution.py:449
  5.4 6.5 %collective-permute-start.1 = (bf16[528,128]{1,0:T(8,128)(2,1)}, bf16[528,128]{1,0:T(8,128)(2,1)S(1)}, u32[]{:S(2)}, u32[]{:S(2)}) collective-permute-start(bf16[528,128]{1,0:T(8,128)(2,1)} %pack_kv.1.shard_ref), channel_id=1, source_target_pairs={{0,6},{32,56},{2,4},{34,58},{4,2},{36,60},{6,0},{38,62},{8,14},{40... | collective-permute-start | bytes 405512 | tf_op jit(solution)/shard_map/ppermute | solution.py:449
  6.2 5.7 %collective-permute-start.2 = (bf16[528,128]{1,0:T(8,128)(2,1)}, bf16[528,128]{1,0:T(8,128)(2,1)S(1)}, u32[]{:S(2)}, u32[]{:S(2)}) collective-permute-start(bf16[528,128]{1,0:T(8,128)(2,1)} %pack_kv.1.shard_ref), channel_id=1, source_target_pairs={{0,2},{32,40},{2,0},{34,42},{4,6},{36,44},{6,4},{38,46},{8,10},{40... | collective-permute-start | bytes 405512 | tf_op jit(solution)/shard_map/ppermute | solution.py:449
  6.2 1.0 %copy-start = (bf16[528,128]{1,0:T(8,128)(2,1)S(1)}, bf16[528,128]{1,0:T(8,128)(2,1)}, u32[]{:S(2)}) copy-start(bf16[528,128]{1,0:T(8,128)(2,1)} %pack_kv.1.shard_ref) | copy-start | bytes 405508
  7.1 1.0 %copy-start.1 = (bf16[256,1024]{1,0:T(8,128)(2,1)S(1)}, bf16[256,1024]{1,0:T(8,128)(2,1)}, u32[]{:S(2)}) copy-start(bf16[256,1024]{1,0:T(8,128)(2,1)} %query_ref.1) | copy-start | bytes 1572868
  9.0 13.8 %collective-permute-start.5 = (bf16[272,1024]{1,0:T(8,128)(2,1)S(1)}, bf16[272,1024]{1,0:T(8,128)(2,1)S(1)}, u32[]{:S(2)}, u32[]{:S(2)}) collective-permute-start(bf16[272,1024]{1,0:T(8,128)(2,1)S(1)} %get-tuple-element.65.refs_0_), channel_id=1, source_target_pairs={{0,64},{32,96},{2,66},{34,98},{4,68},{36,100},{6,70},{38,102},{8,7... | collective-permute-start | bytes 1671176 | tf_op jit(solution)/shard_map/ppermute | solution.py:449
  11.9 5.3 %collective-permute-start.6 = (bf16[2112,128]{1,0:T(8,128)(2,1)S(1)}, bf16[2112,128]{1,0:T(8,128)(2,1)S(1)}, u32[]{:S(2)}, u32[]{:S(2)}) collective-permute-start(bf16[2112,128]{1,0:T(8,128)(2,1)S(1)} %pad_maximum_fusion.refs_1_), channel_id=1, source_target_pairs={{0,32},{32,0},{2,34},{34,2},{4,36},{36,4},{6,38},{38,6},{8,40},{40... | collective-permute-start | bytes 1622024 | tf_op jit(solution)/shard_map/ppermute | solution.py:449
  14.1 9.7 %collective-permute-start.3 = (bf16[2112,128]{1,0:T(8,128)(2,1)S(1)}, bf16[2112,128]{1,0:T(8,128)(2,1)S(1)}, u32[]{:S(2)}, u32[]{:S(2)}) collective-permute-start(bf16[2112,128]{1,0:T(8,128)(2,1)S(1)} %pad_maximum_fusion.refs_1_), channel_id=1, source_target_pairs={{0,24},{32,38},{2,26},{34,36},{4,28},{36,34},{6,30},{38,32},{8,16}... | collective-permute-start | bytes 1622024 | tf_op jit(solution)/shard_map/ppermute | solution.py:449
  16.5 8.5 %collective-permute-start.4 = (bf16[2112,128]{1,0:T(8,128)(2,1)S(1)}, bf16[2112,128]{1,0:T(8,128)(2,1)S(1)}, u32[]{:S(2)}, u32[]{:S(2)}) collective-permute-start(bf16[2112,128]{1,0:T(8,128)(2,1)S(1)} %pad_maximum_fusion.refs_1_), channel_id=1, source_target_pairs={{0,8},{32,34},{2,10},{34,32},{4,12},{36,38},{6,14},{38,36},{8,0},{... | collective-permute-start | bytes 1622024 | tf_op jit(solution)/shard_map/ppermute | solution.py:449
  25.0 6.9 %collective-permute-start.10 = (bf16[2112,128]{1,0:T(8,128)(2,1)S(1)}, bf16[2112,128]{1,0:T(8,128)(2,1)S(1)}, u32[]{:S(2)}, u32[]{:S(2)}) collective-permute-start(bf16[2112,128]{1,0:T(8,128)(2,1)S(1)} %collective-permute-done.3.refs_4_), channel_id=1, source_target_pairs={{0,32},{32,0},{2,34},{34,2},{4,36},{36,4},{6,38},{38,6},{8,40},{40... | collective-permute-start | bytes 1622024 | tf_op jit(solution)/shard_map/ppermute | solution.py:449
  26.6 5.3 %collective-permute-start.9 = (bf16[2112,128]{1,0:T(8,128)(2,1)S(1)}, bf16[2112,128]{1,0:T(8,128)(2,1)S(1)}, u32[]{:S(2)}, u32[]{:S(2)}) collective-permute-start(bf16[2112,128]{1,0:T(8,128)(2,1)S(1)} %collective-permute-done.4.refs_3_), channel_id=1, source_target_pairs={{0,32},{32,0},{2,34},{34,2},{4,36},{36,4},{6,38},{38,6},{8,40},{40... | collective-permute-start | bytes 1622024 | tf_op jit(solution)/shard_map/ppermute | solution.py:449
  26.6 12.9 %collective-permute-start.11 = (bf16[2112,128]{1,0:T(8,128)(2,1)S(1)}, bf16[2112,128]{1,0:T(8,128)(2,1)S(1)}, u32[]{:S(2)}, u32[]{:S(2)}) collective-permute-start(bf16[2112,128]{1,0:T(8,128)(2,1)S(1)} %pad_maximum_fusion.refs_1_), channel_id=1, source_target_pairs={{0,16},{32,36},{2,18},{34,38},{4,20},{36,32},{6,22},{38,34},{8,24}... | collective-permute-start | bytes 1622024 | tf_op jit(solution)/shard_map/ppermute | solution.py:449
  30.0 17.8 %collective-permute-start.7 = (bf16[272,1024]{1,0:T(8,128)(2,1)S(1)}, bf16[272,1024]{1,0:T(8,128)(2,1)S(1)}, u32[]{:S(2)}, u32[]{:S(2)}) collective-permute-start(bf16[272,1024]{1,0:T(8,128)(2,1)S(1)} %get-tuple-element.65.refs_0_), channel_id=1, source_target_pairs={{0,65},{32,97},{2,67},{34,99},{4,69},{36,101},{6,71},{38,103},{8,7... | collective-permute-start | bytes 1671176 | tf_op jit(solution)/shard_map/ppermute | solution.py:449
  31.8 16.0 %collective-permute-start.8 = (bf16[272,1024]{1,0:T(8,128)(2,1)S(1)}, bf16[272,1024]{1,0:T(8,128)(2,1)S(1)}, u32[]{:S(2)}, u32[]{:S(2)}) collective-permute-start(bf16[272,1024]{1,0:T(8,128)(2,1)S(1)} %get-tuple-element.65.refs_0_), channel_id=1, source_target_pairs={{0,1},{32,33},{2,3},{34,35},{4,5},{36,37},{6,7},{38,39},{8,9},{40,... | collective-permute-start | bytes 1671176 | tf_op jit(solution)/shard_map/ppermute | solution.py:449
  39.5 2.8 %collective-permute-start.12 = (bf16[2112,128]{1,0:T(8,128)(2,1)S(1)}, bf16[2112,128]{1,0:T(8,128)(2,1)S(1)}, u32[]{:S(2)}, u32[]{:S(2)}) collective-permute-start(bf16[2112,128]{1,0:T(8,128)(2,1)S(1)} %collective-permute-done.11.refs_7_), channel_id=1, source_target_pairs={{0,32},{32,0},{2,34},{34,2},{4,36},{36,4},{6,38},{38,6},{8,40},{40... | collective-permute-start | bytes 1622024 | tf_op jit(solution)/shard_map/ppermute | solution.py:449
  47.8 24.2 %collective-permute-start.13 = (bf16[144,2048]{1,0:T(8,128)(2,1)S(1)}, bf16[144,2048]{1,0:T(8,128)(2,1)S(1)}, u32[]{:S(2)}, u32[]{:S(2)}) collective-permute-start(bf16[144,2048]{1,0:T(8,128)(2,1)S(1)} %get-tuple-element.61), channel_id=1, source_target_pairs={{0,64},{32,96},{2,66},{34,98},{4,68},{36,100},{6,70},{38,102},{8,7... | collective-permute-start | bytes 1769480 | tf_op jit(solution)/shard_map/ppermute | solution.py:449
  64.7 17.5 %collective-permute-start.15 = (bf16[144,2048]{1,0:T(8,128)(2,1)S(1)}, bf16[144,2048]{1,0:T(8,128)(2,1)S(1)}, u32[]{:S(2)}, u32[]{:S(2)}) collective-permute-start(bf16[144,2048]{1,0:T(8,128)(2,1)S(1)} %get-tuple-element.67), channel_id=1, source_target_pairs={{0,1},{32,33},{2,3},{34,35},{4,5},{36,37},{6,7},{38,39},{8,9},{40,... | collective-permute-start | bytes 1769480 | tf_op jit(solution)/shard_map/ppermute | solution.py:449
  64.7 9.9 %collective-permute-start.14 = (bf16[144,1024]{1,0:T(8,128)(2,1)S(1)}, bf16[144,1024]{1,0:T(8,128)(2,1)S(1)}, u32[]{:S(2)}, u32[]{:S(2)}) collective-permute-start(bf16[144,1024]{1,0:T(8,128)(2,1)S(1)} %get-tuple-element.64), channel_id=1, source_target_pairs={{0,65},{32,97},{2,67},{34,99},{4,69},{36,101},{6,71},{38,103},{8,7... | collective-permute-start | bytes 884744 | tf_op jit(solution)/shard_map/ppermute | solution.py:449
  72.0 10.1 %collective-permute-start.16 = (bf16[144,1024]{1,0:T(8,128)(2,1)S(1)}, bf16[144,1024]{1,0:T(8,128)(2,1)S(1)}, u32[]{:S(2)}, u32[]{:S(2)}) collective-permute-start(bf16[144,1024]{1,0:T(8,128)(2,1)S(1)} %attend.10), channel_id=1, source_target_pairs={{0,65},{32,97},{2,67},{34,99},{4,69},{36,101},{6,71},{38,103},{8,7... | collective-permute-start | bytes 884744 | tf_op jit(solution)/shard_map/ppermute | solution.py:449
